TPU v7x, 32 devices: a whole 2x2x4 slice. The times are simulated.
32 devices in a mesh: groups: 2 (over x), tensor: 16 (over z, y, core).
Axes of the slice: x: 2, y: 2, z: 4, core: 2. Of those that a mesh axis runs over, the one named last changes fastest.
Arguments:
- tokens: bfloat16 [64, 7424], P(('groups', 'tensor')), parts along dimension 0, may hold values from -6 to 6
- gate_weight: bfloat16 [7424, 29696], P(None, 'tensor'), may hold values from -0.0625 to 0.0625
- up_weight: bfloat16 [7424, 29696], P(None, 'tensor'), may hold values from -0.0625 to 0.0625
- down_weight: bfloat16 [29696, 7424], P('tensor'), may hold values from -0.03125 to 0.03125
- valid_counts: int32 [32], P(('groups', 'tensor')), parts along dimension 0, may hold values from 1 to 2, 24 in all
Outputs:
- mixed: bfloat16 [64, 7424], P(('groups', 'tensor')), parts along dimension 0
There are 2 independent parts, one for each index of `groups`. A program takes and returns all parts, laid end to end along the dimension named above; an argument that names none is the same for every part. Nothing has to cross between parts.
Inputs may be any that keep to these rules, and one draw needn't show every extreme that they name: `valid_counts`: the counts sum to 24; some block is full in every draw.
All inputs are finite; a program needn't handle non-finite values.
Results may differ from a plain program's by a relative error of at most 0.005.
Values may be sent and summed in bfloat16 or wider, within the bound.
No kernel may reach another device: no remote copies, remote signals or barrier semaphores. Data moves between devices by JAX's collectives and lax.ppermute only.
A program may use at most 192 MiB of HBM per device.

v0:
```python
import jax
import jax.numpy as jnp
from jax import lax
from jax.sharding import PartitionSpec as P


def per_device(tokens, gate_weight, up_weight, down_weight, valid_counts):
    row_count = tokens.shape[0]
    position = jnp.arange(row_count, dtype=jnp.int32)
    keep = (position < valid_counts[0])[:, None]
    masked = jnp.where(keep, tokens, jnp.zeros_like(tokens))
    gathered = lax.all_gather(masked, "tensor", axis=0, tiled=True)
    gate_value = jnp.dot(gathered, gate_weight, preferred_element_type=jnp.float32)
    up_value = jnp.dot(gathered, up_weight, preferred_element_type=jnp.float32)
    hidden = (jax.nn.silu(gate_value) * up_value).astype(jnp.bfloat16)
    terms = jnp.dot(hidden, down_weight, preferred_element_type=jnp.float32)
    summed = lax.psum_scatter(terms, "tensor", scatter_dimension=0, tiled=True)
    return summed.astype(jnp.bfloat16)


def solution(mesh):
    return jax.shard_map(
        per_device,
        mesh=mesh,
        in_specs=(
            P(("groups", "tensor"), None),
            P(None, "tensor"),
            P(None, "tensor"),
            P("tensor", None),
            P(("groups", "tensor")),
        ),
        out_specs=P(("groups", "tensor"), None),
        check_vma=False,
    )
```

profile of v0, /device:TPU:0, one launch (start us, length us, event | category | flops | bytes accessed | tf_op | source)
XLA Modules:
  0.0 132.2 jit_solution(7585081957134057493)
XLA Ops:
  0.7 0.8 fusion.8
  1.5 24.4 %all-gather = bf16[16,2,7424]{2,1,0:T(2,128)(2,1)S(1)} all-gather(bf16[1,2,7424]{2,1,0:T(2,128)(2,1)S(1)} %fusion.8), channel_id=1, replica_groups=mesh['groups'=2,'tensor'=16] {'tensor'}, dimensions={0}, use_global_device_ids=true | all-gather | bytes 504832 | tf_op jit(solution)/shard_map/all_gather | solution.py:12
  25.9 0.2 reshape.5
  26.1 12.6 %fusion.10 = f32[32,1856]{1,0:T(8,128)S(1)} fusion(bf16[32,7424]{1,0:T(8,128)(2,1)S(1)} %reshape.5, bf16[7424,1856]{0,1:T(8,128)(2,1)} %param.6), kind=kOutput, calls=%fused_computation.14 | convolution fusion | flops 881852416 | bytes 28270592 | tf_op jit(solution)/shard_map/dot_general | solution.py:13
  38.7 0.0 copy-start
  38.8 22.8 %fusion.1 = f32[32,7424]{1,0:T(8,128)S(1)} fusion(bf16[1856,7424]{1,0:T(8,128)(2,1)} %param.8, bf16[32,7424]{1,0:T(8,128)(2,1)S(1)} %reshape.5, bf16[7424,1856]{0,1:T(8,128)(2,1)} %param.7, f32[32,1856]{1,0:T(8,128)S(1)} %fusion.10), kind=kOutput, calls=%fused_computation.2 | convolution fusion | flops 1764061184 | bytes 56778752 | tf_op jit(solution)/shard_map/dot_general | solution.py:16
  61.6 68.7 %all-reduce.2 = bf16[32,7424]{1,0:T(8,128)(2,1)S(1)} all-reduce(f32[32,7424]{1,0:T(8,128)S(1)} %fusion.1), channel_id=2, replica_groups=mesh['groups'=2,'tensor'=16] {'tensor'}, use_global_device_ids=true, to_apply=%region_0.1.clone | all-reduce | flops 237568 | bytes 1425408
  130.3 0.0 copy-done
  130.3 0.6 dynamic-slice
  131.5 0.6 dynamic-slice_convert_fusion
  (1 shorter events, 0.0 us)
Async XLA Ops:
  38.7 91.5 %copy-start = (u32[32]{0:T(128)S(1)}, u32[32]{0:T(128)}, u32[]{:S(2)}) copy-start(u32[32]{0:T(128)} %constant.9) | copy-start | bytes 388
where the time goes:
time: 132 us
  blocking collectives  93.1 us (71%)
  matrix products  35.4 us (27%)
  local copies, waits for them, and re-layouts  1.42 us (1%)
  between operations  1.37 us (1%)
    unnamed x1, blocking collectives  68.7 us
    all_gather x1, blocking collectives, per_device(): gathered = lax.all_gather(masked, 'tensor', axis=0, tiled=True)  24.4 us
    dot_general x1, matrix products, per_device(): terms = jnp.dot(hidden, down_weight, preferred_element_type=jnp.float32)  22.8 us
    dot_general x1, matrix products, per_device(): jnp.dot(gathered, gate_weight, preferred_element_type=jnp.float32)  12.6 us

commit v1 on v0

v1 whole, which is shorter than its diff:
```python
import functools

import jax
import jax.numpy as jnp
from jax import lax
from jax.experimental import pallas as pl
from jax.experimental.pallas import tpu as pltpu
from jax.sharding import PartitionSpec as P

MIB = 1 << 20
VMEM = pl.BlockSpec(memory_space=pltpu.VMEM)
HBM = pl.BlockSpec(memory_space=pltpu.HBM)
ANY = pl.BlockSpec(memory_space=pl.ANY)
BLOCKS = 4
CHUNKS = 2


def cost(flops, moved):
    return pl.CostEstimate(flops=flops, bytes_accessed=moved, transcendentals=0)


def load_kernel(start, source, after, piece, token, sem):
    copy = pltpu.make_async_copy(source.at[pl.ds(start, piece.shape[0])], piece, sem)
    copy.start()
    token[...] = jnp.zeros_like(token)
    copy.wait()


def load(source, after, start, rows):
    shape = (rows, source.shape[1])
    return pl.pallas_call(
        functools.partial(load_kernel, start),
        out_shape=(pltpu.VMEM(shape, source.dtype), jax.ShapeDtypeStruct((8, 128), jnp.float32)),
        in_specs=[HBM, VMEM],
        out_specs=(VMEM, VMEM),
        scratch_shapes=[pltpu.SemaphoreType.DMA],
        compiler_params=pltpu.CompilerParams(vmem_limit_bytes=1 * MIB),
        cost_estimate=cost(0, 2 * rows * source.shape[1]),
    )(source, after)


def join_kernel(mine, theirs, token, joined):
    rows = mine.shape[0]
    joined[:rows, :] = mine[...]
    joined[rows:, :] = theirs[...]


def join(mine, theirs, token):
    rows, width = mine.shape
    return pl.pallas_call(
        join_kernel,
        out_shape=pltpu.VMEM((2 * rows, width), mine.dtype),
        in_specs=[VMEM, VMEM, ANY],
        out_specs=VMEM,
        compiler_params=pltpu.CompilerParams(vmem_limit_bytes=2 * MIB),
        cost_estimate=cost(0, 8 * rows * width),
    )(mine, theirs, token)


def hidden_kernel(rows, mine, theirs, g0, u0, g1, u1, gate, up, down, hidden, d0, d1, d2, d3, tokens, g2, u2, g3, u3, sems):
    def copy(source, block, into, sem):
        return pltpu.make_async_copy(source.at[pl.ds(block * rows, rows)], into, sems.at[sem])

    streamed = [copy(gate, 2, g2, 0), copy(up, 2, u2, 1), copy(gate, 3, g3, 2), copy(up, 3, u3, 3)]
    for one in streamed:
        one.start()
    half = mine.shape[0]
    tokens[:half, :] = mine[...]
    tokens[half:, :] = theirs[...]
    contract = (((1,), (1,)), ((), ()))

    def compute(block, gate_block, up_block):
        half_rows = rows // 2
        gate_value = lax.dot_general(
            gate_block[...], tokens[...], contract, preferred_element_type=jnp.float32
        )
        up_value = lax.dot_general(
            up_block[...], tokens[...], contract, preferred_element_type=jnp.float32
        )
        value = gate_value / (1.0 + jnp.exp(-gate_value)) * up_value
        hidden[block * rows : (block + 1) * rows, :] = value.astype(hidden.dtype)

    later = []

    def bring(block, into):
        later.append(copy(down, block, into, 4 + block))
        later[-1].start()

    compute(0, g0, u0)
    bring(0, d0)
    bring(1, d1)
    compute(1, g1, u1)
    bring(2, d2)
    bring(3, d3)
    streamed[0].wait()
    streamed[1].wait()
    compute(2, g2, u2)
    streamed[2].wait()
    streamed[3].wait()
    compute(3, g3, u3)
    for one in later:
        one.wait()


def hidden_of(mine, theirs, pieces, gate, up, down):
    rows, width = pieces[0].shape
    count = mine.shape[0] + theirs.shape[0]
    block = pltpu.VMEM((rows, width), gate.dtype)
    return pl.pallas_call(
        functools.partial(hidden_kernel, rows),
        out_shape=(pltpu.VMEM((gate.shape[0], count), gate.dtype),) + (pltpu.VMEM((rows, width), gate.dtype),) * 4,
        in_specs=[VMEM] * 6 + [HBM] * 3,
        out_specs=(VMEM,) * 5,
        input_output_aliases={2: 1, 3: 2, 4: 3, 5: 4},
        scratch_shapes=[pltpu.VMEM((count, width), mine.dtype)] + [block] * 4 + [pltpu.SemaphoreType.DMA((8,))],
        compiler_params=pltpu.CompilerParams(vmem_limit_bytes=8 * rows * width + 4 * MIB),
        cost_estimate=cost(4 * count * gate.size, 4 * gate.size),
    )(mine, theirs, *pieces, gate, up, down)


def down_kernel(start, hidden, d0, d1, d2, d3, keep, send):
    rows, columns = d0.shape[0], keep.shape[1]
    half = keep.shape[0]
    step = 1024 if columns > 1024 else columns
    for at in range(0, columns, step):
        size = min(step, columns - at)
        total = None
        for block, piece in enumerate((d0, d1, d2, d3)):
            value = lax.dot_general(
                hidden[block * rows : (block + 1) * rows, :],
                piece[:, start + at : start + at + size],
                (((0,), (0,)), ((), ())),
                preferred_element_type=jnp.float32,
            )
            total = value if total is None else total + value
        keep[:, at : at + size] = total[:half]
        send[:, at : at + size] = total[half:].astype(send.dtype)


def down_of(hidden, pieces, start, columns):
    half = hidden.shape[1] // 2
    return pl.pallas_call(
        functools.partial(down_kernel, start),
        out_shape=(pltpu.VMEM((half, columns), jnp.float32), pltpu.VMEM((half, columns), jnp.bfloat16)),
        in_specs=[VMEM] * 5,
        out_specs=(VMEM, VMEM),
        compiler_params=pltpu.CompilerParams(vmem_limit_bytes=2 * MIB),
        cost_estimate=cost(4 * half * hidden.shape[0] * columns, 2 * hidden.shape[0] * columns),
    )(hidden, *pieces)


def exchange(array, mask, count):
    return lax.ppermute(array, "tensor", [(i, i ^ mask) for i in range(count)])


def masked(terms, own, valid_counts):
    keep = jnp.arange(own, dtype=jnp.int32)[:, None] < valid_counts[0]
    return jnp.where(keep, terms, 0.0).astype(jnp.bfloat16)


def reduced(keep, send, masks, count):
    for at, mask in enumerate(masks):
        total = keep + exchange(send, mask, count).astype(jnp.float32)
        if at + 1 == len(masks):
            return total
        rows = total.shape[0] // 2
        keep, send = total[:rows], total[rows:].astype(jnp.bfloat16)


def plain(count, masks, tokens, gate_weight, up_weight, down_weight, valid_counts):
    own = tokens.shape[0]
    gathered = tokens
    for mask in reversed(masks):
        gathered = jnp.concatenate([gathered, exchange(gathered, mask, count)], axis=0)
    gate_value = jnp.dot(gathered, gate_weight, preferred_element_type=jnp.float32)
    up_value = jnp.dot(gathered, up_weight, preferred_element_type=jnp.float32)
    hidden = (jax.nn.silu(gate_value) * up_value).astype(jnp.bfloat16)
    terms = jnp.dot(hidden, down_weight, preferred_element_type=jnp.float32)
    half = terms.shape[0] // 2
    total = reduced(terms[:half], terms[half:].astype(jnp.bfloat16), masks, count)
    return masked(total, own, valid_counts)


def per_device(count, masks, tokens, gate_weight, up_weight, down_weight, valid_counts):
    own, width = tokens.shape
    gate, up, down_weight = (
        pltpu.with_memory_space_constraint(one, pltpu.HBM)
        for one in (gate_weight.T, up_weight.T, down_weight)
    )
    rows = gate.shape[0] // BLOCKS
    mine, after, pieces = tokens, tokens, []
    wanted = [(gate, 0), (up, 0), (gate, rows), (up, rows)]
    steps = list(reversed(masks))
    for at, mask in enumerate(steps):
        theirs = exchange(mine, mask, count)
        now = wanted[:1] if at + 1 < len(steps) else wanted
        wanted = wanted[len(now) :]
        token = None
        for source, start in now:
            piece, token = load(source, after, start, rows)
            pieces.append(piece)
        if at + 1 < len(steps):
            after = mine = join(mine, theirs, token)
    hidden, *down_pieces = hidden_of(mine, theirs, pieces, gate, up, down_weight)
    columns = width // CHUNKS
    parts = []
    for chunk in range(CHUNKS):
        keep, send = down_of(hidden, down_pieces, chunk * columns, columns)
        parts.append(reduced(keep, send, masks, count))
    return masked(jnp.concatenate(parts, axis=1), own, valid_counts)


def solution(mesh):
    count = mesh.shape["tensor"]
    masks = [1 << bit for bit in range(count.bit_length() - 1)]

    def step(tokens, gate_weight, up_weight, down_weight, valid_counts):
        hidden_rows, width = down_weight.shape
        fits = 8 * hidden_rows * width <= 2 * 56 * MIB
        whole_tiles = hidden_rows % (16 * BLOCKS) == 0 and width % (128 * CHUNKS) == 0
        small = (tokens.shape[0] << len(masks)) <= 64 and len(masks) >= 4
        use = per_device if fits and whole_tiles and small else plain
        return use(count, masks, tokens, gate_weight, up_weight, down_weight, valid_counts)

    return jax.shard_map(
        step,
        mesh=mesh,
        in_specs=(
            P(("groups", "tensor"), None),
            P(None, "tensor"),
            P(None, "tensor"),
            P("tensor", None),
            P(("groups", "tensor")),
        ),
        out_specs=P(("groups", "tensor"), None),
        check_vma=False,
    )
```

time: 132 us -> 68.3 us (0.52)
  blocking collectives: 93.1 us -> 0 us
  Pallas kernels: 0 us -> 41.9 us
  matrix products: 35.4 us -> 0 us
  starting transfers between devices: 0 us -> 16.4 us
  waiting for transfers between devices: 0 us -> 6.4 us
    unnamed x1 -> x0, blocking collectives: 68.7 us -> none
    pallas_call x0 -> x10, Pallas kernels: none -> 41.9 us  [the longest x1 24.9 us: hidden_of(): pl.pallas_call(functools.partial(hidden_kernel, rows), out_shape=(pltpu.V...]
    dot_general x2 -> x0, matrix products: 35.4 us -> none  [the longest x1 22.8 us: per_device(): terms = jnp.dot(hidden, down_weight, preferred_element_type=jnp.float32)]
    all_gather x1 -> x0, blocking collectives: 24.4 us -> none  [per_device(): gathered = lax.all_gather(masked, 'tensor', axis=0, tiled=True)]
    ppermute x0 -> x12, starting transfers between devices: none -> 16.4 us  [exchange(): return lax.ppermute(array, 'tensor', [(i, i ^ mask) for i in range(count)])]
    ppermute x0 -> x12, waiting for transfers between devices: none -> 6.4 us  [exchange(): return lax.ppermute(array, 'tensor', [(i, i ^ mask) for i in range(count)])]
  transfers between devices with their start and end apart: 0 -> 12, of which waited for: 0 -> 6; matrix products, arithmetic and copies ran while one was open for 0% -> 0% of each run, Pallas kernels for 0% -> 22%
where the time goes in v1:
time: 68.3 us; the launch traced here: 68 us
  Pallas kernels  41.9 us (61%)
  starting transfers between devices  16.4 us (24%)
  waiting for transfers between devices  6.4 us (9%)
  local copies, waits for them, and re-layouts  1.56 us (2%)
  between operations  0.89 us (1%)
  other arithmetic  0.86 us (1%)
    pallas_call x1, Pallas kernels, hidden_of(): pl.pallas_call(functools.partial(hidden_kernel, rows), out_shape=(pltpu.V...  24.9 us
    ppermute x12, starting transfers between devices, exchange(): return lax.ppermute(array, 'tensor', [(i, i ^ mask) for i in range(count)])  16.4 us
    pallas_call x4, Pallas kernels, load(): pl.pallas_call(functools.partial(load_kernel, start), out_shape=(pltpu.VM...  12.5 us
    ppermute x12, waiting for transfers between devices, exchange(): return lax.ppermute(array, 'tensor', [(i, i ^ mask) for i in range(count)])  6.4 us
    pallas_call x2, Pallas kernels, down_of(): pl.pallas_call(functools.partial(down_kernel, start), out_shape=(pltpu.VM...  4.49 us
    unnamed x8, local copies, waits for them, and re-layouts  1.47 us
  transfers between devices with their start and end apart: 12, of which 6 were waited for; matrix products, arithmetic and copies ran while one was open for 0% of the time, Pallas kernels for 22%

profile of v1, /device:TPU:0, one launch (start us, length us, event | category | flops | bytes accessed | tf_op | source)
XLA Modules:
  0.0 68.0 jit_solution(6789156877616139221)
XLA Ops:
  0.0 4.0 %collective-permute-start = (bf16[2,7424]{1,0:T(2,128)(2,1)}, bf16[2,7424]{1,0:T(2,128)(2,1)S(1)}, u32[]{:S(2)}, u32[]{:S(2)}) collective-permute-start(bf16[2,7424]{1,0:T(2,128)(2,1)} %mine.1), channel_id=1, source_target_pairs={{0,8},{1,9},{2,10},{3,11},{4,12},{5,13},{6,14},{7,15},{8,0},{9,1},... | collective-permute-start | bytes 89096 | tf_op jit(solution)/shard_map/ppermute | solution.py:153
  4.0 0.8 %copy-done.1 = bf16[2,7424]{1,0:T(2,128)(2,1)S(1)} copy-done((bf16[2,7424]{1,0:T(2,128)(2,1)S(1)}, bf16[2,7424]{1,0:T(2,128)(2,1)}, u32[]{:S(2)}) %copy-start.1) | copy-done | bytes 29720
  4.8 3.0 %shard_map.55 = (bf16[464,7424]{1,0:T(8,128)(2,1)S(1)}, f32[8,128]{1,0:T(8,128)S(1)}) custom-call(bf16[1856,7424]{1,0:T(8,128)(2,1)} %bitcast.4, bf16[2,7424]{1,0:T(2,128)(2,1)S(1)} %copy-done.1), custom_call_target="tpu_custom_call" | custom-call | bytes 6889472 | tf_op jit(solution)/shard_map/pallas_call | solution.py:31
  7.8 0.0 collective-permute-done.theirs
  7.8 1.6 %collective-permute-start.1 = (bf16[4,7424]{1,0:T(4,128)(2,1)S(1)}, bf16[4,7424]{1,0:T(4,128)(2,1)S(1)}, u32[]{:S(2)}, u32[]{:S(2)}) collective-permute-start(bf16[4,7424]{1,0:T(4,128)(2,1)S(1)} %shard_map.56.after.mine), channel_id=1, source_target_pairs={{0,4},{1,5},{2,6},{3,7},{4,0},{5,1},{6,2},{7,3},{8,12},{9,13},{10,... | collective-permute-start | bytes 178184 | tf_op jit(solution)/shard_map/ppermute | solution.py:153
  9.5 3.0 %shard_map.57 = (bf16[464,7424]{1,0:T(8,128)(2,1)S(1)}, f32[8,128]{1,0:T(8,128)S(1)}) custom-call(bf16[1856,7424]{1,0:T(8,128)(2,1)} %bitcast.7, bf16[4,7424]{1,0:T(4,128)(2,1)S(1)} %shard_map.56.after.mine), custom_call_target="tpu_custom_call" | custom-call | bytes 6889472 | tf_op jit(solution)/shard_map/pallas_call | solution.py:31
  12.5 0.0 collective-permute-done.1.theirs
  12.5 1.6 %collective-permute-start.2 = (bf16[8,7424]{1,0:T(8,128)(2,1)S(1)}, bf16[8,7424]{1,0:T(8,128)(2,1)S(1)}, u32[]{:S(2)}, u32[]{:S(2)}) collective-permute-start(bf16[8,7424]{1,0:T(8,128)(2,1)S(1)} %shard_map.58.after.mine), channel_id=1, source_target_pairs={{0,2},{1,3},{2,0},{3,1},{4,6},{5,7},{6,4},{7,5},{8,10},{9,11},{10,... | collective-permute-start | bytes 356360 | tf_op jit(solution)/shard_map/ppermute | solution.py:153
  14.1 3.0 %shard_map.59 = (bf16[464,7424]{1,0:T(8,128)(2,1)S(1)}, f32[8,128]{1,0:T(8,128)S(1)}) custom-call(bf16[1856,7424]{1,0:T(8,128)(2,1)} %bitcast.5, bf16[8,7424]{1,0:T(8,128)(2,1)S(1)} %shard_map.58.after.mine), custom_call_target="tpu_custom_call" | custom-call | bytes 6889472 | tf_op jit(solution)/shard_map/pallas_call | solution.py:31
  17.1 0.3 collective-permute-done.2.theirs
  17.4 0.1 collective-permute-start.3
  18.2 3.6 %shard_map.61 = (bf16[464,7424]{1,0:T(8,128)(2,1)S(1)}, f32[8,128]{1,0:T(8,128)}) custom-call(bf16[1856,7424]{1,0:T(8,128)(2,1)} %bitcast.8, bf16[16,7424]{1,0:T(8,128)(2,1)S(1)} %shard_map.60.after.mine), custom_call_target="tpu_custom_call" | custom-call | bytes 6889472 | tf_op jit(solution)/shard_map/pallas_call | solution.py:31
  21.8 0.0 collective-permute-done.3.theirs
  21.8 0.7 copy-done.3
  22.5 24.9 %shard_map.62 = (bf16[1856,32]{1,0:T(8,128)(2,1)S(1)}, bf16[464,7424]{1,0:T(8,128)(2,1)S(1)}, bf16[464,7424]{1,0:T(8,128)(2,1)S(1)}, bf16[464,7424]{1,0:T(8,128)(2,1)S(1)}, bf16[464,7424]{1,0:T(8,128)(2,1)S(1)}) custom-call(bf16[16,7424]{1,0:T(8,128)(2,1)} %copy-done, ...), custom_call_target="tpu_custom_call", output_to_operand_aliasing={{1}: (2, {}), {2}: (3, {}), {3}: (4, {}), {4}: (5, {})} | custom-call | flops 1763704832 | bytes 55115776 | tf_op jit(solution)/shard_map/pallas_call | solution.py:109
  47.4 2.2 %shard_map.63 = (f32[16,3712]{1,0:T(8,128)S(1)}, bf16[16,3712]{1,0:T(8,128)(2,1)S(1)}) custom-call(bf16[1856,32]{1,0:T(8,128)(2,1)S(1)} %get-tuple-element.28.hidden, bf16[464,7424]{1,0:T(8,128)(2,1)S(1)} %get-tuple-element.29.d0, bf16[464,7424]{1,0:T(8,128)(2,1)S(1)} %get-tuple-element.30.d1, bf16[464,7424]{1,0:T(8,128)(2,1)S(1)} %get-tuple-element.31.d2, ...), custom_call_target="tpu_custom_call" | custom-call | flops 440926208 | bytes 13778944 | tf_op jit(solution)/shard_map/pallas_call | solution.py:142
  49.6 0.5 collective-permute-start.4
  50.2 2.2 %shard_map.64 = (f32[16,3712]{1,0:T(8,128)S(1)}, bf16[16,3712]{1,0:T(8,128)(2,1)S(1)}) custom-call(bf16[1856,32]{1,0:T(8,128)(2,1)S(1)} %get-tuple-element.28.hidden, bf16[464,7424]{1,0:T(8,128)(2,1)S(1)} %get-tuple-element.29.d0, bf16[464,7424]{1,0:T(8,128)(2,1)S(1)} %get-tuple-element.30.d1, bf16[464,7424]{1,0:T(8,128)(2,1)S(1)} %get-tuple-element.31.d2, ...), custom_call_target="tpu_custom_call" | custom-call | flops 440926208 | bytes 13778944 | tf_op jit(solution)/shard_map/pallas_call | solution.py:142
  52.4 0.1 collective-permute-start.8
  52.6 1.6 %collective-permute-start.5 = (bf16[8,3712]{1,0:T(8,128)(2,1)S(1)}, bf16[8,3712]{1,0:T(8,128)(2,1)S(1)}, u32[]{:S(2)}, u32[]{:S(2)}) collective-permute-start(bf16[8,3712]{1,0:T(8,128)(2,1)S(1)} %slice.79), channel_id=1, source_target_pairs={{0,2},{1,3},{2,0},{3,1},{4,6},{5,7},{6,4},{7,5},{8,10},{9,11},{10,... | collective-permute-start | bytes 178184 | tf_op jit(solution)/shard_map/ppermute | solution.py:153
  54.2 0.0 collective-permute-done.8
  54.2 1.2 %collective-permute-start.9 = (bf16[8,3712]{1,0:T(8,128)(2,1)S(1)}, bf16[8,3712]{1,0:T(8,128)(2,1)S(1)}, u32[]{:S(2)}, u32[]{:S(2)}) collective-permute-start(bf16[8,3712]{1,0:T(8,128)(2,1)S(1)} %slice.78), channel_id=1, source_target_pairs={{0,2},{1,3},{2,0},{3,1},{4,6},{5,7},{6,4},{7,5},{8,10},{9,11},{10,... | collective-permute-start | bytes 178184 | tf_op jit(solution)/shard_map/ppermute | solution.py:153
  55.4 1.5 %collective-permute-done.5 = bf16[8,3712]{1,0:T(8,128)(2,1)S(1)} collective-permute-done((bf16[8,3712]{1,0:T(8,128)(2,1)S(1)}, bf16[8,3712]{1,0:T(8,128)(2,1)S(1)}, u32[]{:S(2)}, u32[]{:S(2)}) %collective-permute-start.5) | collective-permute-done | bytes 59424 | tf_op jit(solution)/shard_map/ppermute | solution.py:153
  57.0 1.3 %collective-permute-start.6 = (bf16[4,3712]{1,0:T(4,128)(2,1)S(1)}, bf16[4,3712]{1,0:T(4,128)(2,1)S(1)}, u32[]{:S(2)}, u32[]{:S(2)}) collective-permute-start(bf16[4,3712]{1,0:T(4,128)(2,1)S(1)} %slice.81), channel_id=1, source_target_pairs={{0,4},{1,5},{2,6},{3,7},{4,0},{5,1},{6,2},{7,3},{8,12},{9,13},{10,... | collective-permute-start | bytes 89096 | tf_op jit(solution)/shard_map/ppermute | solution.py:153
  58.3 0.2 collective-permute-done.9
  58.5 1.3 %collective-permute-start.10 = (bf16[4,3712]{1,0:T(4,128)(2,1)S(1)}, bf16[4,3712]{1,0:T(4,128)(2,1)S(1)}, u32[]{:S(2)}, u32[]{:S(2)}) collective-permute-start(bf16[4,3712]{1,0:T(4,128)(2,1)S(1)} %slice.80), channel_id=1, source_target_pairs={{0,4},{1,5},{2,6},{3,7},{4,0},{5,1},{6,2},{7,3},{8,12},{9,13},{10,... | collective-permute-start | bytes 89096 | tf_op jit(solution)/shard_map/ppermute | solution.py:153
  59.8 1.3 %collective-permute-done.6 = bf16[4,3712]{1,0:T(4,128)(2,1)S(1)} collective-permute-done((bf16[4,3712]{1,0:T(4,128)(2,1)S(1)}, bf16[4,3712]{1,0:T(4,128)(2,1)S(1)}, u32[]{:S(2)}, u32[]{:S(2)}) %collective-permute-start.6) | collective-permute-done | bytes 29728 | tf_op jit(solution)/shard_map/ppermute | solution.py:153
  61.1 1.5 %collective-permute-start.7 = (bf16[2,3712]{1,0:T(2,128)(2,1)S(1)}, bf16[2,3712]{1,0:T(2,128)(2,1)S(1)}, u32[]{:S(2)}, u32[]{:S(2)}) collective-permute-start(bf16[2,3712]{1,0:T(2,128)(2,1)S(1)} %slice.83), channel_id=1, source_target_pairs={{0,8},{1,9},{2,10},{3,11},{4,12},{5,13},{6,14},{7,15},{8,0},{9,1},... | collective-permute-start | bytes 44552 | tf_op jit(solution)/shard_map/ppermute | solution.py:153
  62.6 1.6 %collective-permute-start.11 = (bf16[2,3712]{1,0:T(2,128)(2,1)S(1)}, bf16[2,3712]{1,0:T(2,128)(2,1)S(1)}, u32[]{:S(2)}, u32[]{:S(2)}) collective-permute-start(bf16[2,3712]{1,0:T(2,128)(2,1)S(1)} %slice.82), channel_id=1, source_target_pairs={{0,8},{1,9},{2,10},{3,11},{4,12},{5,13},{6,14},{7,15},{8,0},{9,1},... | collective-permute-start | bytes 44552 | tf_op jit(solution)/shard_map/ppermute | solution.py:153
  64.2 1.6 %collective-permute-done.7 = bf16[2,3712]{1,0:T(2,128)(2,1)S(1)} collective-permute-done((bf16[2,3712]{1,0:T(2,128)(2,1)S(1)}, bf16[2,3712]{1,0:T(2,128)(2,1)S(1)}, u32[]{:S(2)}, u32[]{:S(2)}) %collective-permute-start.7) | collective-permute-done | bytes 14880 | tf_op jit(solution)/shard_map/ppermute | solution.py:153
  65.8 1.5 %collective-permute-done.11 = bf16[2,3712]{1,0:T(2,128)(2,1)S(1)} collective-permute-done((bf16[2,3712]{1,0:T(2,128)(2,1)S(1)}, bf16[2,3712]{1,0:T(2,128)(2,1)S(1)}, u32[]{:S(2)}, u32[]{:S(2)}) %collective-permute-start.11) | collective-permute-done | bytes 14880 | tf_op jit(solution)/shard_map/ppermute | solution.py:153
  67.3 0.7 %fusion = bf16[2,7424]{1,0:T(2,128)(2,1)} fusion(bf16[2,3712]{1,0:T(2,128)(2,1)S(1)} %slice_add_fusion.4, bf16[2,3712]{1,0:T(2,128)(2,1)S(1)} %slice_add_fusion.5, pred[2]{0:T(512)(128)(4,1)S(1)} %iota_compare_fusion), kind=kLoop, calls=%fused_computation.11 | loop fusion | flops 74240 | bytes 59394 | tf_op jit(solution)/shard_map/convert_element_type | solution.py:158
  (26 shorter events, 0.3 us)
Async XLA Ops:
  0.0 7.8 %collective-permute-start = (bf16[2,7424]{1,0:T(2,128)(2,1)}, bf16[2,7424]{1,0:T(2,128)(2,1)S(1)}, u32[]{:S(2)}, u32[]{:S(2)}) collective-permute-start(bf16[2,7424]{1,0:T(2,128)(2,1)} %mine.1), channel_id=1, source_target_pairs={{0,8},{1,9},{2,10},{3,11},{4,12},{5,13},{6,14},{7,15},{8,0},{9,1},... | collective-permute-start | bytes 89096 | tf_op jit(solution)/shard_map/ppermute | solution.py:153
  4.0 0.8 %copy-start.1 = (bf16[2,7424]{1,0:T(2,128)(2,1)S(1)}, bf16[2,7424]{1,0:T(2,128)(2,1)}, u32[]{:S(2)}) copy-start(bf16[2,7424]{1,0:T(2,128)(2,1)} %mine.1) | copy-start | bytes 89092
  4.8 3.0 %copy-start.2 = (bf16[2,7424]{1,0:T(2,128)(2,1)S(1)}, bf16[2,7424]{1,0:T(2,128)(2,1)}, u32[]{:S(2)}) copy-start(bf16[2,7424]{1,0:T(2,128)(2,1)} %mine.1) | copy-start | bytes 89092
  7.8 4.6 %collective-permute-start.1 = (bf16[4,7424]{1,0:T(4,128)(2,1)S(1)}, bf16[4,7424]{1,0:T(4,128)(2,1)S(1)}, u32[]{:S(2)}, u32[]{:S(2)}) collective-permute-start(bf16[4,7424]{1,0:T(4,128)(2,1)S(1)} %shard_map.56.after.mine), channel_id=1, source_target_pairs={{0,4},{1,5},{2,6},{3,7},{4,0},{5,1},{6,2},{7,3},{8,12},{9,13},{10,... | collective-permute-start | bytes 178184 | tf_op jit(solution)/shard_map/ppermute | solution.py:153
  12.5 4.9 %collective-permute-start.2 = (bf16[8,7424]{1,0:T(8,128)(2,1)S(1)}, bf16[8,7424]{1,0:T(8,128)(2,1)S(1)}, u32[]{:S(2)}, u32[]{:S(2)}) collective-permute-start(bf16[8,7424]{1,0:T(8,128)(2,1)S(1)} %shard_map.58.after.mine), channel_id=1, source_target_pairs={{0,2},{1,3},{2,0},{3,1},{4,6},{5,7},{6,4},{7,5},{8,10},{9,11},{10,... | collective-permute-start | bytes 356360 | tf_op jit(solution)/shard_map/ppermute | solution.py:153
  17.4 4.3 %copy-start = (bf16[16,7424]{1,0:T(8,128)(2,1)}, bf16[16,7424]{1,0:T(8,128)(2,1)S(1)}, u32[]{:S(2)}) copy-start(bf16[16,7424]{1,0:T(8,128)(2,1)S(1)} %shard_map.60.after.mine) | copy-start | bytes 712708
  17.4 4.3 %collective-permute-start.3 = (bf16[16,7424]{1,0:T(8,128)(2,1)S(1)}, bf16[16,7424]{1,0:T(8,128)(2,1)S(1)}, u32[]{:S(2)}, u32[]{:S(2)}) collective-permute-start(bf16[16,7424]{1,0:T(8,128)(2,1)S(1)} %shard_map.60.after.mine), channel_id=1, source_target_pairs={{0,1},{1,0},{2,3},{3,2},{4,5},{5,4},{6,7},{7,6},{8,9},{9,8},{10,11... | collective-permute-start | bytes 712712 | tf_op jit(solution)/shard_map/ppermute | solution.py:153
  21.8 0.7 %copy-start.3 = (bf16[16,7424]{1,0:T(8,128)(2,1)}, bf16[16,7424]{1,0:T(8,128)(2,1)S(1)}, u32[]{:S(2)}) copy-start(bf16[16,7424]{1,0:T(8,128)(2,1)S(1)} %collective-permute-done.3.theirs) | copy-start | bytes 712708
  49.6 2.9 %collective-permute-start.4 = (bf16[16,3712]{1,0:T(8,128)(2,1)S(1)}, bf16[16,3712]{1,0:T(8,128)(2,1)S(1)}, u32[]{:S(2)}, u32[]{:S(2)}) collective-permute-start(bf16[16,3712]{1,0:T(8,128)(2,1)S(1)} %get-tuple-element.34), channel_id=1, source_target_pairs={{0,1},{1,0},{2,3},{3,2},{4,5},{5,4},{6,7},{7,6},{8,9},{9,8},{10,11... | collective-permute-start | bytes 356360 | tf_op jit(solution)/shard_map/ppermute | solution.py:153
  52.4 1.7 %collective-permute-start.8 = (bf16[16,3712]{1,0:T(8,128)(2,1)S(1)}, bf16[16,3712]{1,0:T(8,128)(2,1)S(1)}, u32[]{:S(2)}, u32[]{:S(2)}) collective-permute-start(bf16[16,3712]{1,0:T(8,128)(2,1)S(1)} %get-tuple-element.36), channel_id=1, source_target_pairs={{0,1},{1,0},{2,3},{3,2},{4,5},{5,4},{6,7},{7,6},{8,9},{9,8},{10,11... | collective-permute-start | bytes 356360 | tf_op jit(solution)/shard_map/ppermute | solution.py:153
  52.6 4.4 %collective-permute-start.5 = (bf16[8,3712]{1,0:T(8,128)(2,1)S(1)}, bf16[8,3712]{1,0:T(8,128)(2,1)S(1)}, u32[]{:S(2)}, u32[]{:S(2)}) collective-permute-start(bf16[8,3712]{1,0:T(8,128)(2,1)S(1)} %slice.79), channel_id=1, source_target_pairs={{0,2},{1,3},{2,0},{3,1},{4,6},{5,7},{6,4},{7,5},{8,10},{9,11},{10,... | collective-permute-start | bytes 178184 | tf_op jit(solution)/shard_map/ppermute | solution.py:153
  54.2 4.3 %collective-permute-start.9 = (bf16[8,3712]{1,0:T(8,128)(2,1)S(1)}, bf16[8,3712]{1,0:T(8,128)(2,1)S(1)}, u32[]{:S(2)}, u32[]{:S(2)}) collective-permute-start(bf16[8,3712]{1,0:T(8,128)(2,1)S(1)} %slice.78), channel_id=1, source_target_pairs={{0,2},{1,3},{2,0},{3,1},{4,6},{5,7},{6,4},{7,5},{8,10},{9,11},{10,... | collective-permute-start | bytes 178184 | tf_op jit(solution)/shard_map/ppermute | solution.py:153
  57.0 4.0 %collective-permute-start.6 = (bf16[4,3712]{1,0:T(4,128)(2,1)S(1)}, bf16[4,3712]{1,0:T(4,128)(2,1)S(1)}, u32[]{:S(2)}, u32[]{:S(2)}) collective-permute-start(bf16[4,3712]{1,0:T(4,128)(2,1)S(1)} %slice.81), channel_id=1, source_target_pairs={{0,4},{1,5},{2,6},{3,7},{4,0},{5,1},{6,2},{7,3},{8,12},{9,13},{10,... | collective-permute-start | bytes 89096 | tf_op jit(solution)/shard_map/ppermute | solution.py:153
  58.5 4.0 %collective-permute-start.10 = (bf16[4,3712]{1,0:T(4,128)(2,1)S(1)}, bf16[4,3712]{1,0:T(4,128)(2,1)S(1)}, u32[]{:S(2)}, u32[]{:S(2)}) collective-permute-start(bf16[4,3712]{1,0:T(4,128)(2,1)S(1)} %slice.80), channel_id=1, source_target_pairs={{0,4},{1,5},{2,6},{3,7},{4,0},{5,1},{6,2},{7,3},{8,12},{9,13},{10,... | collective-permute-start | bytes 89096 | tf_op jit(solution)/shard_map/ppermute | solution.py:153
  61.1 4.7 %collective-permute-start.7 = (bf16[2,3712]{1,0:T(2,128)(2,1)S(1)}, bf16[2,3712]{1,0:T(2,128)(2,1)S(1)}, u32[]{:S(2)}, u32[]{:S(2)}) collective-permute-start(bf16[2,3712]{1,0:T(2,128)(2,1)S(1)} %slice.83), channel_id=1, source_target_pairs={{0,8},{1,9},{2,10},{3,11},{4,12},{5,13},{6,14},{7,15},{8,0},{9,1},... | collective-permute-start | bytes 44552 | tf_op jit(solution)/shard_map/ppermute | solution.py:153
  62.6 4.7 %collective-permute-start.11 = (bf16[2,3712]{1,0:T(2,128)(2,1)S(1)}, bf16[2,3712]{1,0:T(2,128)(2,1)S(1)}, u32[]{:S(2)}, u32[]{:S(2)}) collective-permute-start(bf16[2,3712]{1,0:T(2,128)(2,1)S(1)} %slice.82), channel_id=1, source_target_pairs={{0,8},{1,9},{2,10},{3,11},{4,12},{5,13},{6,14},{7,15},{8,0},{9,1},... | collective-permute-start | bytes 44552 | tf_op jit(solution)/shard_map/ppermute | solution.py:153

commit v2 on v1

v2 whole, which is shorter than its diff:
```python
import functools

import jax
import jax.numpy as jnp
from jax import lax
from jax.experimental import pallas as pl
from jax.experimental.pallas import tpu as pltpu
from jax.sharding import PartitionSpec as P

MIB = 1 << 20
VMEM = pl.BlockSpec(memory_space=pltpu.VMEM)
HBM = pl.BlockSpec(memory_space=pltpu.HBM)
ANY = pl.BlockSpec(memory_space=pl.ANY)
BLOCKS = 4
CHUNKS = 2


def cost(flops, moved):
    return pl.CostEstimate(flops=flops, bytes_accessed=moved, transcendentals=0)


def load_kernel(start, source, *rest):
    piece, token, sem = rest[-3:]
    copy = pltpu.make_async_copy(source.at[pl.ds(start, piece.shape[0])], piece, sem)
    copy.start()
    token[...] = jnp.zeros_like(token)
    copy.wait()


def load(source, after, start, rows):
    shape = (rows, source.shape[1])
    return pl.pallas_call(
        functools.partial(load_kernel, start),
        out_shape=(pltpu.VMEM(shape, source.dtype), pltpu.VMEM((8, 128), jnp.float32)),
        in_specs=[HBM] + [ANY] * len(after),
        out_specs=(VMEM, VMEM),
        scratch_shapes=[pltpu.SemaphoreType.DMA],
        compiler_params=pltpu.CompilerParams(vmem_limit_bytes=1 * MIB),
        cost_estimate=cost(0, 2 * rows * source.shape[1]),
    )(source, *after)


def join_kernel(count, *refs):
    joined = refs[-1]
    at = 0
    for part in refs[:count]:
        joined[at : at + part.shape[0], :] = part[...]
        at += part.shape[0]


def join(parts, tokens):
    rows, width = sum(part.shape[0] for part in parts), parts[0].shape[1]
    return pl.pallas_call(
        functools.partial(join_kernel, len(parts)),
        out_shape=pltpu.VMEM((rows, width), parts[0].dtype),
        in_specs=[VMEM] * len(parts) + [ANY] * len(tokens),
        out_specs=VMEM,
        compiler_params=pltpu.CompilerParams(vmem_limit_bytes=2 * MIB),
        cost_estimate=cost(0, 4 * rows * width),
    )(*parts, *tokens)


def hidden_kernel(rows, mine, theirs, g0, u0, g1, u1, gate, up, down, hidden, d0, d1, d2, tokens, g2, u2, g3, u3, sems):
    def copy(source, block, into, sem):
        return pltpu.make_async_copy(source.at[pl.ds(block * rows, rows)], into, sems.at[sem])

    streamed = [
        copy(gate, 2, g2, 0),
        copy(up, 2, u2, 1),
        copy(gate, 3, g3, 2),
        copy(up, 3, u3, 3),
        copy(down, 0, d0, 4),
        copy(down, 1, d1, 5),
        copy(down, 2, d2, 6),
    ]
    streamed[0].start()
    streamed[1].start()
    half = mine.shape[0]
    tokens[:half, :] = mine[...]
    tokens[half:, :] = theirs[...]
    contract = (((1,), (1,)), ((), ()))

    def product(weight):
        return lax.dot_general(weight[...], tokens[...], contract, preferred_element_type=jnp.float32)

    def finish(block, gate_value, up_value):
        value = gate_value / (1.0 + jnp.exp(-gate_value)) * up_value
        hidden[block * rows : (block + 1) * rows, :] = value.astype(hidden.dtype)

    gate_value = product(g0)
    streamed[2].start()
    finish(0, gate_value, product(u0))
    streamed[3].start()
    gate_value = product(g1)
    streamed[4].start()
    finish(1, gate_value, product(u1))
    streamed[5].start()
    streamed[0].wait()
    gate_value = product(g2)
    streamed[6].start()
    streamed[1].wait()
    finish(2, gate_value, product(u2))
    streamed[2].wait()
    gate_value = product(g3)
    streamed[3].wait()
    finish(3, gate_value, product(u3))
    for one in streamed[4:]:
        one.wait()


def hidden_of(mine, theirs, pieces, gate, up, down):
    rows, width = pieces[0].shape
    count = mine.shape[0] + theirs.shape[0]
    block = pltpu.VMEM((rows, width), gate.dtype)
    return pl.pallas_call(
        functools.partial(hidden_kernel, rows),
        out_shape=(pltpu.VMEM((gate.shape[0], count), gate.dtype),) + (pltpu.VMEM((rows, width), gate.dtype),) * 3,
        in_specs=[VMEM] * 6 + [HBM] * 3,
        out_specs=(VMEM,) * 4,
        input_output_aliases={2: 1, 3: 2, 4: 3},
        scratch_shapes=[pltpu.VMEM((count, width), mine.dtype)] + [block] * 4 + [pltpu.SemaphoreType.DMA((7,))],
        compiler_params=pltpu.CompilerParams(vmem_limit_bytes=8 * rows * width + 7 * MIB),
        cost_estimate=cost(4 * count * gate.size, 4 * gate.size),
    )(*(pltpu.with_memory_space_constraint(one, pltpu.VMEM) for one in (mine, theirs, *pieces)), gate, up, down)


def down_kernel(start, hidden, d0, d1, d2, down, keep, send, d3, sem):
    rows, columns = d0.shape[0], keep.shape[1]
    half = keep.shape[0]
    copy = pltpu.make_async_copy(down.at[pl.ds(3 * rows, rows), pl.ds(start, columns)], d3, sem)
    copy.start()
    total = None
    for block, piece in enumerate((d0, d1, d2, d3)):
        if block == 3:
            copy.wait()
        value = lax.dot_general(
            hidden[block * rows : (block + 1) * rows, :],
            d3[...] if block == 3 else piece[:, start : start + columns],
            (((0,), (0,)), ((), ())),
            preferred_element_type=jnp.float32,
        )
        total = value if total is None else total + value
    keep[...] = total[:half]
    send[...] = total[half:].astype(send.dtype)


def down_of(hidden, pieces, down, start, columns):
    half = hidden.shape[1] // 2
    rows = pieces[0].shape[0]
    return pl.pallas_call(
        functools.partial(down_kernel, start),
        out_shape=(pltpu.VMEM((half, columns), jnp.float32), pltpu.VMEM((half, columns), jnp.bfloat16)),
        in_specs=[VMEM] * 4 + [HBM],
        out_specs=(VMEM, VMEM),
        scratch_shapes=[pltpu.VMEM((rows, columns), down.dtype), pltpu.SemaphoreType.DMA],
        compiler_params=pltpu.CompilerParams(vmem_limit_bytes=8 * MIB),
        cost_estimate=cost(4 * half * hidden.shape[0] * columns, 2 * hidden.shape[0] * columns),
    )(hidden, *pieces, down)


def fold_kernel(keep, came, kept, *sends):
    total = keep[...] + came[...].astype(jnp.float32)
    rows = kept.shape[0]
    kept[...] = total[:rows]
    for at, send in enumerate(sends):
        send[...] = total[(at + 1) * rows : (at + 2) * rows].astype(send.dtype)


def fold(keep, came, ways):
    rows, columns = keep.shape[0] // ways, keep.shape[1]
    return pl.pallas_call(
        fold_kernel,
        out_shape=(pltpu.VMEM((rows, columns), jnp.float32),)
        + (pltpu.VMEM((rows, columns), jnp.bfloat16),) * (ways - 1),
        in_specs=[VMEM, VMEM],
        out_specs=(VMEM,) * ways,
        compiler_params=pltpu.CompilerParams(vmem_limit_bytes=2 * MIB),
        cost_estimate=cost(0, 8 * keep.size),
    )(keep, came)


def exchange(array, mask, count):
    return lax.ppermute(array, "tensor", [(i, i ^ mask) for i in range(count)])


def masked(terms, own, valid_counts):
    keep = jnp.arange(own, dtype=jnp.int32)[:, None] < valid_counts[0]
    return jnp.where(keep, terms, 0.0).astype(jnp.bfloat16)


def reduced(keep, send, masks, count):
    for at, mask in enumerate(masks):
        total = keep + exchange(send, mask, count).astype(jnp.float32)
        if at + 1 == len(masks):
            return total
        rows = total.shape[0] // 2
        keep, send = total[:rows], total[rows:].astype(jnp.bfloat16)


def plain(count, masks, tokens, gate_weight, up_weight, down_weight, valid_counts):
    own = tokens.shape[0]
    gathered = tokens
    for mask in reversed(masks):
        gathered = jnp.concatenate([gathered, exchange(gathered, mask, count)], axis=0)
    gate_value = jnp.dot(gathered, gate_weight, preferred_element_type=jnp.float32)
    up_value = jnp.dot(gathered, up_weight, preferred_element_type=jnp.float32)
    hidden = (jax.nn.silu(gate_value) * up_value).astype(jnp.bfloat16)
    terms = jnp.dot(hidden, down_weight, preferred_element_type=jnp.float32)
    half = terms.shape[0] // 2
    total = reduced(terms[:half], terms[half:].astype(jnp.bfloat16), masks, count)
    return masked(total, own, valid_counts)


def per_device(count, masks, tokens, gate_weight, up_weight, down_weight, valid_counts):
    own, width = tokens.shape
    gate, up, down = (
        pltpu.with_memory_space_constraint(one, pltpu.HBM) for one in (gate_weight.T, up_weight.T, down_weight)
    )
    rows = gate.shape[0] // BLOCKS
    *single, far, farther = masks
    direct = [far, farther, far | farther]
    g0, token = load(gate, (), 0, rows)
    u0, other = load(up, (token,), 0, rows)
    mine = join([tokens] + [exchange(tokens, mask, count) for mask in direct], [token, other])
    pieces = [g0, u0]
    for mask, source in zip(reversed(single[1:]), (gate,)):
        theirs = exchange(mine, mask, count)
        piece, token = load(source, (mine,), rows, rows)
        pieces.append(piece)
        mine = join([mine, theirs], [token])
    theirs = exchange(mine, single[0], count)
    pieces.append(load(up, (mine,), rows, rows)[0])
    hidden, *down_pieces = hidden_of(mine, theirs, pieces, gate, up, down)
    columns = width // CHUNKS
    parts = []
    for chunk in range(CHUNKS):
        keep, send = down_of(hidden, down_pieces, down, chunk * columns, columns)
        for mask in single:
            ways = 4 if mask == single[-1] else 2
            keep, *sends = fold(keep, exchange(send, mask, count), ways)
            send = sends[0]
        for mask, send in zip(direct, sends):
            keep = keep + exchange(send, mask, count).astype(jnp.float32)
        parts.append(keep)
    return masked(jnp.concatenate(parts, axis=1), own, valid_counts)


def solution(mesh):
    count = mesh.shape["tensor"]
    masks = [1 << bit for bit in range(count.bit_length() - 1)]

    def step(tokens, gate_weight, up_weight, down_weight, valid_counts):
        hidden_rows, width = down_weight.shape
        fits = 8 * hidden_rows * width <= 2 * 56 * MIB
        whole_tiles = hidden_rows % (16 * BLOCKS) == 0 and width % (128 * CHUNKS) == 0
        small = (tokens.shape[0] << len(masks)) <= 64 and len(masks) == 4
        use = per_device if fits and whole_tiles and small else plain
        return use(count, masks, tokens, gate_weight, up_weight, down_weight, valid_counts)

    return jax.shard_map(
        step,
        mesh=mesh,
        in_specs=(
            P(("groups", "tensor"), None),
            P(None, "tensor"),
            P(None, "tensor"),
            P("tensor", None),
            P(("groups", "tensor")),
        ),
        out_specs=P(("groups", "tensor"), None),
        check_vma=False,
    )
```

time: 68.3 us -> 72.4 us (1.060)
  starting transfers between devices: 16.4 us -> 19.5 us
  Pallas kernels: 41.9 us -> 44 us
  local copies, waits for them, and re-layouts: 1.56 us -> 0.01 us
    ppermute x12 -> x15, starting transfers between devices: 16.4 us -> 19.5 us  [exchange(): return lax.ppermute(array, 'tensor', [(i, i ^ mask) for i in range(count)])]
    pallas_call x2, Pallas kernels: 4.49 us -> 6.62 us  [down_of(): pl.pallas_call(functools.partial(down_kernel, start), out_shape=(pltpu.VM...]
    unnamed x8 -> x2, local copies, waits for them, and re-layouts: 1.47 us -> 0.01 us
    ppermute x12 -> x15, waiting for transfers between devices: 6.4 us -> 6.93 us  [exchange(): return lax.ppermute(array, 'tensor', [(i, i ^ mask) for i in range(count)])]
  transfers between devices with their start and end apart: 12 -> 15, of which waited for: 6 -> 5; matrix products, arithmetic and copies ran while one was open for 0% -> 0% of each run, Pallas kernels for 22% -> 22%
where the time goes in v2:
time: 72.4 us; the launch traced here: 72 us
  Pallas kernels  44 us (61%)
  starting transfers between devices  19.5 us (27%)
  waiting for transfers between devices  6.93 us (10%)
  between operations  0.83 us (1%)
  other arithmetic  0.77 us (1%)
    pallas_call x1, Pallas kernels, hidden_of(): pl.pallas_call(functools.partial(hidden_kernel, rows), out_shape=(pltpu.V...  24.8 us
    ppermute x15, starting transfers between devices, exchange(): return lax.ppermute(array, 'tensor', [(i, i ^ mask) for i in range(count)])  19.5 us
    pallas_call x4, Pallas kernels, load(): pl.pallas_call(functools.partial(load_kernel, start), out_shape=(pltpu.VM...  12.5 us
    ppermute x15, waiting for transfers between devices, exchange(): return lax.ppermute(array, 'tensor', [(i, i ^ mask) for i in range(count)])  6.93 us
    pallas_call x2, Pallas kernels, down_of(): pl.pallas_call(functools.partial(down_kernel, start), out_shape=(pltpu.VM...  6.62 us
  transfers between devices with their start and end apart: 15, of which 5 were waited for; matrix products, arithmetic and copies ran while one was open for 0% of the time, Pallas kernels for 22%

profile of v2, /device:TPU:0, one launch (start us, length us, event | category | flops | bytes accessed | tf_op | source)
XLA Modules:
  0.0 72.0 jit_solution(12395233137273602053)
XLA Ops:
  0.0 3.0 %collective-permute-start = (bf16[2,7424]{1,0:T(2,128)(2,1)}, bf16[2,7424]{1,0:T(2,128)(2,1)S(1)}, u32[]{:S(2)}, u32[]{:S(2)}) collective-permute-start(bf16[2,7424]{1,0:T(2,128)(2,1)} %refs_0_.1), channel_id=1, source_target_pairs={{0,4},{1,5},{2,6},{3,7},{4,0},{5,1},{6,2},{7,3},{8,12},{9,13},{10,... | collective-permute-start | bytes 89096 | tf_op jit(solution)/shard_map/ppermute | solution.py:183
  3.0 2.6 %collective-permute-start.1 = (bf16[2,7424]{1,0:T(2,128)(2,1)}, bf16[2,7424]{1,0:T(2,128)(2,1)S(1)}, u32[]{:S(2)}, u32[]{:S(2)}) collective-permute-start(bf16[2,7424]{1,0:T(2,128)(2,1)} %refs_0_.1), channel_id=1, source_target_pairs={{0,8},{1,9},{2,10},{3,11},{4,12},{5,13},{6,14},{7,15},{8,0},{9,1},... | collective-permute-start | bytes 89096 | tf_op jit(solution)/shard_map/ppermute | solution.py:183
  5.6 0.0 collective-permute-start.2
  5.6 3.0 %shard_map.55 = (bf16[464,7424]{1,0:T(8,128)(2,1)S(1)}, f32[8,128]{1,0:T(8,128)S(1)}) custom-call(bf16[1856,7424]{1,0:T(8,128)(2,1)} %bitcast.4), custom_call_target="tpu_custom_call" | custom-call | bytes 6889472 | tf_op jit(solution)/shard_map/pallas_call | solution.py:32
  8.6 0.0 copy-start
  8.6 3.0 %shard_map.56 = (bf16[464,7424]{1,0:T(8,128)(2,1)S(1)}, f32[8,128]{1,0:T(8,128)S(1)}) custom-call(bf16[1856,7424]{1,0:T(8,128)(2,1)} %bitcast.7, f32[8,128]{1,0:T(8,128)S(1)} %get-tuple-element.32.rest_0_.refs_4_), custom_call_target="tpu_custom_call" | custom-call | bytes 6889472 | tf_op jit(solution)/shard_map/pallas_call | solution.py:32
  11.6 0.0 collective-permute-done.refs_1_
  11.6 0.0 collective-permute-done.2.refs_3_
  11.6 0.1 shard_map.57.rest_0_.refs_0_
  11.7 1.8 %collective-permute-start.3 = (bf16[8,7424]{1,0:T(8,128)(2,1)S(1)}, bf16[8,7424]{1,0:T(8,128)(2,1)S(1)}, u32[]{:S(2)}, u32[]{:S(2)}) collective-permute-start(bf16[8,7424]{1,0:T(8,128)(2,1)S(1)} %shard_map.57.rest_0_.refs_0_), channel_id=1, source_target_pairs={{0,2},{1,3},{2,0},{3,1},{4,6},{5,7},{6,4},{7,5},{8,10},{9,11},{10,... | collective-permute-start | bytes 356360 | tf_op jit(solution)/shard_map/ppermute | solution.py:183
  13.5 3.0 %shard_map.58 = (bf16[464,7424]{1,0:T(8,128)(2,1)S(1)}, f32[8,128]{1,0:T(8,128)S(1)}) custom-call(bf16[1856,7424]{1,0:T(8,128)(2,1)} %bitcast.5, bf16[8,7424]{1,0:T(8,128)(2,1)S(1)} %shard_map.57.rest_0_.refs_0_), custom_call_target="tpu_custom_call" | custom-call | bytes 6889472 | tf_op jit(solution)/shard_map/pallas_call | solution.py:32
  16.5 0.1 collective-permute-done.3.refs_1_
  16.6 0.1 collective-permute-start.4
  16.7 3.6 %shard_map.60 = (bf16[464,7424]{1,0:T(8,128)(2,1)S(1)}, f32[8,128]{1,0:T(8,128)}) custom-call(bf16[1856,7424]{1,0:T(8,128)(2,1)} %bitcast.8, bf16[16,7424]{1,0:T(8,128)(2,1)S(1)} %shard_map.59.rest_0_.mine), custom_call_target="tpu_custom_call" | custom-call | bytes 6889472 | tf_op jit(solution)/shard_map/pallas_call | solution.py:32
  20.3 0.0 collective-permute-done.4.theirs
  20.3 24.8 %shard_map.61 = (bf16[1856,32]{1,0:T(8,128)(2,1)S(1)}, bf16[464,7424]{1,0:T(8,128)(2,1)S(1)}, bf16[464,7424]{1,0:T(8,128)(2,1)S(1)}, bf16[464,7424]{1,0:T(8,128)(2,1)S(1)}) custom-call(bf16[16,7424]{1,0:T(8,128)(2,1)S(1)} %shard_map.59.rest_0_.mine, ...), custom_call_target="tpu_custom_call", output_to_operand_aliasing={{1}: (2, {}), {2}: (3, {}), {3}: (4, {})} | custom-call | flops 1763704832 | bytes 55115776 | tf_op jit(solution)/shard_map/pallas_call | solution.py:115
  45.1 3.3 %shard_map.62 = (f32[16,3712]{1,0:T(8,128)S(1)}, bf16[16,3712]{1,0:T(8,128)(2,1)S(1)}) custom-call(bf16[1856,32]{1,0:T(8,128)(2,1)S(1)} %get-tuple-element.39.hidden, bf16[464,7424]{1,0:T(8,128)(2,1)S(1)} %get-tuple-element.40.d0, bf16[464,7424]{1,0:T(8,128)(2,1)S(1)} %get-tuple-element.41.d1, bf16[464,7424]{1,0:T(8,128)(2,1)S(1)} %get-tuple-element.42.d2, ...), custom_call_target="tpu_custom_call" | custom-call | flops 440926208 | bytes 13778944 | tf_op jit(solution)/shard_map/pallas_call | solution.py:150
  48.4 0.6 collective-permute-start.5
  48.9 3.3 %shard_map.65 = (f32[16,3712]{1,0:T(8,128)S(1)}, bf16[16,3712]{1,0:T(8,128)(2,1)S(1)}) custom-call(bf16[1856,32]{1,0:T(8,128)(2,1)S(1)} %get-tuple-element.39.hidden, bf16[464,7424]{1,0:T(8,128)(2,1)S(1)} %get-tuple-element.40.d0, bf16[464,7424]{1,0:T(8,128)(2,1)S(1)} %get-tuple-element.41.d1, bf16[464,7424]{1,0:T(8,128)(2,1)S(1)} %get-tuple-element.42.d2, ...), custom_call_target="tpu_custom_call" | custom-call | flops 440926208 | bytes 13778944 | tf_op jit(solution)/shard_map/pallas_call | solution.py:150
  52.3 0.1 collective-permute-start.10
  52.4 1.8 %collective-permute-start.6 = (bf16[8,3712]{1,0:T(8,128)(2,1)S(1)}, bf16[8,3712]{1,0:T(8,128)(2,1)S(1)}, u32[]{:S(2)}, u32[]{:S(2)}) collective-permute-start(bf16[8,3712]{1,0:T(8,128)(2,1)S(1)} %get-tuple-element.46), channel_id=1, source_target_pairs={{0,2},{1,3},{2,0},{3,1},{4,6},{5,7},{6,4},{7,5},{8,10},{9,11},{10,... | collective-permute-start | bytes 178184 | tf_op jit(solution)/shard_map/ppermute | solution.py:183
  54.9 0.6 collective-permute-start.11
  55.5 1.3 %collective-permute-done.6.came = bf16[8,3712]{1,0:T(8,128)(2,1)S(1)} collective-permute-done((bf16[8,3712]{1,0:T(8,128)(2,1)S(1)}, bf16[8,3712]{1,0:T(8,128)(2,1)S(1)}, u32[]{:S(2)}, u32[]{:S(2)}) %collective-permute-start.6) | collective-permute-done | bytes 59424 | tf_op jit(solution)/shard_map/ppermute | solution.py:183
  56.8 1.0 %collective-permute-start.7 = (bf16[2,3712]{1,0:T(2,128)(2,1)S(1)}, bf16[2,3712]{1,0:T(2,128)(2,1)S(1)}, u32[]{:S(2)}, u32[]{:S(2)}) collective-permute-start(bf16[2,3712]{1,0:T(2,128)(2,1)S(1)} %get-tuple-element.48), channel_id=1, source_target_pairs={{0,4},{1,5},{2,6},{3,7},{4,0},{5,1},{6,2},{7,3},{8,12},{9,13},{10,... | collective-permute-start | bytes 44552 | tf_op jit(solution)/shard_map/ppermute | solution.py:183
  57.8 3.5 %collective-permute-start.8 = (bf16[2,3712]{1,0:T(2,128)(2,1)S(1)}, bf16[2,3712]{1,0:T(2,128)(2,1)S(1)}, u32[]{:S(2)}, u32[]{:S(2)}) collective-permute-start(bf16[2,3712]{1,0:T(2,128)(2,1)S(1)} %get-tuple-element.49), channel_id=1, source_target_pairs={{0,8},{1,9},{2,10},{3,11},{4,12},{5,13},{6,14},{7,15},{8,0},{9,1},... | collective-permute-start | bytes 44552 | tf_op jit(solution)/shard_map/ppermute | solution.py:183
  61.3 0.6 collective-permute-start.12
  62.0 3.8 %collective-permute-start.13 = (bf16[2,3712]{1,0:T(2,128)(2,1)S(1)}, bf16[2,3712]{1,0:T(2,128)(2,1)S(1)}, u32[]{:S(2)}, u32[]{:S(2)}) collective-permute-start(bf16[2,3712]{1,0:T(2,128)(2,1)S(1)} %get-tuple-element.57), channel_id=1, source_target_pairs={{0,8},{1,9},{2,10},{3,11},{4,12},{5,13},{6,14},{7,15},{8,0},{9,1},... | collective-permute-start | bytes 44552 | tf_op jit(solution)/shard_map/ppermute | solution.py:183
  65.8 0.0 collective-permute-start.14
  65.8 1.0 %collective-permute-done.9 = bf16[2,3712]{1,0:T(2,128)(2,1)S(1)} collective-permute-done((bf16[2,3712]{1,0:T(2,128)(2,1)S(1)}, bf16[2,3712]{1,0:T(2,128)(2,1)S(1)}, u32[]{:S(2)}, u32[]{:S(2)}) %collective-permute-start.9) | collective-permute-done | bytes 14880 | tf_op jit(solution)/shard_map/ppermute | solution.py:183
  66.9 0.8 %collective-permute-done.13 = bf16[2,3712]{1,0:T(2,128)(2,1)S(1)} collective-permute-done((bf16[2,3712]{1,0:T(2,128)(2,1)S(1)}, bf16[2,3712]{1,0:T(2,128)(2,1)S(1)}, u32[]{:S(2)}, u32[]{:S(2)}) %collective-permute-start.13) | collective-permute-done | bytes 14880 | tf_op jit(solution)/shard_map/ppermute | solution.py:183
  67.6 3.7 %collective-permute-done.14 = bf16[2,3712]{1,0:T(2,128)(2,1)S(1)} collective-permute-done((bf16[2,3712]{1,0:T(2,128)(2,1)S(1)}, bf16[2,3712]{1,0:T(2,128)(2,1)S(1)}, u32[]{:S(2)}, u32[]{:S(2)}) %collective-permute-start.14) | collective-permute-done | bytes 14880 | tf_op jit(solution)/shard_map/ppermute | solution.py:183
  71.3 0.7 fusion
  (17 shorter events, 0.2 us)
Async XLA Ops:
  0.0 11.6 %collective-permute-start = (bf16[2,7424]{1,0:T(2,128)(2,1)}, bf16[2,7424]{1,0:T(2,128)(2,1)S(1)}, u32[]{:S(2)}, u32[]{:S(2)}) collective-permute-start(bf16[2,7424]{1,0:T(2,128)(2,1)} %refs_0_.1), channel_id=1, source_target_pairs={{0,4},{1,5},{2,6},{3,7},{4,0},{5,1},{6,2},{7,3},{8,12},{9,13},{10,... | collective-permute-start | bytes 89096 | tf_op jit(solution)/shard_map/ppermute | solution.py:183
  3.0 8.6 %collective-permute-start.1 = (bf16[2,7424]{1,0:T(2,128)(2,1)}, bf16[2,7424]{1,0:T(2,128)(2,1)S(1)}, u32[]{:S(2)}, u32[]{:S(2)}) collective-permute-start(bf16[2,7424]{1,0:T(2,128)(2,1)} %refs_0_.1), channel_id=1, source_target_pairs={{0,8},{1,9},{2,10},{3,11},{4,12},{5,13},{6,14},{7,15},{8,0},{9,1},... | collective-permute-start | bytes 89096 | tf_op jit(solution)/shard_map/ppermute | solution.py:183
  5.6 6.0 %collective-permute-start.2 = (bf16[2,7424]{1,0:T(2,128)(2,1)}, bf16[2,7424]{1,0:T(2,128)(2,1)S(1)}, u32[]{:S(2)}, u32[]{:S(2)}) collective-permute-start(bf16[2,7424]{1,0:T(2,128)(2,1)} %refs_0_.1), channel_id=1, source_target_pairs={{0,12},{1,13},{2,14},{3,15},{4,8},{5,9},{6,10},{7,11},{8,4},{9,5},... | collective-permute-start | bytes 89096 | tf_op jit(solution)/shard_map/ppermute | solution.py:183
  8.6 3.0 %copy-start = (bf16[2,7424]{1,0:T(2,128)(2,1)S(1)}, bf16[2,7424]{1,0:T(2,128)(2,1)}, u32[]{:S(2)}) copy-start(bf16[2,7424]{1,0:T(2,128)(2,1)} %refs_0_.1) | copy-start | bytes 89092
  11.7 4.9 %collective-permute-start.3 = (bf16[8,7424]{1,0:T(8,128)(2,1)S(1)}, bf16[8,7424]{1,0:T(8,128)(2,1)S(1)}, u32[]{:S(2)}, u32[]{:S(2)}) collective-permute-start(bf16[8,7424]{1,0:T(8,128)(2,1)S(1)} %shard_map.57.rest_0_.refs_0_), channel_id=1, source_target_pairs={{0,2},{1,3},{2,0},{3,1},{4,6},{5,7},{6,4},{7,5},{8,10},{9,11},{10,... | collective-permute-start | bytes 356360 | tf_op jit(solution)/shard_map/ppermute | solution.py:183
  16.6 3.6 %collective-permute-start.4 = (bf16[16,7424]{1,0:T(8,128)(2,1)S(1)}, bf16[16,7424]{1,0:T(8,128)(2,1)S(1)}, u32[]{:S(2)}, u32[]{:S(2)}) collective-permute-start(bf16[16,7424]{1,0:T(8,128)(2,1)S(1)} %shard_map.59.rest_0_.mine), channel_id=1, source_target_pairs={{0,1},{1,0},{2,3},{3,2},{4,5},{5,4},{6,7},{7,6},{8,9},{9,8},{10,11... | collective-permute-start | bytes 712712 | tf_op jit(solution)/shard_map/ppermute | solution.py:183
  48.4 4.0 %collective-permute-start.5 = (bf16[16,3712]{1,0:T(8,128)(2,1)S(1)}, bf16[16,3712]{1,0:T(8,128)(2,1)S(1)}, u32[]{:S(2)}, u32[]{:S(2)}) collective-permute-start(bf16[16,3712]{1,0:T(8,128)(2,1)S(1)} %get-tuple-element.44), channel_id=1, source_target_pairs={{0,1},{1,0},{2,3},{3,2},{4,5},{5,4},{6,7},{7,6},{8,9},{9,8},{10,11... | collective-permute-start | bytes 356360 | tf_op jit(solution)/shard_map/ppermute | solution.py:183
  52.3 2.6 %collective-permute-start.10 = (bf16[16,3712]{1,0:T(8,128)(2,1)S(1)}, bf16[16,3712]{1,0:T(8,128)(2,1)S(1)}, u32[]{:S(2)}, u32[]{:S(2)}) collective-permute-start(bf16[16,3712]{1,0:T(8,128)(2,1)S(1)} %get-tuple-element.52), channel_id=1, source_target_pairs={{0,1},{1,0},{2,3},{3,2},{4,5},{5,4},{6,7},{7,6},{8,9},{9,8},{10,11... | collective-permute-start | bytes 356360 | tf_op jit(solution)/shard_map/ppermute | solution.py:183
  52.4 4.4 %collective-permute-start.6 = (bf16[8,3712]{1,0:T(8,128)(2,1)S(1)}, bf16[8,3712]{1,0:T(8,128)(2,1)S(1)}, u32[]{:S(2)}, u32[]{:S(2)}) collective-permute-start(bf16[8,3712]{1,0:T(8,128)(2,1)S(1)} %get-tuple-element.46), channel_id=1, source_target_pairs={{0,2},{1,3},{2,0},{3,1},{4,6},{5,7},{6,4},{7,5},{8,10},{9,11},{10,... | collective-permute-start | bytes 178184 | tf_op jit(solution)/shard_map/ppermute | solution.py:183
  54.9 6.4 %collective-permute-start.11 = (bf16[8,3712]{1,0:T(8,128)(2,1)S(1)}, bf16[8,3712]{1,0:T(8,128)(2,1)S(1)}, u32[]{:S(2)}, u32[]{:S(2)}) collective-permute-start(bf16[8,3712]{1,0:T(8,128)(2,1)S(1)} %get-tuple-element.54), channel_id=1, source_target_pairs={{0,2},{1,3},{2,0},{3,1},{4,6},{5,7},{6,4},{7,5},{8,10},{9,11},{10,... | collective-permute-start | bytes 178184 | tf_op jit(solution)/shard_map/ppermute | solution.py:183
  56.8 9.0 %collective-permute-start.7 = (bf16[2,3712]{1,0:T(2,128)(2,1)S(1)}, bf16[2,3712]{1,0:T(2,128)(2,1)S(1)}, u32[]{:S(2)}, u32[]{:S(2)}) collective-permute-start(bf16[2,3712]{1,0:T(2,128)(2,1)S(1)} %get-tuple-element.48), channel_id=1, source_target_pairs={{0,4},{1,5},{2,6},{3,7},{4,0},{5,1},{6,2},{7,3},{8,12},{9,13},{10,... | collective-permute-start | bytes 44552 | tf_op jit(solution)/shard_map/ppermute | solution.py:183
  57.8 8.0 %collective-permute-start.8 = (bf16[2,3712]{1,0:T(2,128)(2,1)S(1)}, bf16[2,3712]{1,0:T(2,128)(2,1)S(1)}, u32[]{:S(2)}, u32[]{:S(2)}) collective-permute-start(bf16[2,3712]{1,0:T(2,128)(2,1)S(1)} %get-tuple-element.49), channel_id=1, source_target_pairs={{0,8},{1,9},{2,10},{3,11},{4,12},{5,13},{6,14},{7,15},{8,0},{9,1},... | collective-permute-start | bytes 44552 | tf_op jit(solution)/shard_map/ppermute | solution.py:183
  61.3 5.5 %collective-permute-start.9 = (bf16[2,3712]{1,0:T(2,128)(2,1)S(1)}, bf16[2,3712]{1,0:T(2,128)(2,1)S(1)}, u32[]{:S(2)}, u32[]{:S(2)}) collective-permute-start(bf16[2,3712]{1,0:T(2,128)(2,1)S(1)} %get-tuple-element.50), channel_id=1, source_target_pairs={{0,12},{1,13},{2,14},{3,15},{4,8},{5,9},{6,10},{7,11},{8,4},{9,5},... | collective-permute-start | bytes 44552 | tf_op jit(solution)/shard_map/ppermute | solution.py:183
  61.3 5.5 %collective-permute-start.12 = (bf16[2,3712]{1,0:T(2,128)(2,1)S(1)}, bf16[2,3712]{1,0:T(2,128)(2,1)S(1)}, u32[]{:S(2)}, u32[]{:S(2)}) collective-permute-start(bf16[2,3712]{1,0:T(2,128)(2,1)S(1)} %get-tuple-element.56), channel_id=1, source_target_pairs={{0,4},{1,5},{2,6},{3,7},{4,0},{5,1},{6,2},{7,3},{8,12},{9,13},{10,... | collective-permute-start | bytes 44552 | tf_op jit(solution)/shard_map/ppermute | solution.py:183
  62.0 5.7 %collective-permute-start.13 = (bf16[2,3712]{1,0:T(2,128)(2,1)S(1)}, bf16[2,3712]{1,0:T(2,128)(2,1)S(1)}, u32[]{:S(2)}, u32[]{:S(2)}) collective-permute-start(bf16[2,3712]{1,0:T(2,128)(2,1)S(1)} %get-tuple-element.57), channel_id=1, source_target_pairs={{0,8},{1,9},{2,10},{3,11},{4,12},{5,13},{6,14},{7,15},{8,0},{9,1},... | collective-permute-start | bytes 44552 | tf_op jit(solution)/shard_map/ppermute | solution.py:183
  65.8 5.5 %collective-permute-start.14 = (bf16[2,3712]{1,0:T(2,128)(2,1)S(1)}, bf16[2,3712]{1,0:T(2,128)(2,1)S(1)}, u32[]{:S(2)}, u32[]{:S(2)}) collective-permute-start(bf16[2,3712]{1,0:T(2,128)(2,1)S(1)} %get-tuple-element.58), channel_id=1, source_target_pairs={{0,12},{1,13},{2,14},{3,15},{4,8},{5,9},{6,10},{7,11},{8,4},{9,5},... | collective-permute-start | bytes 44552 | tf_op jit(solution)/shard_map/ppermute | solution.py:183

commit v3 on v2

v3 whole, which is shorter than its diff:
```python
import functools

import jax
import jax.numpy as jnp
from jax import lax
from jax.experimental import pallas as pl
from jax.experimental.pallas import tpu as pltpu
from jax.sharding import PartitionSpec as P

MIB = 1 << 20
VMEM = pl.BlockSpec(memory_space=pltpu.VMEM)
HBM = pl.BlockSpec(memory_space=pltpu.HBM)
ANY = pl.BlockSpec(memory_space=pl.ANY)
BLOCKS = 4
CHUNKS = 2
DEPTH = 2048


def cost(flops, moved):
    return pl.CostEstimate(flops=flops, bytes_accessed=moved, transcendentals=0)


def load_kernel(start, source, *rest):
    piece, token, sem = rest[-3:]
    copy = pltpu.make_async_copy(source.at[pl.ds(start, piece.shape[0])], piece, sem)
    copy.start()
    token[...] = jnp.zeros_like(token)
    copy.wait()


def load(source, after, start, rows):
    shape = (rows, source.shape[1])
    return pl.pallas_call(
        functools.partial(load_kernel, start),
        out_shape=(pltpu.VMEM(shape, source.dtype), pltpu.VMEM((8, 128), jnp.float32)),
        in_specs=[HBM] + [ANY] * len(after),
        out_specs=(VMEM, VMEM),
        scratch_shapes=[pltpu.SemaphoreType.DMA],
        compiler_params=pltpu.CompilerParams(vmem_limit_bytes=1 * MIB),
        cost_estimate=cost(0, 2 * rows * source.shape[1]),
    )(source, *after)


def join_kernel(count, *refs):
    joined = refs[-1]
    at = 0
    for part in refs[:count]:
        joined[at : at + part.shape[0], :] = part[...]
        at += part.shape[0]


def join(parts, tokens):
    rows, width = sum(part.shape[0] for part in parts), parts[0].shape[1]
    return pl.pallas_call(
        functools.partial(join_kernel, len(parts)),
        out_shape=pltpu.VMEM((rows, width), parts[0].dtype),
        in_specs=[VMEM] * len(parts) + [ANY] * len(tokens),
        out_specs=VMEM,
        compiler_params=pltpu.CompilerParams(vmem_limit_bytes=2 * MIB),
        cost_estimate=cost(0, 4 * rows * width),
    )(*parts, *tokens)


def hidden_kernel(rows, mine, theirs, g0, u0, g1, u1, gate, up, down, h0, h1, h2, h3, d0, d1, d2, d3, tokens, g2, u2, g3, u3, sems):
    order = [
        (gate, 2, g2),
        (up, 2, u2),
        (gate, 3, g3),
        (up, 3, u3),
        (down, 0, d0),
        (down, 1, d1),
        (down, 2, d2),
        (down, 3, d3),
    ]
    copies = [
        pltpu.make_async_copy(source.at[pl.ds(block * rows, rows)], into, sems.at[at])
        for at, (source, block, into) in enumerate(order)
    ]
    copies[0].start()
    copies[1].start()
    half, width = mine.shape
    tokens[:half, :] = mine[...]
    tokens[half:, :] = theirs[...]

    def product(weight):
        total = None
        for at in range(0, width, DEPTH):
            value = lax.dot_general(
                tokens[:, at : min(at + DEPTH, width)],
                weight[:, at : min(at + DEPTH, width)],
                (((1,), (1,)), ((), ())),
                preferred_element_type=jnp.float32,
            )
            total = value if total is None else total + value
        return total

    def finish(hidden, gate_value, up_value):
        value = gate_value / (1.0 + jnp.exp(-gate_value)) * up_value
        hidden[...] = value.astype(hidden.dtype)

    gate_value = product(g0)
    copies[2].start()
    finish(h0, gate_value, product(u0))
    copies[3].start()
    copies[4].start()
    gate_value = product(g1)
    copies[5].start()
    finish(h1, gate_value, product(u1))
    copies[6].start()
    copies[0].wait()
    gate_value = product(g2)
    copies[7].start()
    copies[1].wait()
    finish(h2, gate_value, product(u2))
    copies[2].wait()
    gate_value = product(g3)
    copies[3].wait()
    finish(h3, gate_value, product(u3))
    for copy in copies[4:]:
        copy.wait()


def hidden_of(mine, theirs, pieces, gate, up, down):
    rows, width = pieces[0].shape
    count = mine.shape[0] + theirs.shape[0]
    return pl.pallas_call(
        functools.partial(hidden_kernel, rows),
        out_shape=(pltpu.VMEM((count, rows), gate.dtype),) * 4 + (pltpu.VMEM((rows, width), gate.dtype),) * 4,
        in_specs=[VMEM] * 6 + [HBM] * 3,
        out_specs=(VMEM,) * 8,
        input_output_aliases={2: 4, 3: 5, 4: 6, 5: 7},
        scratch_shapes=[pltpu.VMEM((count, width), mine.dtype)]
        + [pltpu.VMEM((rows, width), gate.dtype)] * 4
        + [pltpu.SemaphoreType.DMA((8,))],
        compiler_params=pltpu.CompilerParams(vmem_limit_bytes=8 * rows * width + 4 * MIB),
        cost_estimate=cost(4 * count * gate.size, 4 * gate.size),
    )(*(pltpu.with_memory_space_constraint(one, pltpu.VMEM) for one in (mine, theirs, *pieces)), gate, up, down)


def down_kernel(start, *refs):
    hidden, pieces, (keep, send) = refs[:4], refs[4:8], refs[8:]
    half, columns = keep.shape
    total = None
    for part, piece in zip(hidden, pieces):
        value = jnp.dot(part[...], piece[:, start : start + columns], preferred_element_type=jnp.float32)
        total = value if total is None else total + value
    keep[...] = total[:half]
    send[...] = total[half:].astype(send.dtype)


def down_of(hidden, pieces, start, columns):
    half = hidden[0].shape[0] // 2
    rows = pieces[0].shape[0]
    return pl.pallas_call(
        functools.partial(down_kernel, start),
        out_shape=(pltpu.VMEM((half, columns), jnp.float32), pltpu.VMEM((half, columns), jnp.bfloat16)),
        in_specs=[VMEM] * 8,
        out_specs=(VMEM, VMEM),
        compiler_params=pltpu.CompilerParams(vmem_limit_bytes=4 * MIB),
        cost_estimate=cost(16 * half * rows * columns, 8 * rows * columns),
    )(*(pltpu.with_memory_space_constraint(one, pltpu.VMEM) for one in (*hidden, *pieces)))


def fold_kernel(keep, came, kept, send):
    rows = kept.shape[0]
    kept[...] = keep[:rows, :] + came[:rows, :].astype(jnp.float32)
    send[...] = (keep[rows:, :] + came[rows:, :].astype(jnp.float32)).astype(send.dtype)


def fold(keep, came):
    rows, columns = keep.shape[0] // 2, keep.shape[1]
    return pl.pallas_call(
        fold_kernel,
        out_shape=(pltpu.VMEM((rows, columns), jnp.float32), pltpu.VMEM((rows, columns), jnp.bfloat16)),
        in_specs=[VMEM, VMEM],
        out_specs=(VMEM, VMEM),
        compiler_params=pltpu.CompilerParams(vmem_limit_bytes=2 * MIB),
        cost_estimate=cost(0, 8 * keep.size),
    )(keep, came)


def last_kernel(counts, *refs):
    out = refs[-1]
    at = 0
    for keep, came in zip(refs[:-1:2], refs[1:-1:2]):
        rows, columns = keep.shape
        total = keep[...] + came[...].astype(jnp.float32)
        position = lax.broadcasted_iota(jnp.int32, (rows, columns), 0)
        total = jnp.where(position < counts[0], total, 0.0)
        out[:, at : at + columns] = total.astype(out.dtype)
        at += columns


def last(counts, parts):
    columns = sum(keep.shape[1] for keep, _ in parts)
    flat = [one for part in parts for one in part]
    return pl.pallas_call(
        last_kernel,
        out_shape=jax.ShapeDtypeStruct((flat[0].shape[0], columns), jnp.bfloat16),
        in_specs=[pl.BlockSpec(memory_space=pltpu.SMEM)] + [VMEM] * len(flat),
        out_specs=VMEM,
        compiler_params=pltpu.CompilerParams(vmem_limit_bytes=2 * MIB),
        cost_estimate=cost(0, 8 * columns),
    )(counts, *flat)


def exchange(array, mask, count):
    return lax.ppermute(array, "tensor", [(i, i ^ mask) for i in range(count)])


def masked(terms, own, valid_counts):
    keep = jnp.arange(own, dtype=jnp.int32)[:, None] < valid_counts[0]
    return jnp.where(keep, terms, 0.0).astype(jnp.bfloat16)


def reduced(keep, send, masks, count):
    for at, mask in enumerate(masks):
        total = keep + exchange(send, mask, count).astype(jnp.float32)
        if at + 1 == len(masks):
            return total
        rows = total.shape[0] // 2
        keep, send = total[:rows], total[rows:].astype(jnp.bfloat16)


def plain(count, masks, tokens, gate_weight, up_weight, down_weight, valid_counts):
    own = tokens.shape[0]
    gathered = tokens
    for mask in reversed(masks):
        gathered = jnp.concatenate([gathered, exchange(gathered, mask, count)], axis=0)
    gate_value = jnp.dot(gathered, gate_weight, preferred_element_type=jnp.float32)
    up_value = jnp.dot(gathered, up_weight, preferred_element_type=jnp.float32)
    hidden = (jax.nn.silu(gate_value) * up_value).astype(jnp.bfloat16)
    terms = jnp.dot(hidden, down_weight, preferred_element_type=jnp.float32)
    half = terms.shape[0] // 2
    total = reduced(terms[:half], terms[half:].astype(jnp.bfloat16), masks, count)
    return masked(total, own, valid_counts)


def per_device(count, masks, tokens, gate_weight, up_weight, down_weight, valid_counts):
    own, width = tokens.shape
    gate, up, down = (
        pltpu.with_memory_space_constraint(one, pltpu.HBM) for one in (gate_weight.T, up_weight.T, down_weight)
    )
    rows = gate.shape[0] // BLOCKS
    wanted = [(gate, 0), (up, 0), (gate, rows), (up, rows)]
    mine, after, pieces = tokens, (), []
    for mask, (source, start) in zip(reversed(masks), wanted):
        theirs = exchange(mine, mask, count)
        piece, token = load(source, after, start, rows)
        pieces.append(piece)
        if len(pieces) < len(masks):
            mine = join([mine, theirs], [token])
            after = (mine,)
    down_inputs = hidden_of(mine, theirs, pieces, gate, up, down)
    columns = width // CHUNKS
    parts = []
    for chunk in range(CHUNKS):
        keep, send = down_of(down_inputs[:4], down_inputs[4:], chunk * columns, columns)
        for mask in masks[:-1]:
            keep, send = fold(keep, exchange(send, mask, count))
        parts.append((keep, exchange(send, masks[-1], count)))
    return last(valid_counts, parts)


def solution(mesh):
    count = mesh.shape["tensor"]
    masks = [1 << bit for bit in range(count.bit_length() - 1)]

    def step(tokens, gate_weight, up_weight, down_weight, valid_counts):
        hidden_rows, width = down_weight.shape
        fits = 8 * hidden_rows * width <= 2 * 56 * MIB
        whole_tiles = hidden_rows % (16 * BLOCKS) == 0 and width % (128 * CHUNKS) == 0
        small = (tokens.shape[0] << len(masks)) <= 64 and len(masks) == 4
        use = per_device if fits and whole_tiles and small else plain
        return use(count, masks, tokens, gate_weight, up_weight, down_weight, valid_counts)

    return jax.shard_map(
        step,
        mesh=mesh,
        in_specs=(
            P(("groups", "tensor"), None),
            P(None, "tensor"),
            P(None, "tensor"),
            P("tensor", None),
            P(("groups", "tensor")),
        ),
        out_specs=P(("groups", "tensor"), None),
        check_vma=False,
    )
```

time: 72.4 us -> 65.9 us (0.910)
  starting transfers between devices: 19.5 us -> 17.1 us
  Pallas kernels: 44 us -> 41.9 us
  waiting for transfers between devices: 6.93 us -> 5.87 us
  other arithmetic: 0.77 us -> 0 us
    pallas_call x2, Pallas kernels: 6.62 us -> 4.29 us  [down_of(): pl.pallas_call(functools.partial(down_kernel, start), out_shape=(pltpu.VM...]
    ppermute x15 -> x12, starting transfers between devices: 19.5 us -> 17.1 us  [exchange(): return lax.ppermute(array, 'tensor', [(i, i ^ mask) for i in range(count)])]
    ppermute x15 -> x12, waiting for transfers between devices: 6.93 us -> 5.87 us  [exchange(): return lax.ppermute(array, 'tensor', [(i, i ^ mask) for i in range(count)])]
  transfers between devices with their start and end apart: 15 -> 12, of which waited for: 5 -> 6; matrix products, arithmetic and copies ran while one was open for 0% -> 0% of each run, Pallas kernels for 22% -> 22%
where the time goes in v3:
time: 65.9 us; the launch traced here: 65.7 us
  Pallas kernels  41.9 us (64%)
  starting transfers between devices  17.1 us (26%)
  waiting for transfers between devices  5.87 us (9%)
  between operations  0.8 us (1%)
    pallas_call x1, Pallas kernels, hidden_of(): pl.pallas_call(functools.partial(hidden_kernel, rows), out_shape=(pltpu.V...  24.2 us
    ppermute x12, starting transfers between devices, exchange(): return lax.ppermute(array, 'tensor', [(i, i ^ mask) for i in range(count)])  17.1 us
    pallas_call x4, Pallas kernels, load(): pl.pallas_call(functools.partial(load_kernel, start), out_shape=(pltpu.VM...  12.5 us
    ppermute x12, waiting for transfers between devices, exchange(): return lax.ppermute(array, 'tensor', [(i, i ^ mask) for i in range(count)])  5.87 us
    pallas_call x2, Pallas kernels, down_of(): pl.pallas_call(functools.partial(down_kernel, start), out_shape=(pltpu.VM...  4.29 us
  transfers between devices with their start and end apart: 12, of which 6 were waited for; matrix products, arithmetic and copies ran while one was open for 0% of the time, Pallas kernels for 22%

profile of v3, /device:TPU:0, one launch (start us, length us, event | category | flops | bytes accessed | tf_op | source)
XLA Modules:
  0.0 65.7 jit_solution(2244700340947196124)
XLA Ops:
  0.0 4.0 %collective-permute-start = (bf16[2,7424]{1,0:T(2,128)(2,1)}, bf16[2,7424]{1,0:T(2,128)(2,1)S(1)}, u32[]{:S(2)}, u32[]{:S(2)}) collective-permute-start(bf16[2,7424]{1,0:T(2,128)(2,1)} %refs_0_.1), channel_id=1, source_target_pairs={{0,8},{1,9},{2,10},{3,11},{4,12},{5,13},{6,14},{7,15},{8,0},{9,1},... | collective-permute-start | bytes 89096 | tf_op jit(solution)/shard_map/ppermute | solution.py:208
  4.0 3.0 %shard_map.55 = (bf16[464,7424]{1,0:T(8,128)(2,1)S(1)}, f32[8,128]{1,0:T(8,128)S(1)}) custom-call(bf16[1856,7424]{1,0:T(8,128)(2,1)} %bitcast.2), custom_call_target="tpu_custom_call" | custom-call | bytes 6889472 | tf_op jit(solution)/shard_map/pallas_call | solution.py:33
  7.0 0.0 collective-permute-done.refs_1_
  7.1 1.6 %collective-permute-start.1 = (bf16[4,7424]{1,0:T(4,128)(2,1)S(1)}, bf16[4,7424]{1,0:T(4,128)(2,1)S(1)}, u32[]{:S(2)}, u32[]{:S(2)}) collective-permute-start(bf16[4,7424]{1,0:T(4,128)(2,1)S(1)} %shard_map.56.rest_0_.refs_0_), channel_id=1, source_target_pairs={{0,4},{1,5},{2,6},{3,7},{4,0},{5,1},{6,2},{7,3},{8,12},{9,13},{10,... | collective-permute-start | bytes 178184 | tf_op jit(solution)/shard_map/ppermute | solution.py:208
  8.7 3.0 %shard_map.57 = (bf16[464,7424]{1,0:T(8,128)(2,1)S(1)}, f32[8,128]{1,0:T(8,128)S(1)}) custom-call(bf16[1856,7424]{1,0:T(8,128)(2,1)} %bitcast.5, bf16[4,7424]{1,0:T(4,128)(2,1)S(1)} %shard_map.56.rest_0_.refs_0_), custom_call_target="tpu_custom_call" | custom-call | bytes 6889472 | tf_op jit(solution)/shard_map/pallas_call | solution.py:33
  11.7 0.0 collective-permute-done.1.refs_1_
  11.7 1.6 %collective-permute-start.2 = (bf16[8,7424]{1,0:T(8,128)(2,1)S(1)}, bf16[8,7424]{1,0:T(8,128)(2,1)S(1)}, u32[]{:S(2)}, u32[]{:S(2)}) collective-permute-start(bf16[8,7424]{1,0:T(8,128)(2,1)S(1)} %shard_map.58.rest_0_.refs_0_), channel_id=1, source_target_pairs={{0,2},{1,3},{2,0},{3,1},{4,6},{5,7},{6,4},{7,5},{8,10},{9,11},{10,... | collective-permute-start | bytes 356360 | tf_op jit(solution)/shard_map/ppermute | solution.py:208
  13.3 3.0 %shard_map.59 = (bf16[464,7424]{1,0:T(8,128)(2,1)S(1)}, f32[8,128]{1,0:T(8,128)S(1)}) custom-call(bf16[1856,7424]{1,0:T(8,128)(2,1)} %bitcast.3, bf16[8,7424]{1,0:T(8,128)(2,1)S(1)} %shard_map.58.rest_0_.refs_0_), custom_call_target="tpu_custom_call" | custom-call | bytes 6889472 | tf_op jit(solution)/shard_map/pallas_call | solution.py:33
  16.3 0.3 collective-permute-done.2.refs_1_
  16.7 0.1 collective-permute-start.3
  16.7 3.6 %shard_map.61 = (bf16[464,7424]{1,0:T(8,128)(2,1)S(1)}, f32[8,128]{1,0:T(8,128)}) custom-call(bf16[1856,7424]{1,0:T(8,128)(2,1)} %bitcast.6, bf16[16,7424]{1,0:T(8,128)(2,1)S(1)} %shard_map.60.rest_0_.mine), custom_call_target="tpu_custom_call" | custom-call | bytes 6889472 | tf_op jit(solution)/shard_map/pallas_call | solution.py:33
  20.3 0.0 collective-permute-done.3.theirs
  20.3 24.2 %shard_map.62 = (bf16[32,464]{1,0:T(8,128)(2,1)S(1)}, bf16[32,464]{1,0:T(8,128)(2,1)S(1)}, bf16[32,464]{1,0:T(8,128)(2,1)S(1)}, bf16[32,464]{1,0:T(8,128)(2,1)S(...) custom-call(bf16[16,7424]{1,0:T(8,128)(2,1)S(1)} %shard_map.60.rest_, ...), custom_call_target="tpu_custom_call", output_to_operand_aliasing={{4}: (2, {}), {5}: (3, {}), {6}: (4, {}), {7}: (5, {})} | custom-call | flops 1763704832 | bytes 55115776 | tf_op jit(solution)/shard_map/pallas_call | solution.py:126
  44.6 2.1 %shard_map.67 = (f32[16,3712]{1,0:T(8,128)S(1)}, bf16[16,3712]{1,0:T(8,128)(2,1)S(1)}) custom-call(bf16[32,464]{1,0:T(8,128)(2,1)S(1)} %get-tuple-element.43.refs_0_, bf16[32,464]{1,0:T(8,128)(2,1)S(1)} %get-tuple-element.44.refs_1_, bf16[32,464]{1,0:T(8,128)(2,1)S(1)} %get-tuple-element.45.refs_2_, bf16[32,464]{1,0:T(8,128)(2,1)S(1)} %get-tuple-element.46.refs_3_, ...), custom_call_target="tpu_custom_call" | custom-call | flops 440926208 | bytes 13778944 | tf_op jit(solution)/shard_map/pallas_call | solution.py:154
  46.7 0.6 collective-permute-start.8
  47.3 2.1 %shard_map.63 = (f32[16,3712]{1,0:T(8,128)S(1)}, bf16[16,3712]{1,0:T(8,128)(2,1)S(1)}) custom-call(bf16[32,464]{1,0:T(8,128)(2,1)S(1)} %get-tuple-element.43.refs_0_, bf16[32,464]{1,0:T(8,128)(2,1)S(1)} %get-tuple-element.44.refs_1_, bf16[32,464]{1,0:T(8,128)(2,1)S(1)} %get-tuple-element.45.refs_2_, bf16[32,464]{1,0:T(8,128)(2,1)S(1)} %get-tuple-element.46.refs_3_, ...), custom_call_target="tpu_custom_call" | custom-call | flops 440926208 | bytes 13778944 | tf_op jit(solution)/shard_map/pallas_call | solution.py:154
  49.4 0.1 collective-permute-start.4
  49.5 0.0 collective-permute-done.8.came
  49.5 1.6 %collective-permute-start.9 = (bf16[8,3712]{1,0:T(8,128)(2,1)S(1)}, bf16[8,3712]{1,0:T(8,128)(2,1)S(1)}, u32[]{:S(2)}, u32[]{:S(2)}) collective-permute-start(bf16[8,3712]{1,0:T(8,128)(2,1)S(1)} %get-tuple-element.62), channel_id=1, source_target_pairs={{0,2},{1,3},{2,0},{3,1},{4,6},{5,7},{6,4},{7,5},{8,10},{9,11},{10,... | collective-permute-start | bytes 178184 | tf_op jit(solution)/shard_map/ppermute | solution.py:208
  51.1 0.0 collective-permute-done.4.came
  51.2 1.3 %collective-permute-start.5 = (bf16[8,3712]{1,0:T(8,128)(2,1)S(1)}, bf16[8,3712]{1,0:T(8,128)(2,1)S(1)}, u32[]{:S(2)}, u32[]{:S(2)}) collective-permute-start(bf16[8,3712]{1,0:T(8,128)(2,1)S(1)} %get-tuple-element.54), channel_id=1, source_target_pairs={{0,2},{1,3},{2,0},{3,1},{4,6},{5,7},{6,4},{7,5},{8,10},{9,11},{10,... | collective-permute-start | bytes 178184 | tf_op jit(solution)/shard_map/ppermute | solution.py:208
  52.4 1.5 %collective-permute-done.9.came = bf16[8,3712]{1,0:T(8,128)(2,1)S(1)} collective-permute-done((bf16[8,3712]{1,0:T(8,128)(2,1)S(1)}, bf16[8,3712]{1,0:T(8,128)(2,1)S(1)}, u32[]{:S(2)}, u32[]{:S(2)}) %collective-permute-start.9) | collective-permute-done | bytes 59424 | tf_op jit(solution)/shard_map/ppermute | solution.py:208
  54.0 1.3 %collective-permute-start.10 = (bf16[4,3712]{1,0:T(4,128)(2,1)S(1)}, bf16[4,3712]{1,0:T(4,128)(2,1)S(1)}, u32[]{:S(2)}, u32[]{:S(2)}) collective-permute-start(bf16[4,3712]{1,0:T(4,128)(2,1)S(1)} %get-tuple-element.64), channel_id=1, source_target_pairs={{0,4},{1,5},{2,6},{3,7},{4,0},{5,1},{6,2},{7,3},{8,12},{9,13},{10,... | collective-permute-start | bytes 89096 | tf_op jit(solution)/shard_map/ppermute | solution.py:208
  55.3 0.2 collective-permute-done.5.came
  55.5 1.3 %collective-permute-start.6 = (bf16[4,3712]{1,0:T(4,128)(2,1)S(1)}, bf16[4,3712]{1,0:T(4,128)(2,1)S(1)}, u32[]{:S(2)}, u32[]{:S(2)}) collective-permute-start(bf16[4,3712]{1,0:T(4,128)(2,1)S(1)} %get-tuple-element.56), channel_id=1, source_target_pairs={{0,4},{1,5},{2,6},{3,7},{4,0},{5,1},{6,2},{7,3},{8,12},{9,13},{10,... | collective-permute-start | bytes 89096 | tf_op jit(solution)/shard_map/ppermute | solution.py:208
  56.7 1.3 %collective-permute-done.10.came = bf16[4,3712]{1,0:T(4,128)(2,1)S(1)} collective-permute-done((bf16[4,3712]{1,0:T(4,128)(2,1)S(1)}, bf16[4,3712]{1,0:T(4,128)(2,1)S(1)}, u32[]{:S(2)}, u32[]{:S(2)}) %collective-permute-start.10) | collective-permute-done | bytes 29728 | tf_op jit(solution)/shard_map/ppermute | solution.py:208
  58.1 2.3 %collective-permute-start.11 = (bf16[2,3712]{1,0:T(2,128)(2,1)S(1)}, bf16[2,3712]{1,0:T(2,128)(2,1)S(1)}, u32[]{:S(2)}, u32[]{:S(2)}) collective-permute-start(bf16[2,3712]{1,0:T(2,128)(2,1)S(1)} %get-tuple-element.66), channel_id=1, source_target_pairs={{0,8},{1,9},{2,10},{3,11},{4,12},{5,13},{6,14},{7,15},{8,0},{9,1},... | collective-permute-start | bytes 44552 | tf_op jit(solution)/shard_map/ppermute | solution.py:208
  60.3 0.0 collective-permute-done.6.came
  60.3 1.5 %collective-permute-start.7 = (bf16[2,3712]{1,0:T(2,128)(2,1)S(1)}, bf16[2,3712]{1,0:T(2,128)(2,1)S(1)}, u32[]{:S(2)}, u32[]{:S(2)}) collective-permute-start(bf16[2,3712]{1,0:T(2,128)(2,1)S(1)} %get-tuple-element.58), channel_id=1, source_target_pairs={{0,8},{1,9},{2,10},{3,11},{4,12},{5,13},{6,14},{7,15},{8,0},{9,1},... | collective-permute-start | bytes 44552 | tf_op jit(solution)/shard_map/ppermute | solution.py:208
  62.5 0.2 collective-permute-done.11.refs_3_
  62.7 2.3 %collective-permute-done.7.refs_1_ = bf16[2,3712]{1,0:T(2,128)(2,1)S(1)} collective-permute-done((bf16[2,3712]{1,0:T(2,128)(2,1)S(1)}, bf16[2,3712]{1,0:T(2,128)(2,1)S(1)}, u32[]{:S(2)}, u32[]{:S(2)}) %collective-permute-start.7) | collective-permute-done | bytes 14880 | tf_op jit(solution)/shard_map/ppermute | solution.py:208
  65.0 0.7 shard_map.71
  (11 shorter events, 0.2 us)
Async XLA Ops:
  0.0 7.0 %collective-permute-start = (bf16[2,7424]{1,0:T(2,128)(2,1)}, bf16[2,7424]{1,0:T(2,128)(2,1)S(1)}, u32[]{:S(2)}, u32[]{:S(2)}) collective-permute-start(bf16[2,7424]{1,0:T(2,128)(2,1)} %refs_0_.1), channel_id=1, source_target_pairs={{0,8},{1,9},{2,10},{3,11},{4,12},{5,13},{6,14},{7,15},{8,0},{9,1},... | collective-permute-start | bytes 89096 | tf_op jit(solution)/shard_map/ppermute | solution.py:208
  4.0 3.0 %copy-start = (bf16[2,7424]{1,0:T(2,128)(2,1)S(1)}, bf16[2,7424]{1,0:T(2,128)(2,1)}, u32[]{:S(2)}) copy-start(bf16[2,7424]{1,0:T(2,128)(2,1)} %refs_0_.1) | copy-start | bytes 89092
  7.1 4.6 %collective-permute-start.1 = (bf16[4,7424]{1,0:T(4,128)(2,1)S(1)}, bf16[4,7424]{1,0:T(4,128)(2,1)S(1)}, u32[]{:S(2)}, u32[]{:S(2)}) collective-permute-start(bf16[4,7424]{1,0:T(4,128)(2,1)S(1)} %shard_map.56.rest_0_.refs_0_), channel_id=1, source_target_pairs={{0,4},{1,5},{2,6},{3,7},{4,0},{5,1},{6,2},{7,3},{8,12},{9,13},{10,... | collective-permute-start | bytes 178184 | tf_op jit(solution)/shard_map/ppermute | solution.py:208
  11.7 4.9 %collective-permute-start.2 = (bf16[8,7424]{1,0:T(8,128)(2,1)S(1)}, bf16[8,7424]{1,0:T(8,128)(2,1)S(1)}, u32[]{:S(2)}, u32[]{:S(2)}) collective-permute-start(bf16[8,7424]{1,0:T(8,128)(2,1)S(1)} %shard_map.58.rest_0_.refs_0_), channel_id=1, source_target_pairs={{0,2},{1,3},{2,0},{3,1},{4,6},{5,7},{6,4},{7,5},{8,10},{9,11},{10,... | collective-permute-start | bytes 356360 | tf_op jit(solution)/shard_map/ppermute | solution.py:208
  16.7 3.6 %collective-permute-start.3 = (bf16[16,7424]{1,0:T(8,128)(2,1)S(1)}, bf16[16,7424]{1,0:T(8,128)(2,1)S(1)}, u32[]{:S(2)}, u32[]{:S(2)}) collective-permute-start(bf16[16,7424]{1,0:T(8,128)(2,1)S(1)} %shard_map.60.rest_0_.mine), channel_id=1, source_target_pairs={{0,1},{1,0},{2,3},{3,2},{4,5},{5,4},{6,7},{7,6},{8,9},{9,8},{10,11... | collective-permute-start | bytes 712712 | tf_op jit(solution)/shard_map/ppermute | solution.py:208
  46.7 2.8 %collective-permute-start.8 = (bf16[16,3712]{1,0:T(8,128)(2,1)S(1)}, bf16[16,3712]{1,0:T(8,128)(2,1)S(1)}, u32[]{:S(2)}, u32[]{:S(2)}) collective-permute-start(bf16[16,3712]{1,0:T(8,128)(2,1)S(1)} %get-tuple-element.60), channel_id=1, source_target_pairs={{0,1},{1,0},{2,3},{3,2},{4,5},{5,4},{6,7},{7,6},{8,9},{9,8},{10,11... | collective-permute-start | bytes 356360 | tf_op jit(solution)/shard_map/ppermute | solution.py:208
  49.4 1.7 %collective-permute-start.4 = (bf16[16,3712]{1,0:T(8,128)(2,1)S(1)}, bf16[16,3712]{1,0:T(8,128)(2,1)S(1)}, u32[]{:S(2)}, u32[]{:S(2)}) collective-permute-start(bf16[16,3712]{1,0:T(8,128)(2,1)S(1)} %get-tuple-element.52), channel_id=1, source_target_pairs={{0,1},{1,0},{2,3},{3,2},{4,5},{5,4},{6,7},{7,6},{8,9},{9,8},{10,11... | collective-permute-start | bytes 356360 | tf_op jit(solution)/shard_map/ppermute | solution.py:208
  49.5 4.4 %collective-permute-start.9 = (bf16[8,3712]{1,0:T(8,128)(2,1)S(1)}, bf16[8,3712]{1,0:T(8,128)(2,1)S(1)}, u32[]{:S(2)}, u32[]{:S(2)}) collective-permute-start(bf16[8,3712]{1,0:T(8,128)(2,1)S(1)} %get-tuple-element.62), channel_id=1, source_target_pairs={{0,2},{1,3},{2,0},{3,1},{4,6},{5,7},{6,4},{7,5},{8,10},{9,11},{10,... | collective-permute-start | bytes 178184 | tf_op jit(solution)/shard_map/ppermute | solution.py:208
  51.2 4.3 %collective-permute-start.5 = (bf16[8,3712]{1,0:T(8,128)(2,1)S(1)}, bf16[8,3712]{1,0:T(8,128)(2,1)S(1)}, u32[]{:S(2)}, u32[]{:S(2)}) collective-permute-start(bf16[8,3712]{1,0:T(8,128)(2,1)S(1)} %get-tuple-element.54), channel_id=1, source_target_pairs={{0,2},{1,3},{2,0},{3,1},{4,6},{5,7},{6,4},{7,5},{8,10},{9,11},{10,... | collective-permute-start | bytes 178184 | tf_op jit(solution)/shard_map/ppermute | solution.py:208
  54.0 4.0 %collective-permute-start.10 = (bf16[4,3712]{1,0:T(4,128)(2,1)S(1)}, bf16[4,3712]{1,0:T(4,128)(2,1)S(1)}, u32[]{:S(2)}, u32[]{:S(2)}) collective-permute-start(bf16[4,3712]{1,0:T(4,128)(2,1)S(1)} %get-tuple-element.64), channel_id=1, source_target_pairs={{0,4},{1,5},{2,6},{3,7},{4,0},{5,1},{6,2},{7,3},{8,12},{9,13},{10,... | collective-permute-start | bytes 89096 | tf_op jit(solution)/shard_map/ppermute | solution.py:208
  55.5 4.9 %collective-permute-start.6 = (bf16[4,3712]{1,0:T(4,128)(2,1)S(1)}, bf16[4,3712]{1,0:T(4,128)(2,1)S(1)}, u32[]{:S(2)}, u32[]{:S(2)}) collective-permute-start(bf16[4,3712]{1,0:T(4,128)(2,1)S(1)} %get-tuple-element.56), channel_id=1, source_target_pairs={{0,4},{1,5},{2,6},{3,7},{4,0},{5,1},{6,2},{7,3},{8,12},{9,13},{10,... | collective-permute-start | bytes 89096 | tf_op jit(solution)/shard_map/ppermute | solution.py:208
  58.1 4.7 %collective-permute-start.11 = (bf16[2,3712]{1,0:T(2,128)(2,1)S(1)}, bf16[2,3712]{1,0:T(2,128)(2,1)S(1)}, u32[]{:S(2)}, u32[]{:S(2)}) collective-permute-start(bf16[2,3712]{1,0:T(2,128)(2,1)S(1)} %get-tuple-element.66), channel_id=1, source_target_pairs={{0,8},{1,9},{2,10},{3,11},{4,12},{5,13},{6,14},{7,15},{8,0},{9,1},... | collective-permute-start | bytes 44552 | tf_op jit(solution)/shard_map/ppermute | solution.py:208
  60.3 4.7 %collective-permute-start.7 = (bf16[2,3712]{1,0:T(2,128)(2,1)S(1)}, bf16[2,3712]{1,0:T(2,128)(2,1)S(1)}, u32[]{:S(2)}, u32[]{:S(2)}) collective-permute-start(bf16[2,3712]{1,0:T(2,128)(2,1)S(1)} %get-tuple-element.58), channel_id=1, source_target_pairs={{0,8},{1,9},{2,10},{3,11},{4,12},{5,13},{6,14},{7,15},{8,0},{9,1},... | collective-permute-start | bytes 44552 | tf_op jit(solution)/shard_map/ppermute | solution.py:208

commit v4 on v3

--- a/solution.py
+++ b/solution.py
@@ -11,27 +11,27 @@
 VMEM = pl.BlockSpec(memory_space=pltpu.VMEM)
 HBM = pl.BlockSpec(memory_space=pltpu.HBM)
 ANY = pl.BlockSpec(memory_space=pl.ANY)
-BLOCKS = 4
+BLOCKS = 2
 CHUNKS = 2
-DEPTH = 2048
 
 
 def cost(flops, moved):
     return pl.CostEstimate(flops=flops, bytes_accessed=moved, transcendentals=0)
 
 
-def load_kernel(start, source, *rest):
+def load_kernel(start, share, source, *rest):
     piece, token, sem = rest[-3:]
-    copy = pltpu.make_async_copy(source.at[pl.ds(start, piece.shape[0])], piece, sem)
+    at = pl.multiple_of(lax.axis_index("groups") * share + start, 16)
+    copy = pltpu.make_async_copy(source.at[pl.ds(at, piece.shape[0])], piece, sem)
     copy.start()
     token[...] = jnp.zeros_like(token)
     copy.wait()
 
 
-def load(source, after, start, rows):
+def load(source, after, start, rows, share):
     shape = (rows, source.shape[1])
     return pl.pallas_call(
-        functools.partial(load_kernel, start),
+        functools.partial(load_kernel, start, share),
         out_shape=(pltpu.VMEM(shape, source.dtype), pltpu.VMEM((8, 128), jnp.float32)),
         in_specs=[HBM] + [ANY] * len(after),
         out_specs=(VMEM, VMEM),
@@ -61,84 +61,38 @@
     )(*parts, *tokens)
 
 
-def hidden_kernel(rows, mine, theirs, g0, u0, g1, u1, gate, up, down, h0, h1, h2, h3, d0, d1, d2, d3, tokens, g2, u2, g3, u3, sems):
-    order = [
-        (gate, 2, g2),
-        (up, 2, u2),
-        (gate, 3, g3),
-        (up, 3, u3),
-        (down, 0, d0),
-        (down, 1, d1),
-        (down, 2, d2),
-        (down, 3, d3),
-    ]
-    copies = [
-        pltpu.make_async_copy(source.at[pl.ds(block * rows, rows)], into, sems.at[at])
-        for at, (source, block, into) in enumerate(order)
-    ]
-    copies[0].start()
-    copies[1].start()
-    half, width = mine.shape
+def hidden_kernel(mine, theirs, *refs):
+    pieces, hidden, tokens = refs[: 2 * BLOCKS], refs[2 * BLOCKS : -1], refs[-1]
+    half = mine.shape[0]
     tokens[:half, :] = mine[...]
     tokens[half:, :] = theirs[...]
-
-    def product(weight):
-        total = None
-        for at in range(0, width, DEPTH):
-            value = lax.dot_general(
-                tokens[:, at : min(at + DEPTH, width)],
-                weight[:, at : min(at + DEPTH, width)],
-                (((1,), (1,)), ((), ())),
-                preferred_element_type=jnp.float32,
+    for gate, up, out in zip(pieces[::2], pieces[1::2], hidden):
+        gate_value, up_value = (
+            lax.dot_general(
+                tokens[...], weight[...], (((1,), (1,)), ((), ())), preferred_element_type=jnp.float32
             )
-            total = value if total is None else total + value
-        return total
-
-    def finish(hidden, gate_value, up_value):
+            for weight in (gate, up)
+        )
         value = gate_value / (1.0 + jnp.exp(-gate_value)) * up_value
-        hidden[...] = value.astype(hidden.dtype)
-
-    gate_value = product(g0)
-    copies[2].start()
-    finish(h0, gate_value, product(u0))
-    copies[3].start()
-    copies[4].start()
-    gate_value = product(g1)
-    copies[5].start()
-    finish(h1, gate_value, product(u1))
-    copies[6].start()
-    copies[0].wait()
-    gate_value = product(g2)
-    copies[7].start()
-    copies[1].wait()
-    finish(h2, gate_value, product(u2))
-    copies[2].wait()
-    gate_value = product(g3)
-    copies[3].wait()
-    finish(h3, gate_value, product(u3))
-    for copy in copies[4:]:
-        copy.wait()
-
-
-def hidden_of(mine, theirs, pieces, gate, up, down):
+        out[...] = value.astype(out.dtype)
+
+
+def hidden_of(mine, theirs, pieces):
     rows, width = pieces[0].shape
     count = mine.shape[0] + theirs.shape[0]
     return pl.pallas_call(
-        functools.partial(hidden_kernel, rows),
-        out_shape=(pltpu.VMEM((count, rows), gate.dtype),) * 4 + (pltpu.VMEM((rows, width), gate.dtype),) * 4,
-        in_specs=[VMEM] * 6 + [HBM] * 3,
-        out_specs=(VMEM,) * 8,
-        input_output_aliases={2: 4, 3: 5, 4: 6, 5: 7},
-        scratch_shapes=[pltpu.VMEM((count, width), mine.dtype)]
-        + [pltpu.VMEM((rows, width), gate.dtype)] * 4
-        + [pltpu.SemaphoreType.DMA((8,))],
-        compiler_params=pltpu.CompilerParams(vmem_limit_bytes=8 * rows * width + 4 * MIB),
-        cost_estimate=cost(4 * count * gate.size, 4 * gate.size),
-    )(*(pltpu.with_memory_space_constraint(one, pltpu.VMEM) for one in (mine, theirs, *pieces)), gate, up, down)
+        hidden_kernel,
+        out_shape=(pltpu.VMEM((count, rows), mine.dtype),) * BLOCKS,
+        in_specs=[VMEM] * (2 + 2 * BLOCKS),
+        out_specs=(VMEM,) * BLOCKS,
+        scratch_shapes=[pltpu.VMEM((count, width), mine.dtype)],
+        compiler_params=pltpu.CompilerParams(vmem_limit_bytes=12 * MIB),
+        cost_estimate=cost(4 * BLOCKS * count * rows * width, 4 * BLOCKS * rows * width),
+    )(*(pltpu.with_memory_space_constraint(one, pltpu.VMEM) for one in (mine, theirs, *pieces)))
 
 
 def down_kernel(start, *refs):
-    hidden, pieces, (keep, send) = refs[:4], refs[4:8], refs[8:]
+    hidden, pieces, (keep, send) = refs[:BLOCKS], refs[BLOCKS:-2], refs[-2:]
     half, columns = keep.shape
     total = None
     for part, piece in zip(hidden, pieces):
@@ -154,10 +108,10 @@
     return pl.pallas_call(
         functools.partial(down_kernel, start),
         out_shape=(pltpu.VMEM((half, columns), jnp.float32), pltpu.VMEM((half, columns), jnp.bfloat16)),
-        in_specs=[VMEM] * 8,
+        in_specs=[VMEM] * (2 * BLOCKS),
         out_specs=(VMEM, VMEM),
         compiler_params=pltpu.CompilerParams(vmem_limit_bytes=4 * MIB),
-        cost_estimate=cost(16 * half * rows * columns, 8 * rows * columns),
+        cost_estimate=cost(4 * BLOCKS * half * rows * columns, 2 * BLOCKS * rows * columns),
     )(*(pltpu.with_memory_space_constraint(one, pltpu.VMEM) for one in (*hidden, *pieces)))
 
 
@@ -205,6 +159,8 @@
 
 
 def exchange(array, mask, count):
+    if mask == 0:
+        return lax.ppermute(array, "groups", [(0, 1), (1, 0)])
     return lax.ppermute(array, "tensor", [(i, i ^ mask) for i in range(count)])
 
 
@@ -241,21 +197,26 @@
     gate, up, down = (
         pltpu.with_memory_space_constraint(one, pltpu.HBM) for one in (gate_weight.T, up_weight.T, down_weight)
     )
-    rows = gate.shape[0] // BLOCKS
-    wanted = [(gate, 0), (up, 0), (gate, rows), (up, rows)]
+    share = gate.shape[0] // 2
+    rows = share // BLOCKS
+    wanted = [[(gate, 0)], [(up, 0)], [(gate, rows)], [(up, rows), (down, 0)], [(down, rows)]]
+    masks = [*masks, 0]
     mine, after, pieces = tokens, (), []
-    for mask, (source, start) in zip(reversed(masks), wanted):
+    for step, (mask, sources) in enumerate(zip(reversed(masks), wanted)):
         theirs = exchange(mine, mask, count)
-        piece, token = load(source, after, start, rows)
-        pieces.append(piece)
-        if len(pieces) < len(masks):
-            mine = join([mine, theirs], [token])
+        tokens_of = []
+        for source, start in sources:
+            piece, token = load(source, after, start, rows, share)
+            pieces.append(piece)
+            tokens_of.append(token)
+        if step + 1 < len(masks):
+            mine = join([mine, theirs], tokens_of)
             after = (mine,)
-    down_inputs = hidden_of(mine, theirs, pieces, gate, up, down)
+    hidden = hidden_of(mine, theirs, pieces[: 2 * BLOCKS])
     columns = width // CHUNKS
     parts = []
     for chunk in range(CHUNKS):
-        keep, send = down_of(down_inputs[:4], down_inputs[4:], chunk * columns, columns)
+        keep, send = down_of(hidden, pieces[2 * BLOCKS :], chunk * columns, columns)
         for mask in masks[:-1]:
             keep, send = fold(keep, exchange(send, mask, count))
         parts.append((keep, exchange(send, masks[-1], count)))
@@ -268,9 +229,9 @@
 
     def step(tokens, gate_weight, up_weight, down_weight, valid_counts):
         hidden_rows, width = down_weight.shape
-        fits = 8 * hidden_rows * width <= 2 * 56 * MIB
-        whole_tiles = hidden_rows % (16 * BLOCKS) == 0 and width % (128 * CHUNKS) == 0
-        small = (tokens.shape[0] << len(masks)) <= 64 and len(masks) == 4
+        fits = 3 * hidden_rows * width <= 44 * MIB
+        whole_tiles = hidden_rows % (2 * 16 * BLOCKS) == 0 and width % (128 * CHUNKS) == 0
+        small = (tokens.shape[0] << len(masks)) <= 64 and len(masks) == 4 and mesh.shape["groups"] == 2
         use = per_device if fits and whole_tiles and small else plain
         return use(count, masks, tokens, gate_weight, up_weight, down_weight, valid_counts)
 

time: 65.9 us -> 61.3 us (0.930)
  Pallas kernels: 41.9 us -> 29.7 us
  starting transfers between devices: 17.1 us -> 21 us
  waiting for transfers between devices: 5.87 us -> 9.5 us
    pallas_call x5 -> x7, Pallas kernels: 36.7 us -> 26.3 us  [the longest x6 18.4 us: load(): pl.pallas_call(functools.partial(load_kernel, start, share), out_shape=(p...]
    ppermute x0 -> x3, starting transfers between devices: none -> 5.26 us  [exchange(): return lax.ppermute(array, 'groups', [(0, 1), (1, 0)])]
    ppermute x0 -> x3, waiting for transfers between devices: none -> 1.97 us  [exchange(): return lax.ppermute(array, 'groups', [(0, 1), (1, 0)])]
    pallas_call x2, Pallas kernels: 4.29 us -> 2.41 us  [down_of(): pl.pallas_call(functools.partial(down_kernel, start), out_shape=(pltpu.VM...]
    ppermute x12, waiting for transfers between devices: 5.87 us -> 7.53 us  [exchange(): return lax.ppermute(array, 'tensor', [(i, i ^ mask) for i in range(count)])]
    ppermute x12, starting transfers between devices: 17.1 us -> 15.7 us  [exchange(): return lax.ppermute(array, 'tensor', [(i, i ^ mask) for i in range(count)])]
  transfers between devices with their start and end apart: 12 -> 15, of which waited for: 6 -> 8; matrix products, arithmetic and copies ran while one was open for 0% -> 0% of each run, Pallas kernels for 22% -> 33%
where the time goes in v4:
time: 61.3 us; the launch traced here: 61 us
  Pallas kernels  29.7 us (48%)
  starting transfers between devices  21 us (34%)
  waiting for transfers between devices  9.5 us (15%)
  between operations  0.83 us (1%)
    pallas_call x6, Pallas kernels, load(): pl.pallas_call(functools.partial(load_kernel, start, share), out_shape=(p...  18.4 us
    ppermute x12, starting transfers between devices, exchange(): return lax.ppermute(array, 'tensor', [(i, i ^ mask) for i in range(count)])  15.7 us
    pallas_call x1, Pallas kernels, hidden_of(): pl.pallas_call(hidden_kernel, out_shape=(pltpu.VMEM((count, rows), mine.d...  7.88 us
    ppermute x12, waiting for transfers between devices, exchange(): return lax.ppermute(array, 'tensor', [(i, i ^ mask) for i in range(count)])  7.53 us
    ppermute x3, starting transfers between devices, exchange(): return lax.ppermute(array, 'groups', [(0, 1), (1, 0)])  5.26 us
    pallas_call x2, Pallas kernels, down_of(): pl.pallas_call(functools.partial(down_kernel, start), out_shape=(pltpu.VM...  2.41 us
    ppermute x3, waiting for transfers between devices, exchange(): return lax.ppermute(array, 'groups', [(0, 1), (1, 0)])  1.97 us
  transfers between devices with their start and end apart: 15, of which 8 were waited for; matrix products, arithmetic and copies ran while one was open for 0% of the time, Pallas kernels for 33%

profile of v4, /device:TPU:0, one launch (start us, length us, event | category | flops | bytes accessed | tf_op | source)
XLA Modules:
  0.0 61.0 jit_solution(10097981514746219244)
XLA Ops:
  0.0 2.9 %collective-permute-start = (bf16[2,7424]{1,0:T(2,128)(2,1)}, bf16[2,7424]{1,0:T(2,128)(2,1)S(1)}, u32[]{:S(2)}, u32[]{:S(2)}) collective-permute-start(bf16[2,7424]{1,0:T(2,128)(2,1)} %refs_0_.1), channel_id=1, source_target_pairs={{0,16},{16,0},{1,17},{17,1},{2,18},{18,2},{3,19},{19,3},{4,20},{20... | collective-permute-start | bytes 89096 | tf_op jit(solution)/shard_map/ppermute | solution.py:163
  2.9 3.0 %shard_map.55 = (bf16[464,7424]{1,0:T(8,128)(2,1)S(1)}, f32[8,128]{1,0:T(8,128)S(1)}) custom-call(bf16[1856,7424]{1,0:T(8,128)(2,1)} %bitcast.2), custom_call_target="tpu_custom_call" | custom-call | bytes 6889472 | tf_op jit(solution)/shard_map/pallas_call | solution.py:33
  6.0 2.7 %collective-permute-start.1 = (bf16[4,7424]{1,0:T(4,128)(2,1)S(1)}, bf16[4,7424]{1,0:T(4,128)(2,1)S(1)}, u32[]{:S(2)}, u32[]{:S(2)}) collective-permute-start(bf16[4,7424]{1,0:T(4,128)(2,1)S(1)} %shard_map.56.rest_0_.refs_0_), channel_id=1, source_target_pairs={{0,8},{1,9},{2,10},{3,11},{4,12},{5,13},{6,14},{7,15},{8,0},{9,1},... | collective-permute-start | bytes 178184 | tf_op jit(solution)/shard_map/ppermute | solution.py:164
  8.6 3.0 %shard_map.57 = (bf16[464,7424]{1,0:T(8,128)(2,1)S(1)}, f32[8,128]{1,0:T(8,128)S(1)}) custom-call(bf16[1856,7424]{1,0:T(8,128)(2,1)} %bitcast.4, bf16[4,7424]{1,0:T(4,128)(2,1)S(1)} %shard_map.56.rest_0_.refs_0_), custom_call_target="tpu_custom_call" | custom-call | bytes 6889472 | tf_op jit(solution)/shard_map/pallas_call | solution.py:33
  11.6 1.6 %collective-permute-start.2 = (bf16[8,7424]{1,0:T(8,128)(2,1)S(1)}, bf16[8,7424]{1,0:T(8,128)(2,1)S(1)}, u32[]{:S(2)}, u32[]{:S(2)}) collective-permute-start(bf16[8,7424]{1,0:T(8,128)(2,1)S(1)} %shard_map.58.rest_0_.refs_0_), channel_id=1, source_target_pairs={{0,4},{1,5},{2,6},{3,7},{4,0},{5,1},{6,2},{7,3},{8,12},{9,13},{10,... | collective-permute-start | bytes 356360 | tf_op jit(solution)/shard_map/ppermute | solution.py:164
  13.3 3.0 %shard_map.59 = (bf16[464,7424]{1,0:T(8,128)(2,1)S(1)}, f32[8,128]{1,0:T(8,128)S(1)}) custom-call(bf16[1856,7424]{1,0:T(8,128)(2,1)} %bitcast.3, bf16[8,7424]{1,0:T(8,128)(2,1)S(1)} %shard_map.58.rest_0_.refs_0_), custom_call_target="tpu_custom_call" | custom-call | bytes 6889472 | tf_op jit(solution)/shard_map/pallas_call | solution.py:33
  16.3 0.3 collective-permute-done.2.refs_1_
  16.6 1.6 %collective-permute-start.3 = (bf16[16,7424]{1,0:T(8,128)(2,1)S(1)}, bf16[16,7424]{1,0:T(8,128)(2,1)S(1)}, u32[]{:S(2)}, u32[]{:S(2)}) collective-permute-start(bf16[16,7424]{1,0:T(8,128)(2,1)S(1)} %shard_map.60.rest_0_.refs_0_), channel_id=1, source_target_pairs={{0,2},{1,3},{2,0},{3,1},{4,6},{5,7},{6,4},{7,5},{8,10},{9,11},{10,... | collective-permute-start | bytes 712712 | tf_op jit(solution)/shard_map/ppermute | solution.py:164
  18.2 3.0 %shard_map.61 = (bf16[464,7424]{1,0:T(8,128)(2,1)S(1)}, f32[8,128]{1,0:T(8,128)S(1)}) custom-call(bf16[1856,7424]{1,0:T(8,128)(2,1)} %bitcast.5, bf16[16,7424]{1,0:T(8,128)(2,1)S(1)} %shard_map.60.rest_0_.refs_0_), custom_call_target="tpu_custom_call" | custom-call | bytes 6889472 | tf_op jit(solution)/shard_map/pallas_call | solution.py:33
  21.1 3.0 %shard_map.62 = (bf16[464,7424]{1,0:T(8,128)(2,1)S(1)}, f32[8,128]{1,0:T(8,128)S(1)}) custom-call(bf16[1856,7424]{1,0:T(8,128)(2,1)} %source.3, bf16[16,7424]{1,0:T(8,128)(2,1)S(1)} %shard_map.60.rest_0_.refs_0_), custom_call_target="tpu_custom_call" | custom-call | bytes 6889472 | tf_op jit(solution)/shard_map/pallas_call | solution.py:33
  24.2 3.6 %shard_map.65 = (bf16[464,7424]{1,0:T(8,128)(2,1)S(1)}, f32[8,128]{1,0:T(8,128)}) custom-call(bf16[1856,7424]{1,0:T(8,128)(2,1)} %source.3, bf16[32,7424]{1,0:T(8,128)(2,1)S(1)} %shard_map.63.mine.rest_0_), custom_call_target="tpu_custom_call" | custom-call | bytes 6889472 | tf_op jit(solution)/shard_map/pallas_call | solution.py:33
  27.8 7.9 %shard_map.64 = (bf16[64,464]{1,0:T(8,128)(2,1)S(1)}, bf16[64,464]{1,0:T(8,128)(2,1)S(1)}) custom-call(bf16[32,7424]{1,0:T(8,128)(2,1)S(1)} %shard_map.63.mine.rest_0_, bf16[32,7424]{1,0:T(8,128)(2,1)S(1)} %collective-permute-done.4.theirs, bf16[464,7424]{1,0:T(8,128)(2,1)S(1)} %get-tuple-element.43.refs_0_, ...), custom_call_target="tpu_custom_call" | custom-call | flops 1763704832 | bytes 27557888 | tf_op jit(solution)/shard_map/pallas_call | solution.py:83
  35.7 1.2 %shard_map.71 = (f32[32,3712]{1,0:T(8,128)S(1)}, bf16[32,3712]{1,0:T(8,128)(2,1)S(1)}) custom-call(bf16[64,464]{1,0:T(8,128)(2,1)S(1)} %get-tuple-element.47.refs_0_, bf16[64,464]{1,0:T(8,128)(2,1)S(1)} %get-tuple-element.48.refs_1_, bf16[464,7424]{1,0:T(8,128)(2,1)S(1)} %get-tuple-element.49.refs_2_, bf16[464,7424]{1,0:T(8,128)(2,1)S(1)} %get-tuple-element.50.refs_3_), custom_call_target="tpu_custom_call" | custom-call | flops 440926208 | bytes 6889472 | tf_op jit(solution)/shard_map/pallas_call | solution.py:108
  36.9 0.6 collective-permute-start.10
  37.5 1.2 %shard_map.66 = (f32[32,3712]{1,0:T(8,128)S(1)}, bf16[32,3712]{1,0:T(8,128)(2,1)S(1)}) custom-call(bf16[64,464]{1,0:T(8,128)(2,1)S(1)} %get-tuple-element.47.refs_0_, bf16[64,464]{1,0:T(8,128)(2,1)S(1)} %get-tuple-element.48.refs_1_, bf16[464,7424]{1,0:T(8,128)(2,1)S(1)} %get-tuple-element.49.refs_2_, bf16[464,7424]{1,0:T(8,128)(2,1)S(1)} %get-tuple-element.50.refs_3_), custom_call_target="tpu_custom_call" | custom-call | flops 440926208 | bytes 6889472 | tf_op jit(solution)/shard_map/pallas_call | solution.py:108
  38.7 0.1 collective-permute-start.5
  38.8 0.6 collective-permute-start.11
  39.4 0.9 %collective-permute-done.5.came = bf16[32,3712]{1,0:T(8,128)(2,1)S(1)} collective-permute-done((bf16[32,3712]{1,0:T(8,128)(2,1)S(1)}, bf16[32,3712]{1,0:T(8,128)(2,1)S(1)}, u32[]{:S(2)}, u32[]{:S(2)}) %collective-permute-start.5) | collective-permute-done | bytes 237600 | tf_op jit(solution)/shard_map/ppermute | solution.py:164
  40.3 0.7 %collective-permute-start.6 = (bf16[16,3712]{1,0:T(8,128)(2,1)S(1)}, bf16[16,3712]{1,0:T(8,128)(2,1)S(1)}, u32[]{:S(2)}, u32[]{:S(2)}) collective-permute-start(bf16[16,3712]{1,0:T(8,128)(2,1)S(1)} %get-tuple-element.54), channel_id=1, source_target_pairs={{0,2},{1,3},{2,0},{3,1},{4,6},{5,7},{6,4},{7,5},{8,10},{9,11},{10,... | collective-permute-start | bytes 356360 | tf_op jit(solution)/shard_map/ppermute | solution.py:164
  41.0 3.9 %collective-permute-done.11.came = bf16[16,3712]{1,0:T(8,128)(2,1)S(1)} collective-permute-done((bf16[16,3712]{1,0:T(8,128)(2,1)S(1)}, bf16[16,3712]{1,0:T(8,128)(2,1)S(1)}, u32[]{:S(2)}, u32[]{:S(2)}) %collective-permute-start.11) | collective-permute-done | bytes 118816 | tf_op jit(solution)/shard_map/ppermute | solution.py:164
  44.9 1.6 %collective-permute-start.12 = (bf16[8,3712]{1,0:T(8,128)(2,1)S(1)}, bf16[8,3712]{1,0:T(8,128)(2,1)S(1)}, u32[]{:S(2)}, u32[]{:S(2)}) collective-permute-start(bf16[8,3712]{1,0:T(8,128)(2,1)S(1)} %get-tuple-element.66), channel_id=1, source_target_pairs={{0,4},{1,5},{2,6},{3,7},{4,0},{5,1},{6,2},{7,3},{8,12},{9,13},{10,... | collective-permute-start | bytes 178184 | tf_op jit(solution)/shard_map/ppermute | solution.py:164
  46.6 0.5 collective-permute-done.6.came
  47.1 1.6 %collective-permute-start.7 = (bf16[8,3712]{1,0:T(8,128)(2,1)S(1)}, bf16[8,3712]{1,0:T(8,128)(2,1)S(1)}, u32[]{:S(2)}, u32[]{:S(2)}) collective-permute-start(bf16[8,3712]{1,0:T(8,128)(2,1)S(1)} %get-tuple-element.56), channel_id=1, source_target_pairs={{0,4},{1,5},{2,6},{3,7},{4,0},{5,1},{6,2},{7,3},{8,12},{9,13},{10,... | collective-permute-start | bytes 178184 | tf_op jit(solution)/shard_map/ppermute | solution.py:164
  48.7 0.5 collective-permute-done.12.came
  49.2 2.4 %collective-permute-start.13 = (bf16[4,3712]{1,0:T(4,128)(2,1)S(1)}, bf16[4,3712]{1,0:T(4,128)(2,1)S(1)}, u32[]{:S(2)}, u32[]{:S(2)}) collective-permute-start(bf16[4,3712]{1,0:T(4,128)(2,1)S(1)} %get-tuple-element.68), channel_id=1, source_target_pairs={{0,8},{1,9},{2,10},{3,11},{4,12},{5,13},{6,14},{7,15},{8,0},{9,1},... | collective-permute-start | bytes 89096 | tf_op jit(solution)/shard_map/ppermute | solution.py:164
  51.7 2.1 %collective-permute-start.8 = (bf16[4,3712]{1,0:T(4,128)(2,1)S(1)}, bf16[4,3712]{1,0:T(4,128)(2,1)S(1)}, u32[]{:S(2)}, u32[]{:S(2)}) collective-permute-start(bf16[4,3712]{1,0:T(4,128)(2,1)S(1)} %get-tuple-element.58), channel_id=1, source_target_pairs={{0,8},{1,9},{2,10},{3,11},{4,12},{5,13},{6,14},{7,15},{8,0},{9,1},... | collective-permute-start | bytes 89096 | tf_op jit(solution)/shard_map/ppermute | solution.py:164
  53.8 0.3 collective-permute-done.13.came
  54.1 1.2 %collective-permute-start.14 = (bf16[2,3712]{1,0:T(2,128)(2,1)S(1)}, bf16[2,3712]{1,0:T(2,128)(2,1)S(1)}, u32[]{:S(2)}, u32[]{:S(2)}) collective-permute-start(bf16[2,3712]{1,0:T(2,128)(2,1)S(1)} %get-tuple-element.70), channel_id=1, source_target_pairs={{0,16},{16,0},{1,17},{17,1},{2,18},{18,2},{3,19},{19,3},{4,20},{20... | collective-permute-start | bytes 44552 | tf_op jit(solution)/shard_map/ppermute | solution.py:163
  55.3 1.3 %collective-permute-done.8.came = bf16[4,3712]{1,0:T(4,128)(2,1)S(1)} collective-permute-done((bf16[4,3712]{1,0:T(4,128)(2,1)S(1)}, bf16[4,3712]{1,0:T(4,128)(2,1)S(1)}, u32[]{:S(2)}, u32[]{:S(2)}) %collective-permute-start.8) | collective-permute-done | bytes 29728 | tf_op jit(solution)/shard_map/ppermute | solution.py:164
  56.6 1.2 %collective-permute-start.9 = (bf16[2,3712]{1,0:T(2,128)(2,1)S(1)}, bf16[2,3712]{1,0:T(2,128)(2,1)S(1)}, u32[]{:S(2)}, u32[]{:S(2)}) collective-permute-start(bf16[2,3712]{1,0:T(2,128)(2,1)S(1)} %get-tuple-element.60), channel_id=1, source_target_pairs={{0,16},{16,0},{1,17},{17,1},{2,18},{18,2},{3,19},{19,3},{4,20},{20... | collective-permute-start | bytes 44552 | tf_op jit(solution)/shard_map/ppermute | solution.py:163
  58.4 2.0 %collective-permute-done.9.refs_1_ = bf16[2,3712]{1,0:T(2,128)(2,1)S(1)} collective-permute-done((bf16[2,3712]{1,0:T(2,128)(2,1)S(1)}, bf16[2,3712]{1,0:T(2,128)(2,1)S(1)}, u32[]{:S(2)}, u32[]{:S(2)}) %collective-permute-start.9) | collective-permute-done | bytes 14880 | tf_op jit(solution)/shard_map/ppermute | solution.py:163
  60.4 0.7 %shard_map.76 = bf16[2,7424]{1,0:T(2,128)(2,1)} custom-call(s32[1]{0:T(128)S(6)} %copy.6.counts, f32[2,3712]{1,0:T(2,128)S(1)} %get-tuple-element.59.refs_0_, bf16[2,3712]{1,0:T(2,128)(2,1)S(1)} %collective-permute-done.9.refs_1_, f32[2,3712]{1,0:T(2,128)S(1)} %get-tuple-element.69.refs_2_, bf16[2,3712]{1,0:T(2,128)(2,1)S(1)} %collective-permute-done.14.refs_3_), custom_call_target="tpu_custom_call" | custom-call | bytes 59392 | tf_op jit(solution)/shard_map/pallas_call | solution.py:151
  (22 shorter events, 0.5 us)
Async XLA Ops:
  0.0 5.9 %collective-permute-start = (bf16[2,7424]{1,0:T(2,128)(2,1)}, bf16[2,7424]{1,0:T(2,128)(2,1)S(1)}, u32[]{:S(2)}, u32[]{:S(2)}) collective-permute-start(bf16[2,7424]{1,0:T(2,128)(2,1)} %refs_0_.1), channel_id=1, source_target_pairs={{0,16},{16,0},{1,17},{17,1},{2,18},{18,2},{3,19},{19,3},{4,20},{20... | collective-permute-start | bytes 89096 | tf_op jit(solution)/shard_map/ppermute | solution.py:163
  2.9 3.0 %copy-start = (bf16[2,7424]{1,0:T(2,128)(2,1)S(1)}, bf16[2,7424]{1,0:T(2,128)(2,1)}, u32[]{:S(2)}) copy-start(bf16[2,7424]{1,0:T(2,128)(2,1)} %refs_0_.1) | copy-start | bytes 89092
  6.0 5.6 %collective-permute-start.1 = (bf16[4,7424]{1,0:T(4,128)(2,1)S(1)}, bf16[4,7424]{1,0:T(4,128)(2,1)S(1)}, u32[]{:S(2)}, u32[]{:S(2)}) collective-permute-start(bf16[4,7424]{1,0:T(4,128)(2,1)S(1)} %shard_map.56.rest_0_.refs_0_), channel_id=1, source_target_pairs={{0,8},{1,9},{2,10},{3,11},{4,12},{5,13},{6,14},{7,15},{8,0},{9,1},... | collective-permute-start | bytes 178184 | tf_op jit(solution)/shard_map/ppermute | solution.py:164
  11.6 4.9 %collective-permute-start.2 = (bf16[8,7424]{1,0:T(8,128)(2,1)S(1)}, bf16[8,7424]{1,0:T(8,128)(2,1)S(1)}, u32[]{:S(2)}, u32[]{:S(2)}) collective-permute-start(bf16[8,7424]{1,0:T(8,128)(2,1)S(1)} %shard_map.58.rest_0_.refs_0_), channel_id=1, source_target_pairs={{0,4},{1,5},{2,6},{3,7},{4,0},{5,1},{6,2},{7,3},{8,12},{9,13},{10,... | collective-permute-start | bytes 356360 | tf_op jit(solution)/shard_map/ppermute | solution.py:164
  16.6 7.5 %collective-permute-start.3 = (bf16[16,7424]{1,0:T(8,128)(2,1)S(1)}, bf16[16,7424]{1,0:T(8,128)(2,1)S(1)}, u32[]{:S(2)}, u32[]{:S(2)}) collective-permute-start(bf16[16,7424]{1,0:T(8,128)(2,1)S(1)} %shard_map.60.rest_0_.refs_0_), channel_id=1, source_target_pairs={{0,2},{1,3},{2,0},{3,1},{4,6},{5,7},{6,4},{7,5},{8,10},{9,11},{10,... | collective-permute-start | bytes 712712 | tf_op jit(solution)/shard_map/ppermute | solution.py:164
  24.2 3.7 %collective-permute-start.4 = (bf16[32,7424]{1,0:T(8,128)(2,1)S(1)}, bf16[32,7424]{1,0:T(8,128)(2,1)S(1)}, u32[]{:S(2)}, u32[]{:S(2)}) collective-permute-start(bf16[32,7424]{1,0:T(8,128)(2,1)S(1)} %shard_map.63.mine.rest_0_), channel_id=1, source_target_pairs={{0,1},{1,0},{2,3},{3,2},{4,5},{5,4},{6,7},{7,6},{8,9},{9,8},{10,11... | collective-permute-start | bytes 1425416 | tf_op jit(solution)/shard_map/ppermute | solution.py:164
  36.9 1.9 %collective-permute-start.10 = (bf16[32,3712]{1,0:T(8,128)(2,1)S(1)}, bf16[32,3712]{1,0:T(8,128)(2,1)S(1)}, u32[]{:S(2)}, u32[]{:S(2)}) collective-permute-start(bf16[32,3712]{1,0:T(8,128)(2,1)S(1)} %get-tuple-element.62), channel_id=1, source_target_pairs={{0,1},{1,0},{2,3},{3,2},{4,5},{5,4},{6,7},{7,6},{8,9},{9,8},{10,11... | collective-permute-start | bytes 712712 | tf_op jit(solution)/shard_map/ppermute | solution.py:164
  38.7 1.6 %collective-permute-start.5 = (bf16[32,3712]{1,0:T(8,128)(2,1)S(1)}, bf16[32,3712]{1,0:T(8,128)(2,1)S(1)}, u32[]{:S(2)}, u32[]{:S(2)}) collective-permute-start(bf16[32,3712]{1,0:T(8,128)(2,1)S(1)} %get-tuple-element.52), channel_id=1, source_target_pairs={{0,1},{1,0},{2,3},{3,2},{4,5},{5,4},{6,7},{7,6},{8,9},{9,8},{10,11... | collective-permute-start | bytes 712712 | tf_op jit(solution)/shard_map/ppermute | solution.py:164
  38.8 6.1 %collective-permute-start.11 = (bf16[16,3712]{1,0:T(8,128)(2,1)S(1)}, bf16[16,3712]{1,0:T(8,128)(2,1)S(1)}, u32[]{:S(2)}, u32[]{:S(2)}) collective-permute-start(bf16[16,3712]{1,0:T(8,128)(2,1)S(1)} %get-tuple-element.64), channel_id=1, source_target_pairs={{0,2},{1,3},{2,0},{3,1},{4,6},{5,7},{6,4},{7,5},{8,10},{9,11},{10,... | collective-permute-start | bytes 356360 | tf_op jit(solution)/shard_map/ppermute | solution.py:164
  40.3 6.8 %collective-permute-start.6 = (bf16[16,3712]{1,0:T(8,128)(2,1)S(1)}, bf16[16,3712]{1,0:T(8,128)(2,1)S(1)}, u32[]{:S(2)}, u32[]{:S(2)}) collective-permute-start(bf16[16,3712]{1,0:T(8,128)(2,1)S(1)} %get-tuple-element.54), channel_id=1, source_target_pairs={{0,2},{1,3},{2,0},{3,1},{4,6},{5,7},{6,4},{7,5},{8,10},{9,11},{10,... | collective-permute-start | bytes 356360 | tf_op jit(solution)/shard_map/ppermute | solution.py:164
  44.9 4.3 %collective-permute-start.12 = (bf16[8,3712]{1,0:T(8,128)(2,1)S(1)}, bf16[8,3712]{1,0:T(8,128)(2,1)S(1)}, u32[]{:S(2)}, u32[]{:S(2)}) collective-permute-start(bf16[8,3712]{1,0:T(8,128)(2,1)S(1)} %get-tuple-element.66), channel_id=1, source_target_pairs={{0,4},{1,5},{2,6},{3,7},{4,0},{5,1},{6,2},{7,3},{8,12},{9,13},{10,... | collective-permute-start | bytes 178184 | tf_op jit(solution)/shard_map/ppermute | solution.py:164
  47.1 4.6 %collective-permute-start.7 = (bf16[8,3712]{1,0:T(8,128)(2,1)S(1)}, bf16[8,3712]{1,0:T(8,128)(2,1)S(1)}, u32[]{:S(2)}, u32[]{:S(2)}) collective-permute-start(bf16[8,3712]{1,0:T(8,128)(2,1)S(1)} %get-tuple-element.56), channel_id=1, source_target_pairs={{0,4},{1,5},{2,6},{3,7},{4,0},{5,1},{6,2},{7,3},{8,12},{9,13},{10,... | collective-permute-start | bytes 178184 | tf_op jit(solution)/shard_map/ppermute | solution.py:164
  49.2 4.8 %collective-permute-start.13 = (bf16[4,3712]{1,0:T(4,128)(2,1)S(1)}, bf16[4,3712]{1,0:T(4,128)(2,1)S(1)}, u32[]{:S(2)}, u32[]{:S(2)}) collective-permute-start(bf16[4,3712]{1,0:T(4,128)(2,1)S(1)} %get-tuple-element.68), channel_id=1, source_target_pairs={{0,8},{1,9},{2,10},{3,11},{4,12},{5,13},{6,14},{7,15},{8,0},{9,1},... | collective-permute-start | bytes 89096 | tf_op jit(solution)/shard_map/ppermute | solution.py:164
  51.7 4.8 %collective-permute-start.8 = (bf16[4,3712]{1,0:T(4,128)(2,1)S(1)}, bf16[4,3712]{1,0:T(4,128)(2,1)S(1)}, u32[]{:S(2)}, u32[]{:S(2)}) collective-permute-start(bf16[4,3712]{1,0:T(4,128)(2,1)S(1)} %get-tuple-element.58), channel_id=1, source_target_pairs={{0,8},{1,9},{2,10},{3,11},{4,12},{5,13},{6,14},{7,15},{8,0},{9,1},... | collective-permute-start | bytes 89096 | tf_op jit(solution)/shard_map/ppermute | solution.py:164
  54.1 4.3 %collective-permute-start.14 = (bf16[2,3712]{1,0:T(2,128)(2,1)S(1)}, bf16[2,3712]{1,0:T(2,128)(2,1)S(1)}, u32[]{:S(2)}, u32[]{:S(2)}) collective-permute-start(bf16[2,3712]{1,0:T(2,128)(2,1)S(1)} %get-tuple-element.70), channel_id=1, source_target_pairs={{0,16},{16,0},{1,17},{17,1},{2,18},{18,2},{3,19},{19,3},{4,20},{20... | collective-permute-start | bytes 44552 | tf_op jit(solution)/shard_map/ppermute | solution.py:163
  56.6 3.8 %collective-permute-start.9 = (bf16[2,3712]{1,0:T(2,128)(2,1)S(1)}, bf16[2,3712]{1,0:T(2,128)(2,1)S(1)}, u32[]{:S(2)}, u32[]{:S(2)}) collective-permute-start(bf16[2,3712]{1,0:T(2,128)(2,1)S(1)} %get-tuple-element.60), channel_id=1, source_target_pairs={{0,16},{16,0},{1,17},{17,1},{2,18},{18,2},{3,19},{19,3},{4,20},{20... | collective-permute-start | bytes 44552 | tf_op jit(solution)/shard_map/ppermute | solution.py:163

commit v5 on v4

--- a/solution.py
+++ b/solution.py
@@ -61,8 +61,19 @@
     )(*parts, *tokens)
 
 
-def hidden_kernel(mine, theirs, *refs):
-    pieces, hidden, tokens = refs[: 2 * BLOCKS], refs[2 * BLOCKS : -1], refs[-1]
+def hidden_kernel(share, mine, theirs, *refs):
+    pieces, down, refs = refs[: 2 * BLOCKS], refs[2 * BLOCKS], refs[2 * BLOCKS + 1 :]
+    hidden, brought, (tokens, sems) = refs[:BLOCKS], refs[BLOCKS:-2], refs[-2:]
+    rows = pieces[0].shape[0]
+    first = lax.axis_index("groups") * share
+    copies = [
+        pltpu.make_async_copy(
+            down.at[pl.ds(pl.multiple_of(first + block * rows, 16), rows)], into, sems.at[block]
+        )
+        for block, into in enumerate(brought)
+    ]
+    for copy in copies:
+        copy.start()
     half = mine.shape[0]
     tokens[:half, :] = mine[...]
     tokens[half:, :] = theirs[...]
@@ -75,20 +86,22 @@
         )
         value = gate_value / (1.0 + jnp.exp(-gate_value)) * up_value
         out[...] = value.astype(out.dtype)
-
-
-def hidden_of(mine, theirs, pieces):
+    for copy in copies:
+        copy.wait()
+
+
+def hidden_of(mine, theirs, pieces, down, share):
     rows, width = pieces[0].shape
     count = mine.shape[0] + theirs.shape[0]
     return pl.pallas_call(
-        hidden_kernel,
-        out_shape=(pltpu.VMEM((count, rows), mine.dtype),) * BLOCKS,
-        in_specs=[VMEM] * (2 + 2 * BLOCKS),
-        out_specs=(VMEM,) * BLOCKS,
-        scratch_shapes=[pltpu.VMEM((count, width), mine.dtype)],
+        functools.partial(hidden_kernel, share),
+        out_shape=(pltpu.VMEM((count, rows), mine.dtype),) * BLOCKS + (pltpu.VMEM((rows, width), down.dtype),) * BLOCKS,
+        in_specs=[VMEM] * (2 + 2 * BLOCKS) + [HBM],
+        out_specs=(VMEM,) * (2 * BLOCKS),
+        scratch_shapes=[pltpu.VMEM((count, width), mine.dtype), pltpu.SemaphoreType.DMA((BLOCKS,))],
         compiler_params=pltpu.CompilerParams(vmem_limit_bytes=12 * MIB),
-        cost_estimate=cost(4 * BLOCKS * count * rows * width, 4 * BLOCKS * rows * width),
-    )(*(pltpu.with_memory_space_constraint(one, pltpu.VMEM) for one in (mine, theirs, *pieces)))
+        cost_estimate=cost(4 * BLOCKS * count * rows * width, 6 * BLOCKS * rows * width),
+    )(*(pltpu.with_memory_space_constraint(one, pltpu.VMEM) for one in (mine, theirs, *pieces)), down)
 
 
 def down_kernel(start, *refs):
@@ -115,20 +128,30 @@
     )(*(pltpu.with_memory_space_constraint(one, pltpu.VMEM) for one in (*hidden, *pieces)))
 
 
-def fold_kernel(keep, came, kept, send):
+def fold_kernel(swapped, keep, came, kept, send):
+    total = keep[...] + came[...].astype(jnp.float32)
     rows = kept.shape[0]
-    kept[...] = keep[:rows, :] + came[:rows, :].astype(jnp.float32)
-    send[...] = (keep[rows:, :] + came[rows:, :].astype(jnp.float32)).astype(send.dtype)
-
-
-def fold(keep, came):
+    if swapped:
+        part = rows // 2
+        for at in range(2):
+            start = 2 * at * part
+            kept[at * part : (at + 1) * part, :] = total[start : start + part]
+        send[...] = jnp.concatenate(
+            [total[part : 2 * part], total[3 * part : 4 * part]], axis=0
+        ).astype(send.dtype)
+    else:
+        kept[...] = total[:rows]
+        send[...] = total[rows:].astype(send.dtype)
+
+
+def fold(keep, came, swapped):
     rows, columns = keep.shape[0] // 2, keep.shape[1]
     return pl.pallas_call(
-        fold_kernel,
+        functools.partial(fold_kernel, swapped),
         out_shape=(pltpu.VMEM((rows, columns), jnp.float32), pltpu.VMEM((rows, columns), jnp.bfloat16)),
         in_specs=[VMEM, VMEM],
         out_specs=(VMEM, VMEM),
-        compiler_params=pltpu.CompilerParams(vmem_limit_bytes=2 * MIB),
+        compiler_params=pltpu.CompilerParams(vmem_limit_bytes=4 * MIB),
         cost_estimate=cost(0, 8 * keep.size),
     )(keep, came)
 
@@ -199,27 +222,31 @@
     )
     share = gate.shape[0] // 2
     rows = share // BLOCKS
-    wanted = [[(gate, 0)], [(up, 0)], [(gate, rows)], [(up, rows), (down, 0)], [(down, rows)]]
+    wanted = [[(gate, 0)], [(up, 0)], [(gate, rows)], [(up, rows)], []]
     masks = [*masks, 0]
     mine, after, pieces = tokens, (), []
     for step, (mask, sources) in enumerate(zip(reversed(masks), wanted)):
         theirs = exchange(mine, mask, count)
-        tokens_of = []
+        ends = []
         for source, start in sources:
-            piece, token = load(source, after, start, rows, share)
+            piece, end = load(source, after, start, rows, share)
             pieces.append(piece)
-            tokens_of.append(token)
+            ends.append(end)
         if step + 1 < len(masks):
-            mine = join([mine, theirs], tokens_of)
+            mine = join([mine, theirs], ends)
             after = (mine,)
-    hidden = hidden_of(mine, theirs, pieces[: 2 * BLOCKS])
+    outs = hidden_of(mine, theirs, pieces, down, share)
     columns = width // CHUNKS
     parts = []
     for chunk in range(CHUNKS):
-        keep, send = down_of(hidden, pieces[2 * BLOCKS :], chunk * columns, columns)
-        for mask in masks[:-1]:
-            keep, send = fold(keep, exchange(send, mask, count))
-        parts.append((keep, exchange(send, masks[-1], count)))
+        keep, send = down_of(outs[:BLOCKS], outs[BLOCKS:], chunk * columns, columns)
+        order = list(masks)
+        swap = chunk % 2 == 1
+        if swap:
+            order[1], order[2] = order[2], order[1]
+        for step, mask in enumerate(order[:-1]):
+            keep, send = fold(keep, exchange(send, mask, count), swap and step == 0)
+        parts.append((keep, exchange(send, order[-1], count)))
     return last(valid_counts, parts)
 
 

time: 61.3 us -> 62.2 us (1.015)
  waiting for transfers between devices: 9.5 us -> 11.9 us
  Pallas kernels: 29.7 us -> 27.9 us
    pallas_call x6 -> x4, Pallas kernels: 18.4 us -> 11.9 us  [load(): pl.pallas_call(functools.partial(load_kernel, start, share), out_shape=(p...]
    pallas_call x9, Pallas kernels: 8.14 us -> 12.9 us  [the longest x1 12.6 us: hidden_of(): pl.pallas_call(functools.partial(hidden_kernel, share), out_shape=(pltpu....]
    ppermute x12, waiting for transfers between devices: 7.53 us -> 9.89 us  [exchange(): return lax.ppermute(array, 'tensor', [(i, i ^ mask) for i in range(count)])]
    ppermute x12, starting transfers between devices: 15.7 us -> 16.5 us  [exchange(): return lax.ppermute(array, 'tensor', [(i, i ^ mask) for i in range(count)])]
  transfers between devices with their start and end apart: 15 -> 15, of which waited for: 8 -> 8; matrix products, arithmetic and copies ran while one was open for 0% -> 0% of each run, Pallas kernels for 33% -> 21%
where the time goes in v5:
time: 62.2 us; the launch traced here: 62 us
  Pallas kernels  27.9 us (45%)
  starting transfers between devices  21.4 us (34%)
  waiting for transfers between devices  11.9 us (19%)
  between operations  0.8 us (1%)
    ppermute x12, starting transfers between devices, exchange(): return lax.ppermute(array, 'tensor', [(i, i ^ mask) for i in range(count)])  16.5 us
    pallas_call x1, Pallas kernels, hidden_of(): pl.pallas_call(functools.partial(hidden_kernel, share), out_shape=(pltpu....  12.6 us
    pallas_call x4, Pallas kernels, load(): pl.pallas_call(functools.partial(load_kernel, start, share), out_shape=(p...  11.9 us
    ppermute x12, waiting for transfers between devices, exchange(): return lax.ppermute(array, 'tensor', [(i, i ^ mask) for i in range(count)])  9.89 us
    ppermute x3, starting transfers between devices, exchange(): return lax.ppermute(array, 'groups', [(0, 1), (1, 0)])  4.94 us
    pallas_call x2, Pallas kernels, down_of(): pl.pallas_call(functools.partial(down_kernel, start), out_shape=(pltpu.VM...  2.4 us
    ppermute x3, waiting for transfers between devices, exchange(): return lax.ppermute(array, 'groups', [(0, 1), (1, 0)])  1.98 us
  transfers between devices with their start and end apart: 15, of which 8 were waited for; matrix products, arithmetic and copies ran while one was open for 0% of the time, Pallas kernels for 21%

profile of v5, /device:TPU:0, one launch (start us, length us, event | category | flops | bytes accessed | tf_op | source)
XLA Modules:
  0.0 62.0 jit_solution(6060263795349146)
XLA Ops:
  0.0 2.9 %collective-permute-start = (bf16[2,7424]{1,0:T(2,128)(2,1)}, bf16[2,7424]{1,0:T(2,128)(2,1)S(1)}, u32[]{:S(2)}, u32[]{:S(2)}) collective-permute-start(bf16[2,7424]{1,0:T(2,128)(2,1)} %refs_0_.1), channel_id=1, source_target_pairs={{0,16},{16,0},{1,17},{17,1},{2,18},{18,2},{3,19},{19,3},{4,20},{20... | collective-permute-start | bytes 89096 | tf_op jit(solution)/shard_map/ppermute | solution.py:186
  2.9 3.0 %shard_map.55 = (bf16[464,7424]{1,0:T(8,128)(2,1)S(1)}, f32[8,128]{1,0:T(8,128)S(1)}) custom-call(bf16[1856,7424]{1,0:T(8,128)(2,1)} %bitcast.2), custom_call_target="tpu_custom_call" | custom-call | bytes 6889472 | tf_op jit(solution)/shard_map/pallas_call | solution.py:33
  6.0 2.7 %collective-permute-start.1 = (bf16[4,7424]{1,0:T(4,128)(2,1)S(1)}, bf16[4,7424]{1,0:T(4,128)(2,1)S(1)}, u32[]{:S(2)}, u32[]{:S(2)}) collective-permute-start(bf16[4,7424]{1,0:T(4,128)(2,1)S(1)} %shard_map.56.rest_0_.refs_0_), channel_id=1, source_target_pairs={{0,8},{1,9},{2,10},{3,11},{4,12},{5,13},{6,14},{7,15},{8,0},{9,1},... | collective-permute-start | bytes 178184 | tf_op jit(solution)/shard_map/ppermute | solution.py:187
  8.6 3.0 %shard_map.57 = (bf16[464,7424]{1,0:T(8,128)(2,1)S(1)}, f32[8,128]{1,0:T(8,128)S(1)}) custom-call(bf16[1856,7424]{1,0:T(8,128)(2,1)} %bitcast.4, bf16[4,7424]{1,0:T(4,128)(2,1)S(1)} %shard_map.56.rest_0_.refs_0_), custom_call_target="tpu_custom_call" | custom-call | bytes 6889472 | tf_op jit(solution)/shard_map/pallas_call | solution.py:33
  11.6 1.6 %collective-permute-start.2 = (bf16[8,7424]{1,0:T(8,128)(2,1)S(1)}, bf16[8,7424]{1,0:T(8,128)(2,1)S(1)}, u32[]{:S(2)}, u32[]{:S(2)}) collective-permute-start(bf16[8,7424]{1,0:T(8,128)(2,1)S(1)} %shard_map.58.rest_0_.refs_0_), channel_id=1, source_target_pairs={{0,4},{1,5},{2,6},{3,7},{4,0},{5,1},{6,2},{7,3},{8,12},{9,13},{10,... | collective-permute-start | bytes 356360 | tf_op jit(solution)/shard_map/ppermute | solution.py:187
  13.3 3.0 %shard_map.59 = (bf16[464,7424]{1,0:T(8,128)(2,1)S(1)}, f32[8,128]{1,0:T(8,128)S(1)}) custom-call(bf16[1856,7424]{1,0:T(8,128)(2,1)} %bitcast.3, bf16[8,7424]{1,0:T(8,128)(2,1)S(1)} %shard_map.58.rest_0_.refs_0_), custom_call_target="tpu_custom_call" | custom-call | bytes 6889472 | tf_op jit(solution)/shard_map/pallas_call | solution.py:33
  16.3 0.3 collective-permute-done.2.refs_1_
  16.6 1.6 %collective-permute-start.3 = (bf16[16,7424]{1,0:T(8,128)(2,1)S(1)}, bf16[16,7424]{1,0:T(8,128)(2,1)S(1)}, u32[]{:S(2)}, u32[]{:S(2)}) collective-permute-start(bf16[16,7424]{1,0:T(8,128)(2,1)S(1)} %shard_map.60.rest_0_.refs_0_), channel_id=1, source_target_pairs={{0,2},{1,3},{2,0},{3,1},{4,6},{5,7},{6,4},{7,5},{8,10},{9,11},{10,... | collective-permute-start | bytes 712712 | tf_op jit(solution)/shard_map/ppermute | solution.py:187
  18.2 3.0 %shard_map.61 = (bf16[464,7424]{1,0:T(8,128)(2,1)S(1)}, f32[8,128]{1,0:T(8,128)S(1)}) custom-call(bf16[1856,7424]{1,0:T(8,128)(2,1)} %bitcast.5, bf16[16,7424]{1,0:T(8,128)(2,1)S(1)} %shard_map.60.rest_0_.refs_0_), custom_call_target="tpu_custom_call" | custom-call | bytes 6889472 | tf_op jit(solution)/shard_map/pallas_call | solution.py:33
  21.1 1.9 %collective-permute-done.3.refs_1_ = bf16[16,7424]{1,0:T(8,128)(2,1)S(1)} collective-permute-done((bf16[16,7424]{1,0:T(8,128)(2,1)S(1)}, bf16[16,7424]{1,0:T(8,128)(2,1)S(1)}, u32[]{:S(2)}, u32[]{:S(2)}) %collective-permute-start.3) | collective-permute-done | bytes 237600 | tf_op jit(solution)/shard_map/ppermute | solution.py:187
  23.1 0.1 collective-permute-start.4
  23.2 1.8 %collective-permute-done.4.theirs = bf16[32,7424]{1,0:T(8,128)(2,1)S(1)} collective-permute-done((bf16[32,7424]{1,0:T(8,128)(2,1)S(1)}, bf16[32,7424]{1,0:T(8,128)(2,1)S(1)}, u32[]{:S(2)}, u32[]{:S(2)}) %collective-permute-start.4) | collective-permute-done | bytes 475168 | tf_op jit(solution)/shard_map/ppermute | solution.py:187
  25.0 12.6 %shard_map.63 = (bf16[64,464]{1,0:T(8,128)(2,1)S(1)}, bf16[64,464]{1,0:T(8,128)(2,1)S(1)}, bf16[464,7424]{1,0:T(8,128)(2,1)S(1)}, bf16[464,7424]{1,0:T(8,128)(2,1)S(1)}) custom-call(bf16[32,7424]{1,0:T(8,128)(2,1)S(1)} %shard_map.62.mine, bf16[32,7424]{1,0:T(8,128)(2,1)S(1)} %collective-permute-done.4.theirs, ...), custom_call_target="tpu_custom_call" | custom-call | flops 1763704832 | bytes 41336832 | tf_op jit(solution)/shard_map/pallas_call | solution.py:96
  37.6 1.2 %shard_map.69 = (f32[32,3712]{1,0:T(8,128)S(1)}, bf16[32,3712]{1,0:T(8,128)(2,1)S(1)}) custom-call(bf16[64,464]{1,0:T(8,128)(2,1)S(1)} %get-tuple-element.45.refs_0_, bf16[64,464]{1,0:T(8,128)(2,1)S(1)} %get-tuple-element.46.refs_1_, bf16[464,7424]{1,0:T(8,128)(2,1)S(1)} %get-tuple-element.47.refs_2_, bf16[464,7424]{1,0:T(8,128)(2,1)S(1)} %get-tuple-element.48.refs_3_), custom_call_target="tpu_custom_call" | custom-call | flops 440926208 | bytes 6889472 | tf_op jit(solution)/shard_map/pallas_call | solution.py:121
  38.8 0.2 collective-permute-start.10
  39.0 1.2 %shard_map.64 = (f32[32,3712]{1,0:T(8,128)S(1)}, bf16[32,3712]{1,0:T(8,128)(2,1)S(1)}) custom-call(bf16[64,464]{1,0:T(8,128)(2,1)S(1)} %get-tuple-element.45.refs_0_, bf16[64,464]{1,0:T(8,128)(2,1)S(1)} %get-tuple-element.46.refs_1_, bf16[464,7424]{1,0:T(8,128)(2,1)S(1)} %get-tuple-element.47.refs_2_, bf16[464,7424]{1,0:T(8,128)(2,1)S(1)} %get-tuple-element.48.refs_3_), custom_call_target="tpu_custom_call" | custom-call | flops 440926208 | bytes 6889472 | tf_op jit(solution)/shard_map/pallas_call | solution.py:121
  40.2 0.4 collective-permute-start.5
  40.7 1.3 %collective-permute-start.11 = (bf16[16,3712]{1,0:T(8,128)(2,1)S(1)}, bf16[16,3712]{1,0:T(8,128)(2,1)S(1)}, u32[]{:S(2)}, u32[]{:S(2)}) collective-permute-start(bf16[16,3712]{1,0:T(8,128)(2,1)S(1)} %get-tuple-element.62), channel_id=1, source_target_pairs={{0,4},{1,5},{2,6},{3,7},{4,0},{5,1},{6,2},{7,3},{8,12},{9,13},{10,... | collective-permute-start | bytes 356360 | tf_op jit(solution)/shard_map/ppermute | solution.py:187
  42.1 0.1 shard_map.65
  42.1 1.6 %collective-permute-start.6 = (bf16[16,3712]{1,0:T(8,128)(2,1)S(1)}, bf16[16,3712]{1,0:T(8,128)(2,1)S(1)}, u32[]{:S(2)}, u32[]{:S(2)}) collective-permute-start(bf16[16,3712]{1,0:T(8,128)(2,1)S(1)} %get-tuple-element.52), channel_id=1, source_target_pairs={{0,2},{1,3},{2,0},{3,1},{4,6},{5,7},{6,4},{7,5},{8,10},{9,11},{10,... | collective-permute-start | bytes 356360 | tf_op jit(solution)/shard_map/ppermute | solution.py:187
  43.7 2.3 %collective-permute-done.11.came = bf16[16,3712]{1,0:T(8,128)(2,1)S(1)} collective-permute-done((bf16[16,3712]{1,0:T(8,128)(2,1)S(1)}, bf16[16,3712]{1,0:T(8,128)(2,1)S(1)}, u32[]{:S(2)}, u32[]{:S(2)}) %collective-permute-start.11) | collective-permute-done | bytes 118816 | tf_op jit(solution)/shard_map/ppermute | solution.py:187
  46.1 1.6 %collective-permute-start.12 = (bf16[8,3712]{1,0:T(8,128)(2,1)S(1)}, bf16[8,3712]{1,0:T(8,128)(2,1)S(1)}, u32[]{:S(2)}, u32[]{:S(2)}) collective-permute-start(bf16[8,3712]{1,0:T(8,128)(2,1)S(1)} %get-tuple-element.64), channel_id=1, source_target_pairs={{0,2},{1,3},{2,0},{3,1},{4,6},{5,7},{6,4},{7,5},{8,10},{9,11},{10,... | collective-permute-start | bytes 178184 | tf_op jit(solution)/shard_map/ppermute | solution.py:187
  47.7 1.3 %collective-permute-start.7 = (bf16[8,3712]{1,0:T(8,128)(2,1)S(1)}, bf16[8,3712]{1,0:T(8,128)(2,1)S(1)}, u32[]{:S(2)}, u32[]{:S(2)}) collective-permute-start(bf16[8,3712]{1,0:T(8,128)(2,1)S(1)} %get-tuple-element.54), channel_id=1, source_target_pairs={{0,4},{1,5},{2,6},{3,7},{4,0},{5,1},{6,2},{7,3},{8,12},{9,13},{10,... | collective-permute-start | bytes 178184 | tf_op jit(solution)/shard_map/ppermute | solution.py:187
  49.1 1.3 %collective-permute-done.12.came = bf16[8,3712]{1,0:T(8,128)(2,1)S(1)} collective-permute-done((bf16[8,3712]{1,0:T(8,128)(2,1)S(1)}, bf16[8,3712]{1,0:T(8,128)(2,1)S(1)}, u32[]{:S(2)}, u32[]{:S(2)}) %collective-permute-start.12) | collective-permute-done | bytes 59424 | tf_op jit(solution)/shard_map/ppermute | solution.py:187
  50.4 2.2 %collective-permute-start.13 = (bf16[4,3712]{1,0:T(4,128)(2,1)S(1)}, bf16[4,3712]{1,0:T(4,128)(2,1)S(1)}, u32[]{:S(2)}, u32[]{:S(2)}) collective-permute-start(bf16[4,3712]{1,0:T(4,128)(2,1)S(1)} %get-tuple-element.66), channel_id=1, source_target_pairs={{0,8},{1,9},{2,10},{3,11},{4,12},{5,13},{6,14},{7,15},{8,0},{9,1},... | collective-permute-start | bytes 89096 | tf_op jit(solution)/shard_map/ppermute | solution.py:187
  52.7 1.8 %collective-permute-start.8 = (bf16[4,3712]{1,0:T(4,128)(2,1)S(1)}, bf16[4,3712]{1,0:T(4,128)(2,1)S(1)}, u32[]{:S(2)}, u32[]{:S(2)}) collective-permute-start(bf16[4,3712]{1,0:T(4,128)(2,1)S(1)} %get-tuple-element.56), channel_id=1, source_target_pairs={{0,8},{1,9},{2,10},{3,11},{4,12},{5,13},{6,14},{7,15},{8,0},{9,1},... | collective-permute-start | bytes 89096 | tf_op jit(solution)/shard_map/ppermute | solution.py:187
  54.4 0.8 %collective-permute-done.13.came = bf16[4,3712]{1,0:T(4,128)(2,1)S(1)} collective-permute-done((bf16[4,3712]{1,0:T(4,128)(2,1)S(1)}, bf16[4,3712]{1,0:T(4,128)(2,1)S(1)}, u32[]{:S(2)}, u32[]{:S(2)}) %collective-permute-start.13) | collective-permute-done | bytes 29728 | tf_op jit(solution)/shard_map/ppermute | solution.py:187
  55.3 0.9 %collective-permute-start.14 = (bf16[2,3712]{1,0:T(2,128)(2,1)S(1)}, bf16[2,3712]{1,0:T(2,128)(2,1)S(1)}, u32[]{:S(2)}, u32[]{:S(2)}) collective-permute-start(bf16[2,3712]{1,0:T(2,128)(2,1)S(1)} %get-tuple-element.68), channel_id=1, source_target_pairs={{0,16},{16,0},{1,17},{17,1},{2,18},{18,2},{3,19},{19,3},{4,20},{20... | collective-permute-start | bytes 44552 | tf_op jit(solution)/shard_map/ppermute | solution.py:186
  56.1 1.4 %collective-permute-done.8.came = bf16[4,3712]{1,0:T(4,128)(2,1)S(1)} collective-permute-done((bf16[4,3712]{1,0:T(4,128)(2,1)S(1)}, bf16[4,3712]{1,0:T(4,128)(2,1)S(1)}, u32[]{:S(2)}, u32[]{:S(2)}) %collective-permute-start.8) | collective-permute-done | bytes 29728 | tf_op jit(solution)/shard_map/ppermute | solution.py:187
  57.5 1.1 %collective-permute-start.9 = (bf16[2,3712]{1,0:T(2,128)(2,1)S(1)}, bf16[2,3712]{1,0:T(2,128)(2,1)S(1)}, u32[]{:S(2)}, u32[]{:S(2)}) collective-permute-start(bf16[2,3712]{1,0:T(2,128)(2,1)S(1)} %get-tuple-element.58), channel_id=1, source_target_pairs={{0,16},{16,0},{1,17},{17,1},{2,18},{18,2},{3,19},{19,3},{4,20},{20... | collective-permute-start | bytes 44552 | tf_op jit(solution)/shard_map/ppermute | solution.py:186
  59.4 2.0 %collective-permute-done.9.refs_1_ = bf16[2,3712]{1,0:T(2,128)(2,1)S(1)} collective-permute-done((bf16[2,3712]{1,0:T(2,128)(2,1)S(1)}, bf16[2,3712]{1,0:T(2,128)(2,1)S(1)}, u32[]{:S(2)}, u32[]{:S(2)}) %collective-permute-start.9) | collective-permute-done | bytes 14880 | tf_op jit(solution)/shard_map/ppermute | solution.py:186
  61.3 0.7 %shard_map.74 = bf16[2,7424]{1,0:T(2,128)(2,1)} custom-call(s32[1]{0:T(128)S(6)} %copy.6.counts, f32[2,3712]{1,0:T(2,128)S(1)} %get-tuple-element.57.refs_0_, bf16[2,3712]{1,0:T(2,128)(2,1)S(1)} %collective-permute-done.9.refs_1_, f32[2,3712]{1,0:T(2,128)S(1)} %get-tuple-element.67.refs_2_, bf16[2,3712]{1,0:T(2,128)(2,1)S(1)} %collective-permute-done.14.refs_3_), custom_call_target="tpu_custom_call" | custom-call | bytes 59392 | tf_op jit(solution)/shard_map/pallas_call | solution.py:174
  (20 shorter events, 0.3 us)
Async XLA Ops:
  0.0 5.9 %collective-permute-start = (bf16[2,7424]{1,0:T(2,128)(2,1)}, bf16[2,7424]{1,0:T(2,128)(2,1)S(1)}, u32[]{:S(2)}, u32[]{:S(2)}) collective-permute-start(bf16[2,7424]{1,0:T(2,128)(2,1)} %refs_0_.1), channel_id=1, source_target_pairs={{0,16},{16,0},{1,17},{17,1},{2,18},{18,2},{3,19},{19,3},{4,20},{20... | collective-permute-start | bytes 89096 | tf_op jit(solution)/shard_map/ppermute | solution.py:186
  2.9 3.0 %copy-start = (bf16[2,7424]{1,0:T(2,128)(2,1)S(1)}, bf16[2,7424]{1,0:T(2,128)(2,1)}, u32[]{:S(2)}) copy-start(bf16[2,7424]{1,0:T(2,128)(2,1)} %refs_0_.1) | copy-start | bytes 89092
  6.0 5.6 %collective-permute-start.1 = (bf16[4,7424]{1,0:T(4,128)(2,1)S(1)}, bf16[4,7424]{1,0:T(4,128)(2,1)S(1)}, u32[]{:S(2)}, u32[]{:S(2)}) collective-permute-start(bf16[4,7424]{1,0:T(4,128)(2,1)S(1)} %shard_map.56.rest_0_.refs_0_), channel_id=1, source_target_pairs={{0,8},{1,9},{2,10},{3,11},{4,12},{5,13},{6,14},{7,15},{8,0},{9,1},... | collective-permute-start | bytes 178184 | tf_op jit(solution)/shard_map/ppermute | solution.py:187
  11.6 4.9 %collective-permute-start.2 = (bf16[8,7424]{1,0:T(8,128)(2,1)S(1)}, bf16[8,7424]{1,0:T(8,128)(2,1)S(1)}, u32[]{:S(2)}, u32[]{:S(2)}) collective-permute-start(bf16[8,7424]{1,0:T(8,128)(2,1)S(1)} %shard_map.58.rest_0_.refs_0_), channel_id=1, source_target_pairs={{0,4},{1,5},{2,6},{3,7},{4,0},{5,1},{6,2},{7,3},{8,12},{9,13},{10,... | collective-permute-start | bytes 356360 | tf_op jit(solution)/shard_map/ppermute | solution.py:187
  16.6 6.5 %collective-permute-start.3 = (bf16[16,7424]{1,0:T(8,128)(2,1)S(1)}, bf16[16,7424]{1,0:T(8,128)(2,1)S(1)}, u32[]{:S(2)}, u32[]{:S(2)}) collective-permute-start(bf16[16,7424]{1,0:T(8,128)(2,1)S(1)} %shard_map.60.rest_0_.refs_0_), channel_id=1, source_target_pairs={{0,2},{1,3},{2,0},{3,1},{4,6},{5,7},{6,4},{7,5},{8,10},{9,11},{10,... | collective-permute-start | bytes 712712 | tf_op jit(solution)/shard_map/ppermute | solution.py:187
  23.1 1.9 %collective-permute-start.4 = (bf16[32,7424]{1,0:T(8,128)(2,1)S(1)}, bf16[32,7424]{1,0:T(8,128)(2,1)S(1)}, u32[]{:S(2)}, u32[]{:S(2)}) collective-permute-start(bf16[32,7424]{1,0:T(8,128)(2,1)S(1)} %shard_map.62.mine), channel_id=1, source_target_pairs={{0,1},{1,0},{2,3},{3,2},{4,5},{5,4},{6,7},{7,6},{8,9},{9,8},{10,11... | collective-permute-start | bytes 1425416 | tf_op jit(solution)/shard_map/ppermute | solution.py:187
  38.8 1.9 %collective-permute-start.10 = (bf16[32,3712]{1,0:T(8,128)(2,1)S(1)}, bf16[32,3712]{1,0:T(8,128)(2,1)S(1)}, u32[]{:S(2)}, u32[]{:S(2)}) collective-permute-start(bf16[32,3712]{1,0:T(8,128)(2,1)S(1)} %get-tuple-element.60), channel_id=1, source_target_pairs={{0,1},{1,0},{2,3},{3,2},{4,5},{5,4},{6,7},{7,6},{8,9},{9,8},{10,11... | collective-permute-start | bytes 712712 | tf_op jit(solution)/shard_map/ppermute | solution.py:187
  40.2 1.8 %collective-permute-start.5 = (bf16[32,3712]{1,0:T(8,128)(2,1)S(1)}, bf16[32,3712]{1,0:T(8,128)(2,1)S(1)}, u32[]{:S(2)}, u32[]{:S(2)}) collective-permute-start(bf16[32,3712]{1,0:T(8,128)(2,1)S(1)} %get-tuple-element.50), channel_id=1, source_target_pairs={{0,1},{1,0},{2,3},{3,2},{4,5},{5,4},{6,7},{7,6},{8,9},{9,8},{10,11... | collective-permute-start | bytes 712712 | tf_op jit(solution)/shard_map/ppermute | solution.py:187
  40.7 5.3 %collective-permute-start.11 = (bf16[16,3712]{1,0:T(8,128)(2,1)S(1)}, bf16[16,3712]{1,0:T(8,128)(2,1)S(1)}, u32[]{:S(2)}, u32[]{:S(2)}) collective-permute-start(bf16[16,3712]{1,0:T(8,128)(2,1)S(1)} %get-tuple-element.62), channel_id=1, source_target_pairs={{0,4},{1,5},{2,6},{3,7},{4,0},{5,1},{6,2},{7,3},{8,12},{9,13},{10,... | collective-permute-start | bytes 356360 | tf_op jit(solution)/shard_map/ppermute | solution.py:187
  42.1 5.5 %collective-permute-start.6 = (bf16[16,3712]{1,0:T(8,128)(2,1)S(1)}, bf16[16,3712]{1,0:T(8,128)(2,1)S(1)}, u32[]{:S(2)}, u32[]{:S(2)}) collective-permute-start(bf16[16,3712]{1,0:T(8,128)(2,1)S(1)} %get-tuple-element.52), channel_id=1, source_target_pairs={{0,2},{1,3},{2,0},{3,1},{4,6},{5,7},{6,4},{7,5},{8,10},{9,11},{10,... | collective-permute-start | bytes 356360 | tf_op jit(solution)/shard_map/ppermute | solution.py:187
  46.1 4.3 %collective-permute-start.12 = (bf16[8,3712]{1,0:T(8,128)(2,1)S(1)}, bf16[8,3712]{1,0:T(8,128)(2,1)S(1)}, u32[]{:S(2)}, u32[]{:S(2)}) collective-permute-start(bf16[8,3712]{1,0:T(8,128)(2,1)S(1)} %get-tuple-element.64), channel_id=1, source_target_pairs={{0,2},{1,3},{2,0},{3,1},{4,6},{5,7},{6,4},{7,5},{8,10},{9,11},{10,... | collective-permute-start | bytes 178184 | tf_op jit(solution)/shard_map/ppermute | solution.py:187
  47.7 4.9 %collective-permute-start.7 = (bf16[8,3712]{1,0:T(8,128)(2,1)S(1)}, bf16[8,3712]{1,0:T(8,128)(2,1)S(1)}, u32[]{:S(2)}, u32[]{:S(2)}) collective-permute-start(bf16[8,3712]{1,0:T(8,128)(2,1)S(1)} %get-tuple-element.54), channel_id=1, source_target_pairs={{0,4},{1,5},{2,6},{3,7},{4,0},{5,1},{6,2},{7,3},{8,12},{9,13},{10,... | collective-permute-start | bytes 178184 | tf_op jit(solution)/shard_map/ppermute | solution.py:187
  50.4 4.8 %collective-permute-start.13 = (bf16[4,3712]{1,0:T(4,128)(2,1)S(1)}, bf16[4,3712]{1,0:T(4,128)(2,1)S(1)}, u32[]{:S(2)}, u32[]{:S(2)}) collective-permute-start(bf16[4,3712]{1,0:T(4,128)(2,1)S(1)} %get-tuple-element.66), channel_id=1, source_target_pairs={{0,8},{1,9},{2,10},{3,11},{4,12},{5,13},{6,14},{7,15},{8,0},{9,1},... | collective-permute-start | bytes 89096 | tf_op jit(solution)/shard_map/ppermute | solution.py:187
  52.7 4.8 %collective-permute-start.8 = (bf16[4,3712]{1,0:T(4,128)(2,1)S(1)}, bf16[4,3712]{1,0:T(4,128)(2,1)S(1)}, u32[]{:S(2)}, u32[]{:S(2)}) collective-permute-start(bf16[4,3712]{1,0:T(4,128)(2,1)S(1)} %get-tuple-element.56), channel_id=1, source_target_pairs={{0,8},{1,9},{2,10},{3,11},{4,12},{5,13},{6,14},{7,15},{8,0},{9,1},... | collective-permute-start | bytes 89096 | tf_op jit(solution)/shard_map/ppermute | solution.py:187
  55.3 4.1 %collective-permute-start.14 = (bf16[2,3712]{1,0:T(2,128)(2,1)S(1)}, bf16[2,3712]{1,0:T(2,128)(2,1)S(1)}, u32[]{:S(2)}, u32[]{:S(2)}) collective-permute-start(bf16[2,3712]{1,0:T(2,128)(2,1)S(1)} %get-tuple-element.68), channel_id=1, source_target_pairs={{0,16},{16,0},{1,17},{17,1},{2,18},{18,2},{3,19},{19,3},{4,20},{20... | collective-permute-start | bytes 44552 | tf_op jit(solution)/shard_map/ppermute | solution.py:186
  57.5 3.8 %collective-permute-start.9 = (bf16[2,3712]{1,0:T(2,128)(2,1)S(1)}, bf16[2,3712]{1,0:T(2,128)(2,1)S(1)}, u32[]{:S(2)}, u32[]{:S(2)}) collective-permute-start(bf16[2,3712]{1,0:T(2,128)(2,1)S(1)} %get-tuple-element.58), channel_id=1, source_target_pairs={{0,16},{16,0},{1,17},{17,1},{2,18},{18,2},{3,19},{19,3},{4,20},{20... | collective-permute-start | bytes 44552 | tf_op jit(solution)/shard_map/ppermute | solution.py:186

commit v6 on v4

--- a/solution.py
+++ b/solution.py
@@ -19,26 +19,35 @@
     return pl.CostEstimate(flops=flops, bytes_accessed=moved, transcendentals=0)
 
 
-def load_kernel(start, share, source, *rest):
-    piece, token, sem = rest[-3:]
-    at = pl.multiple_of(lax.axis_index("groups") * share + start, 16)
-    copy = pltpu.make_async_copy(source.at[pl.ds(at, piece.shape[0])], piece, sem)
-    copy.start()
+def load_kernel(starts, share, *refs):
+    count = len(starts)
+    sources, pieces, token, sems = refs[:count], refs[-count - 2 : -2], refs[-2], refs[-1]
+    first = lax.axis_index("groups") * share
+    copies = [
+        pltpu.make_async_copy(
+            source.at[pl.ds(pl.multiple_of(first + start, 16), piece.shape[0])], piece, sems.at[at]
+        )
+        for at, (source, start, piece) in enumerate(zip(sources, starts, pieces))
+    ]
+    for copy in copies:
+        copy.start()
     token[...] = jnp.zeros_like(token)
-    copy.wait()
-
-
-def load(source, after, start, rows, share):
-    shape = (rows, source.shape[1])
-    return pl.pallas_call(
-        functools.partial(load_kernel, start, share),
-        out_shape=(pltpu.VMEM(shape, source.dtype), pltpu.VMEM((8, 128), jnp.float32)),
-        in_specs=[HBM] + [ANY] * len(after),
-        out_specs=(VMEM, VMEM),
-        scratch_shapes=[pltpu.SemaphoreType.DMA],
+    for copy in copies:
+        copy.wait()
+
+
+def load(wanted, after, share):
+    pieces = tuple(pltpu.VMEM((rows, source.shape[1]), source.dtype) for source, _, rows in wanted)
+    moved = sum(2 * rows * source.shape[1] for source, _, rows in wanted)
+    return pl.pallas_call(
+        functools.partial(load_kernel, [start for _, start, _ in wanted], share),
+        out_shape=(*pieces, pltpu.VMEM((8, 128), jnp.float32)),
+        in_specs=[HBM] * len(wanted) + [ANY] * len(after),
+        out_specs=(VMEM,) * (len(wanted) + 1),
+        scratch_shapes=[pltpu.SemaphoreType.DMA((len(wanted),))],
         compiler_params=pltpu.CompilerParams(vmem_limit_bytes=1 * MIB),
-        cost_estimate=cost(0, 2 * rows * source.shape[1]),
-    )(source, *after)
+        cost_estimate=cost(0, moved),
+    )(*(source for source, _, _ in wanted), *after)
 
 
 def join_kernel(count, *refs):
@@ -78,16 +87,17 @@
 
 
 def hidden_of(mine, theirs, pieces):
-    rows, width = pieces[0].shape
+    width = mine.shape[1]
+    rows = sum(piece.shape[0] for piece in pieces[::2])
     count = mine.shape[0] + theirs.shape[0]
     return pl.pallas_call(
         hidden_kernel,
-        out_shape=(pltpu.VMEM((count, rows), mine.dtype),) * BLOCKS,
+        out_shape=tuple(pltpu.VMEM((count, piece.shape[0]), mine.dtype) for piece in pieces[::2]),
         in_specs=[VMEM] * (2 + 2 * BLOCKS),
         out_specs=(VMEM,) * BLOCKS,
         scratch_shapes=[pltpu.VMEM((count, width), mine.dtype)],
         compiler_params=pltpu.CompilerParams(vmem_limit_bytes=12 * MIB),
-        cost_estimate=cost(4 * BLOCKS * count * rows * width, 4 * BLOCKS * rows * width),
+        cost_estimate=cost(4 * count * rows * width, 4 * rows * width),
     )(*(pltpu.with_memory_space_constraint(one, pltpu.VMEM) for one in (mine, theirs, *pieces)))
 
 
@@ -104,21 +114,22 @@
 
 def down_of(hidden, pieces, start, columns):
     half = hidden[0].shape[0] // 2
-    rows = pieces[0].shape[0]
+    rows = sum(piece.shape[0] for piece in pieces)
     return pl.pallas_call(
         functools.partial(down_kernel, start),
         out_shape=(pltpu.VMEM((half, columns), jnp.float32), pltpu.VMEM((half, columns), jnp.bfloat16)),
         in_specs=[VMEM] * (2 * BLOCKS),
         out_specs=(VMEM, VMEM),
         compiler_params=pltpu.CompilerParams(vmem_limit_bytes=4 * MIB),
-        cost_estimate=cost(4 * BLOCKS * half * rows * columns, 2 * BLOCKS * rows * columns),
+        cost_estimate=cost(4 * half * rows * columns, 2 * rows * columns),
     )(*(pltpu.with_memory_space_constraint(one, pltpu.VMEM) for one in (*hidden, *pieces)))
 
 
 def fold_kernel(keep, came, kept, send):
+    total = keep[...] + came[...].astype(jnp.float32)
     rows = kept.shape[0]
-    kept[...] = keep[:rows, :] + came[:rows, :].astype(jnp.float32)
-    send[...] = (keep[rows:, :] + came[rows:, :].astype(jnp.float32)).astype(send.dtype)
+    kept[...] = total[:rows]
+    send[...] = total[rows:].astype(send.dtype)
 
 
 def fold(keep, came):
@@ -128,7 +139,7 @@
         out_shape=(pltpu.VMEM((rows, columns), jnp.float32), pltpu.VMEM((rows, columns), jnp.bfloat16)),
         in_specs=[VMEM, VMEM],
         out_specs=(VMEM, VMEM),
-        compiler_params=pltpu.CompilerParams(vmem_limit_bytes=2 * MIB),
+        compiler_params=pltpu.CompilerParams(vmem_limit_bytes=4 * MIB),
         cost_estimate=cost(0, 8 * keep.size),
     )(keep, came)
 
@@ -158,10 +169,9 @@
     )(counts, *flat)
 
 
-def exchange(array, mask, count):
-    if mask == 0:
-        return lax.ppermute(array, "groups", [(0, 1), (1, 0)])
-    return lax.ppermute(array, "tensor", [(i, i ^ mask) for i in range(count)])
+def exchange(array, masks, count):
+    pairs = [(i, i ^ masks[i % 2]) for i in range(2 * count)]
+    return lax.ppermute(array, ("groups", "tensor"), pairs)
 
 
 def masked(terms, own, valid_counts):
@@ -169,27 +179,14 @@
     return jnp.where(keep, terms, 0.0).astype(jnp.bfloat16)
 
 
-def reduced(keep, send, masks, count):
-    for at, mask in enumerate(masks):
-        total = keep + exchange(send, mask, count).astype(jnp.float32)
-        if at + 1 == len(masks):
-            return total
-        rows = total.shape[0] // 2
-        keep, send = total[:rows], total[rows:].astype(jnp.bfloat16)
-
-
 def plain(count, masks, tokens, gate_weight, up_weight, down_weight, valid_counts):
     own = tokens.shape[0]
-    gathered = tokens
-    for mask in reversed(masks):
-        gathered = jnp.concatenate([gathered, exchange(gathered, mask, count)], axis=0)
+    gathered = lax.all_gather(tokens, "tensor", axis=0, tiled=True)
     gate_value = jnp.dot(gathered, gate_weight, preferred_element_type=jnp.float32)
     up_value = jnp.dot(gathered, up_weight, preferred_element_type=jnp.float32)
     hidden = (jax.nn.silu(gate_value) * up_value).astype(jnp.bfloat16)
     terms = jnp.dot(hidden, down_weight, preferred_element_type=jnp.float32)
-    half = terms.shape[0] // 2
-    total = reduced(terms[:half], terms[half:].astype(jnp.bfloat16), masks, count)
-    return masked(total, own, valid_counts)
+    return masked(lax.psum_scatter(terms, "tensor", scatter_dimension=0, tiled=True), own, valid_counts)
 
 
 def per_device(count, masks, tokens, gate_weight, up_weight, down_weight, valid_counts):
@@ -198,25 +195,31 @@
         pltpu.with_memory_space_constraint(one, pltpu.HBM) for one in (gate_weight.T, up_weight.T, down_weight)
     )
     share = gate.shape[0] // 2
-    rows = share // BLOCKS
-    wanted = [[(gate, 0)], [(up, 0)], [(gate, rows)], [(up, rows), (down, 0)], [(down, rows)]]
-    masks = [*masks, 0]
-    mine, after, pieces = tokens, (), []
+    first = second = share // BLOCKS
+    wanted = [
+        [(gate, 0, first)],
+        [(up, 0, first)],
+        [(gate, first, second)],
+        [(up, first, second), (down, 0, first)],
+        [(down, first, second)],
+    ]
+    core, y, near, far = masks
+    x = count
+    masks = [(core, core), (y, x), (x, y), (near, near), (far, far)]
+    mine, after, loaded = tokens, (), []
     for step, (mask, sources) in enumerate(zip(reversed(masks), wanted)):
         theirs = exchange(mine, mask, count)
-        tokens_of = []
-        for source, start in sources:
-            piece, token = load(source, after, start, rows, share)
-            pieces.append(piece)
-            tokens_of.append(token)
+        *pieces, end = load(sources, after, share)
+        loaded += pieces
         if step + 1 < len(masks):
-            mine = join([mine, theirs], tokens_of)
+            mine = join([mine, theirs], [end])
             after = (mine,)
-    hidden = hidden_of(mine, theirs, pieces[: 2 * BLOCKS])
+    g0, u0, g1, u1, d0, d1 = loaded
+    hidden = hidden_of(mine, theirs, [g0, u0, g1, u1])
     columns = width // CHUNKS
     parts = []
     for chunk in range(CHUNKS):
-        keep, send = down_of(hidden, pieces[2 * BLOCKS :], chunk * columns, columns)
+        keep, send = down_of(hidden, (d0, d1), chunk * columns, columns)
         for mask in masks[:-1]:
             keep, send = fold(keep, exchange(send, mask, count))
         parts.append((keep, exchange(send, masks[-1], count)))

time: 61.3 us -> 59.1 us (0.964)
  waiting for transfers between devices: 9.5 us -> 7.37 us
  Pallas kernels: 29.7 us -> 28.7 us
  starting transfers between devices: 21 us -> 22 us
    ppermute x15, waiting for transfers between devices: 9.5 us -> 7.37 us  [exchange(): return lax.ppermute(array, ('groups', 'tensor'), pairs)]
    pallas_call x7 -> x6, Pallas kernels: 26.3 us -> 25.3 us  [the longest x5 17.4 us: load(): pl.pallas_call(functools.partial(load_kernel, [start for _, start, _ in w...]
    ppermute x15, starting transfers between devices: 21 us -> 22 us  [exchange(): return lax.ppermute(array, ('groups', 'tensor'), pairs)]
  transfers between devices with their start and end apart: 15 -> 15, of which waited for: 8 -> 7; matrix products, arithmetic and copies ran while one was open for 0% -> 0% of each run, Pallas kernels for 33% -> 32%
where the time goes in v6:
time: 59.1 us; the launch traced here: 58.8 us
  Pallas kernels  28.7 us (49%)
  starting transfers between devices  22 us (37%)
  waiting for transfers between devices  7.37 us (12%)
  between operations  0.83 us (1%)
    ppermute x15, starting transfers between devices, exchange(): return lax.ppermute(array, ('groups', 'tensor'), pairs)  22 us
    pallas_call x5, Pallas kernels, load(): pl.pallas_call(functools.partial(load_kernel, [start for _, start, _ in w...  17.4 us
    pallas_call x1, Pallas kernels, hidden_of(): pl.pallas_call(hidden_kernel, out_shape=tuple((pltpu.VMEM((count, piece.s...  7.89 us
    ppermute x15, waiting for transfers between devices, exchange(): return lax.ppermute(array, ('groups', 'tensor'), pairs)  7.37 us
    pallas_call x2, Pallas kernels, down_of(): pl.pallas_call(functools.partial(down_kernel, start), out_shape=(pltpu.VM...  2.41 us
  transfers between devices with their start and end apart: 15, of which 7 were waited for; matrix products, arithmetic and copies ran while one was open for 0% of the time, Pallas kernels for 32%

profile of v6, /device:TPU:0, one launch (start us, length us, event | category | flops | bytes accessed | tf_op | source)
XLA Modules:
  0.0 58.8 jit_solution(8371604464845125662)
XLA Ops:
  0.0 4.0 %collective-permute-start = (bf16[2,7424]{1,0:T(2,128)(2,1)}, bf16[2,7424]{1,0:T(2,128)(2,1)S(1)}, u32[]{:S(2)}, u32[]{:S(2)}) collective-permute-start(bf16[2,7424]{1,0:T(2,128)(2,1)} %refs_0_.2), channel_id=1, source_target_pairs={{0,8},{1,9},{2,10},{3,11},{4,12},{5,13},{6,14},{7,15},{8,0},{9,1},... | collective-permute-start | bytes 89096 | tf_op jit(solution)/shard_map/ppermute | solution.py:174
  4.0 3.0 %shard_map.55 = (bf16[464,7424]{1,0:T(8,128)(2,1)S(1)}, f32[8,128]{1,0:T(8,128)S(1)}) custom-call(bf16[1856,7424]{1,0:T(8,128)(2,1)} %bitcast.2), custom_call_target="tpu_custom_call" | custom-call | bytes 6889472 | tf_op jit(solution)/shard_map/pallas_call | solution.py:42
  7.0 0.0 collective-permute-done.refs_1_
  7.1 1.6 %collective-permute-start.1 = (bf16[4,7424]{1,0:T(4,128)(2,1)S(1)}, bf16[4,7424]{1,0:T(4,128)(2,1)S(1)}, u32[]{:S(2)}, u32[]{:S(2)}) collective-permute-start(bf16[4,7424]{1,0:T(4,128)(2,1)S(1)} %shard_map.56.refs_1_.refs_0_), channel_id=1, source_target_pairs={{0,4},{1,5},{2,6},{3,7},{4,0},{5,1},{6,2},{7,3},{8,12},{9,13},{10,... | collective-permute-start | bytes 178184 | tf_op jit(solution)/shard_map/ppermute | solution.py:174
  8.7 3.0 %shard_map.57 = (bf16[464,7424]{1,0:T(8,128)(2,1)S(1)}, f32[8,128]{1,0:T(8,128)S(1)}) custom-call(bf16[1856,7424]{1,0:T(8,128)(2,1)} %bitcast.4, bf16[4,7424]{1,0:T(4,128)(2,1)S(1)} %shard_map.56.refs_1_.refs_0_), custom_call_target="tpu_custom_call" | custom-call | bytes 6889472 | tf_op jit(solution)/shard_map/pallas_call | solution.py:42
  11.7 1.6 %collective-permute-start.2 = (bf16[8,7424]{1,0:T(8,128)(2,1)S(1)}, bf16[8,7424]{1,0:T(8,128)(2,1)S(1)}, u32[]{:S(2)}, u32[]{:S(2)}) collective-permute-start(bf16[8,7424]{1,0:T(8,128)(2,1)S(1)} %shard_map.58.refs_1_.refs_0_), channel_id=1, source_target_pairs={{0,16},{1,3},{2,18},{3,1},{4,20},{5,7},{6,22},{7,5},{8,24},{9,11},... | collective-permute-start | bytes 356360 | tf_op jit(solution)/shard_map/ppermute | solution.py:174
  13.3 3.0 %shard_map.59 = (bf16[464,7424]{1,0:T(8,128)(2,1)S(1)}, f32[8,128]{1,0:T(8,128)S(1)}) custom-call(bf16[1856,7424]{1,0:T(8,128)(2,1)} %bitcast.3, bf16[8,7424]{1,0:T(8,128)(2,1)S(1)} %shard_map.58.refs_1_.refs_0_), custom_call_target="tpu_custom_call" | custom-call | bytes 6889472 | tf_op jit(solution)/shard_map/pallas_call | solution.py:42
  16.3 0.4 collective-permute-done.2.refs_1_
  16.7 1.6 %collective-permute-start.3 = (bf16[16,7424]{1,0:T(8,128)(2,1)S(1)}, bf16[16,7424]{1,0:T(8,128)(2,1)S(1)}, u32[]{:S(2)}, u32[]{:S(2)}) collective-permute-start(bf16[16,7424]{1,0:T(8,128)(2,1)S(1)} %shard_map.60.refs_2_.refs_0_), channel_id=1, source_target_pairs={{0,2},{1,17},{2,0},{3,19},{4,6},{5,21},{6,4},{7,23},{8,10},{9,25},... | collective-permute-start | bytes 712712 | tf_op jit(solution)/shard_map/ppermute | solution.py:174
  18.2 4.9 %shard_map.61 = (bf16[464,7424]{1,0:T(8,128)(2,1)S(1)}, bf16[464,7424]{1,0:T(8,128)(2,1)S(1)}, f32[8,128]{1,0:T(8,128)S(1)}) custom-call(bf16[1856,7424]{1,0:T(8,128)(2,1)} %bitcast.5, bf16[1856,7424]{1,0:T(8,128)(2,1)} %refs_0_.3, bf16[16,7424]{1,0:T(8,128)(2,1)S(1)} %shard_map.60.refs_2_.refs_0_), custom_call_target="tpu_custom_call" | custom-call | bytes 13778944 | tf_op jit(solution)/shard_map/pallas_call | solution.py:42
  23.2 0.1 collective-permute-start.4
  23.3 3.6 %shard_map.64 = (bf16[464,7424]{1,0:T(8,128)(2,1)S(1)}, f32[8,128]{1,0:T(8,128)}) custom-call(bf16[1856,7424]{1,0:T(8,128)(2,1)} %refs_0_.3, bf16[32,7424]{1,0:T(8,128)(2,1)S(1)} %shard_map.62.mine.refs_1_), custom_call_target="tpu_custom_call" | custom-call | bytes 6889472 | tf_op jit(solution)/shard_map/pallas_call | solution.py:42
  26.9 7.9 %shard_map.63 = (bf16[64,464]{1,0:T(8,128)(2,1)S(1)}, bf16[64,464]{1,0:T(8,128)(2,1)S(1)}) custom-call(bf16[32,7424]{1,0:T(8,128)(2,1)S(1)} %shard_map.62.mine.refs_1_, bf16[32,7424]{1,0:T(8,128)(2,1)S(1)} %collective-permute-done.4.theirs, bf16[464,7424]{1,0:T(8,128)(2,1)S(1)} %get-tuple-element.41.refs_0_, ...), custom_call_target="tpu_custom_call" | custom-call | flops 1763704832 | bytes 27557888 | tf_op jit(solution)/shard_map/pallas_call | solution.py:93
  34.8 1.2 %shard_map.70 = (f32[32,3712]{1,0:T(8,128)S(1)}, bf16[32,3712]{1,0:T(8,128)(2,1)S(1)}) custom-call(bf16[64,464]{1,0:T(8,128)(2,1)S(1)} %get-tuple-element.45.refs_0_, bf16[64,464]{1,0:T(8,128)(2,1)S(1)} %get-tuple-element.46.refs_1_, bf16[464,7424]{1,0:T(8,128)(2,1)S(1)} %get-tuple-element.47.refs_2_, bf16[464,7424]{1,0:T(8,128)(2,1)S(1)} %get-tuple-element.48.refs_3_), custom_call_target="tpu_custom_call" | custom-call | flops 440926208 | bytes 6889472 | tf_op jit(solution)/shard_map/pallas_call | solution.py:118
  36.0 0.6 collective-permute-start.10
  36.5 1.2 %shard_map.65 = (f32[32,3712]{1,0:T(8,128)S(1)}, bf16[32,3712]{1,0:T(8,128)(2,1)S(1)}) custom-call(bf16[64,464]{1,0:T(8,128)(2,1)S(1)} %get-tuple-element.45.refs_0_, bf16[64,464]{1,0:T(8,128)(2,1)S(1)} %get-tuple-element.46.refs_1_, bf16[464,7424]{1,0:T(8,128)(2,1)S(1)} %get-tuple-element.47.refs_2_, bf16[464,7424]{1,0:T(8,128)(2,1)S(1)} %get-tuple-element.48.refs_3_), custom_call_target="tpu_custom_call" | custom-call | flops 440926208 | bytes 6889472 | tf_op jit(solution)/shard_map/pallas_call | solution.py:118
  37.8 0.1 collective-permute-start.5
  37.9 1.2 %collective-permute-start.11 = (bf16[16,3712]{1,0:T(8,128)(2,1)S(1)}, bf16[16,3712]{1,0:T(8,128)(2,1)S(1)}, u32[]{:S(2)}, u32[]{:S(2)}) collective-permute-start(bf16[16,3712]{1,0:T(8,128)(2,1)S(1)} %get-tuple-element.62), channel_id=1, source_target_pairs={{0,2},{1,17},{2,0},{3,19},{4,6},{5,21},{6,4},{7,23},{8,10},{9,25},... | collective-permute-start | bytes 356360 | tf_op jit(solution)/shard_map/ppermute | solution.py:174
  39.1 0.2 collective-permute-done.5.came
  39.4 1.2 %collective-permute-start.6 = (bf16[16,3712]{1,0:T(8,128)(2,1)S(1)}, bf16[16,3712]{1,0:T(8,128)(2,1)S(1)}, u32[]{:S(2)}, u32[]{:S(2)}) collective-permute-start(bf16[16,3712]{1,0:T(8,128)(2,1)S(1)} %get-tuple-element.52), channel_id=1, source_target_pairs={{0,2},{1,17},{2,0},{3,19},{4,6},{5,21},{6,4},{7,23},{8,10},{9,25},... | collective-permute-start | bytes 356360 | tf_op jit(solution)/shard_map/ppermute | solution.py:174
  40.6 2.2 %collective-permute-done.11.came = bf16[16,3712]{1,0:T(8,128)(2,1)S(1)} collective-permute-done((bf16[16,3712]{1,0:T(8,128)(2,1)S(1)}, bf16[16,3712]{1,0:T(8,128)(2,1)S(1)}, u32[]{:S(2)}, u32[]{:S(2)}) %collective-permute-start.11) | collective-permute-done | bytes 118816 | tf_op jit(solution)/shard_map/ppermute | solution.py:174
  42.8 1.6 %collective-permute-start.12 = (bf16[8,3712]{1,0:T(8,128)(2,1)S(1)}, bf16[8,3712]{1,0:T(8,128)(2,1)S(1)}, u32[]{:S(2)}, u32[]{:S(2)}) collective-permute-start(bf16[8,3712]{1,0:T(8,128)(2,1)S(1)} %get-tuple-element.64), channel_id=1, source_target_pairs={{0,16},{1,3},{2,18},{3,1},{4,20},{5,7},{6,22},{7,5},{8,24},{9,11},... | collective-permute-start | bytes 178184 | tf_op jit(solution)/shard_map/ppermute | solution.py:174
  44.4 1.4 %collective-permute-start.7 = (bf16[8,3712]{1,0:T(8,128)(2,1)S(1)}, bf16[8,3712]{1,0:T(8,128)(2,1)S(1)}, u32[]{:S(2)}, u32[]{:S(2)}) collective-permute-start(bf16[8,3712]{1,0:T(8,128)(2,1)S(1)} %get-tuple-element.54), channel_id=1, source_target_pairs={{0,16},{1,3},{2,18},{3,1},{4,20},{5,7},{6,22},{7,5},{8,24},{9,11},... | collective-permute-start | bytes 178184 | tf_op jit(solution)/shard_map/ppermute | solution.py:174
  45.9 1.2 %collective-permute-done.12.came = bf16[8,3712]{1,0:T(8,128)(2,1)S(1)} collective-permute-done((bf16[8,3712]{1,0:T(8,128)(2,1)S(1)}, bf16[8,3712]{1,0:T(8,128)(2,1)S(1)}, u32[]{:S(2)}, u32[]{:S(2)}) %collective-permute-start.12) | collective-permute-done | bytes 59424 | tf_op jit(solution)/shard_map/ppermute | solution.py:174
  47.1 1.3 %collective-permute-start.13 = (bf16[4,3712]{1,0:T(4,128)(2,1)S(1)}, bf16[4,3712]{1,0:T(4,128)(2,1)S(1)}, u32[]{:S(2)}, u32[]{:S(2)}) collective-permute-start(bf16[4,3712]{1,0:T(4,128)(2,1)S(1)} %get-tuple-element.66), channel_id=1, source_target_pairs={{0,4},{1,5},{2,6},{3,7},{4,0},{5,1},{6,2},{7,3},{8,12},{9,13},{10,... | collective-permute-start | bytes 89096 | tf_op jit(solution)/shard_map/ppermute | solution.py:174
  48.4 0.3 collective-permute-done.7.came
  48.7 1.3 %collective-permute-start.8 = (bf16[4,3712]{1,0:T(4,128)(2,1)S(1)}, bf16[4,3712]{1,0:T(4,128)(2,1)S(1)}, u32[]{:S(2)}, u32[]{:S(2)}) collective-permute-start(bf16[4,3712]{1,0:T(4,128)(2,1)S(1)} %get-tuple-element.56), channel_id=1, source_target_pairs={{0,4},{1,5},{2,6},{3,7},{4,0},{5,1},{6,2},{7,3},{8,12},{9,13},{10,... | collective-permute-start | bytes 89096 | tf_op jit(solution)/shard_map/ppermute | solution.py:174
  50.0 1.1 %collective-permute-done.13.came = bf16[4,3712]{1,0:T(4,128)(2,1)S(1)} collective-permute-done((bf16[4,3712]{1,0:T(4,128)(2,1)S(1)}, bf16[4,3712]{1,0:T(4,128)(2,1)S(1)}, u32[]{:S(2)}, u32[]{:S(2)}) %collective-permute-start.13) | collective-permute-done | bytes 29728 | tf_op jit(solution)/shard_map/ppermute | solution.py:174
  51.1 2.4 %collective-permute-start.14 = (bf16[2,3712]{1,0:T(2,128)(2,1)S(1)}, bf16[2,3712]{1,0:T(2,128)(2,1)S(1)}, u32[]{:S(2)}, u32[]{:S(2)}) collective-permute-start(bf16[2,3712]{1,0:T(2,128)(2,1)S(1)} %get-tuple-element.68), channel_id=1, source_target_pairs={{0,8},{1,9},{2,10},{3,11},{4,12},{5,13},{6,14},{7,15},{8,0},{9,1},... | collective-permute-start | bytes 44552 | tf_op jit(solution)/shard_map/ppermute | solution.py:174
  53.5 2.1 %collective-permute-start.9 = (bf16[2,3712]{1,0:T(2,128)(2,1)S(1)}, bf16[2,3712]{1,0:T(2,128)(2,1)S(1)}, u32[]{:S(2)}, u32[]{:S(2)}) collective-permute-start(bf16[2,3712]{1,0:T(2,128)(2,1)S(1)} %get-tuple-element.58), channel_id=1, source_target_pairs={{0,8},{1,9},{2,10},{3,11},{4,12},{5,13},{6,14},{7,15},{8,0},{9,1},... | collective-permute-start | bytes 44552 | tf_op jit(solution)/shard_map/ppermute | solution.py:174
  56.2 1.9 %collective-permute-done.9.refs_1_ = bf16[2,3712]{1,0:T(2,128)(2,1)S(1)} collective-permute-done((bf16[2,3712]{1,0:T(2,128)(2,1)S(1)}, bf16[2,3712]{1,0:T(2,128)(2,1)S(1)}, u32[]{:S(2)}, u32[]{:S(2)}) %collective-permute-start.9) | collective-permute-done | bytes 14880 | tf_op jit(solution)/shard_map/ppermute | solution.py:174
  58.2 0.7 %shard_map.75 = bf16[2,7424]{1,0:T(2,128)(2,1)} custom-call(s32[1]{0:T(128)S(6)} %copy.6.counts, f32[2,3712]{1,0:T(2,128)S(1)} %get-tuple-element.57.refs_0_, bf16[2,3712]{1,0:T(2,128)(2,1)S(1)} %collective-permute-done.9.refs_1_, f32[2,3712]{1,0:T(2,128)S(1)} %get-tuple-element.67.refs_2_, bf16[2,3712]{1,0:T(2,128)(2,1)S(1)} %collective-permute-done.14.refs_3_), custom_call_target="tpu_custom_call" | custom-call | bytes 59392 | tf_op jit(solution)/shard_map/pallas_call | solution.py:162
  (21 shorter events, 0.3 us)
Async XLA Ops:
  0.0 7.0 %collective-permute-start = (bf16[2,7424]{1,0:T(2,128)(2,1)}, bf16[2,7424]{1,0:T(2,128)(2,1)S(1)}, u32[]{:S(2)}, u32[]{:S(2)}) collective-permute-start(bf16[2,7424]{1,0:T(2,128)(2,1)} %refs_0_.2), channel_id=1, source_target_pairs={{0,8},{1,9},{2,10},{3,11},{4,12},{5,13},{6,14},{7,15},{8,0},{9,1},... | collective-permute-start | bytes 89096 | tf_op jit(solution)/shard_map/ppermute | solution.py:174
  4.0 3.0 %copy-start = (bf16[2,7424]{1,0:T(2,128)(2,1)S(1)}, bf16[2,7424]{1,0:T(2,128)(2,1)}, u32[]{:S(2)}) copy-start(bf16[2,7424]{1,0:T(2,128)(2,1)} %refs_0_.2) | copy-start | bytes 89092
  7.1 4.6 %collective-permute-start.1 = (bf16[4,7424]{1,0:T(4,128)(2,1)S(1)}, bf16[4,7424]{1,0:T(4,128)(2,1)S(1)}, u32[]{:S(2)}, u32[]{:S(2)}) collective-permute-start(bf16[4,7424]{1,0:T(4,128)(2,1)S(1)} %shard_map.56.refs_1_.refs_0_), channel_id=1, source_target_pairs={{0,4},{1,5},{2,6},{3,7},{4,0},{5,1},{6,2},{7,3},{8,12},{9,13},{10,... | collective-permute-start | bytes 178184 | tf_op jit(solution)/shard_map/ppermute | solution.py:174
  11.7 4.9 %collective-permute-start.2 = (bf16[8,7424]{1,0:T(8,128)(2,1)S(1)}, bf16[8,7424]{1,0:T(8,128)(2,1)S(1)}, u32[]{:S(2)}, u32[]{:S(2)}) collective-permute-start(bf16[8,7424]{1,0:T(8,128)(2,1)S(1)} %shard_map.58.refs_1_.refs_0_), channel_id=1, source_target_pairs={{0,16},{1,3},{2,18},{3,1},{4,20},{5,7},{6,22},{7,5},{8,24},{9,11},... | collective-permute-start | bytes 356360 | tf_op jit(solution)/shard_map/ppermute | solution.py:174
  16.7 6.5 %collective-permute-start.3 = (bf16[16,7424]{1,0:T(8,128)(2,1)S(1)}, bf16[16,7424]{1,0:T(8,128)(2,1)S(1)}, u32[]{:S(2)}, u32[]{:S(2)}) collective-permute-start(bf16[16,7424]{1,0:T(8,128)(2,1)S(1)} %shard_map.60.refs_2_.refs_0_), channel_id=1, source_target_pairs={{0,2},{1,17},{2,0},{3,19},{4,6},{5,21},{6,4},{7,23},{8,10},{9,25},... | collective-permute-start | bytes 712712 | tf_op jit(solution)/shard_map/ppermute | solution.py:174
  23.2 3.7 %collective-permute-start.4 = (bf16[32,7424]{1,0:T(8,128)(2,1)S(1)}, bf16[32,7424]{1,0:T(8,128)(2,1)S(1)}, u32[]{:S(2)}, u32[]{:S(2)}) collective-permute-start(bf16[32,7424]{1,0:T(8,128)(2,1)S(1)} %shard_map.62.mine.refs_1_), channel_id=1, source_target_pairs={{0,1},{1,0},{2,3},{3,2},{4,5},{5,4},{6,7},{7,6},{8,9},{9,8},{10,11... | collective-permute-start | bytes 1425416 | tf_op jit(solution)/shard_map/ppermute | solution.py:174
  36.0 1.9 %collective-permute-start.10 = (bf16[32,3712]{1,0:T(8,128)(2,1)S(1)}, bf16[32,3712]{1,0:T(8,128)(2,1)S(1)}, u32[]{:S(2)}, u32[]{:S(2)}) collective-permute-start(bf16[32,3712]{1,0:T(8,128)(2,1)S(1)} %get-tuple-element.60), channel_id=1, source_target_pairs={{0,1},{1,0},{2,3},{3,2},{4,5},{5,4},{6,7},{7,6},{8,9},{9,8},{10,11... | collective-permute-start | bytes 712712 | tf_op jit(solution)/shard_map/ppermute | solution.py:174
  37.8 1.6 %collective-permute-start.5 = (bf16[32,3712]{1,0:T(8,128)(2,1)S(1)}, bf16[32,3712]{1,0:T(8,128)(2,1)S(1)}, u32[]{:S(2)}, u32[]{:S(2)}) collective-permute-start(bf16[32,3712]{1,0:T(8,128)(2,1)S(1)} %get-tuple-element.50), channel_id=1, source_target_pairs={{0,1},{1,0},{2,3},{3,2},{4,5},{5,4},{6,7},{7,6},{8,9},{9,8},{10,11... | collective-permute-start | bytes 712712 | tf_op jit(solution)/shard_map/ppermute | solution.py:174
  37.9 4.9 %collective-permute-start.11 = (bf16[16,3712]{1,0:T(8,128)(2,1)S(1)}, bf16[16,3712]{1,0:T(8,128)(2,1)S(1)}, u32[]{:S(2)}, u32[]{:S(2)}) collective-permute-start(bf16[16,3712]{1,0:T(8,128)(2,1)S(1)} %get-tuple-element.62), channel_id=1, source_target_pairs={{0,2},{1,17},{2,0},{3,19},{4,6},{5,21},{6,4},{7,23},{8,10},{9,25},... | collective-permute-start | bytes 356360 | tf_op jit(solution)/shard_map/ppermute | solution.py:174
  39.4 5.0 %collective-permute-start.6 = (bf16[16,3712]{1,0:T(8,128)(2,1)S(1)}, bf16[16,3712]{1,0:T(8,128)(2,1)S(1)}, u32[]{:S(2)}, u32[]{:S(2)}) collective-permute-start(bf16[16,3712]{1,0:T(8,128)(2,1)S(1)} %get-tuple-element.52), channel_id=1, source_target_pairs={{0,2},{1,17},{2,0},{3,19},{4,6},{5,21},{6,4},{7,23},{8,10},{9,25},... | collective-permute-start | bytes 356360 | tf_op jit(solution)/shard_map/ppermute | solution.py:174
  42.8 4.3 %collective-permute-start.12 = (bf16[8,3712]{1,0:T(8,128)(2,1)S(1)}, bf16[8,3712]{1,0:T(8,128)(2,1)S(1)}, u32[]{:S(2)}, u32[]{:S(2)}) collective-permute-start(bf16[8,3712]{1,0:T(8,128)(2,1)S(1)} %get-tuple-element.64), channel_id=1, source_target_pairs={{0,16},{1,3},{2,18},{3,1},{4,20},{5,7},{6,22},{7,5},{8,24},{9,11},... | collective-permute-start | bytes 178184 | tf_op jit(solution)/shard_map/ppermute | solution.py:174
  44.4 4.3 %collective-permute-start.7 = (bf16[8,3712]{1,0:T(8,128)(2,1)S(1)}, bf16[8,3712]{1,0:T(8,128)(2,1)S(1)}, u32[]{:S(2)}, u32[]{:S(2)}) collective-permute-start(bf16[8,3712]{1,0:T(8,128)(2,1)S(1)} %get-tuple-element.54), channel_id=1, source_target_pairs={{0,16},{1,3},{2,18},{3,1},{4,20},{5,7},{6,22},{7,5},{8,24},{9,11},... | collective-permute-start | bytes 178184 | tf_op jit(solution)/shard_map/ppermute | solution.py:174
  47.1 3.9 %collective-permute-start.13 = (bf16[4,3712]{1,0:T(4,128)(2,1)S(1)}, bf16[4,3712]{1,0:T(4,128)(2,1)S(1)}, u32[]{:S(2)}, u32[]{:S(2)}) collective-permute-start(bf16[4,3712]{1,0:T(4,128)(2,1)S(1)} %get-tuple-element.66), channel_id=1, source_target_pairs={{0,4},{1,5},{2,6},{3,7},{4,0},{5,1},{6,2},{7,3},{8,12},{9,13},{10,... | collective-permute-start | bytes 89096 | tf_op jit(solution)/shard_map/ppermute | solution.py:174
  48.7 4.8 %collective-permute-start.8 = (bf16[4,3712]{1,0:T(4,128)(2,1)S(1)}, bf16[4,3712]{1,0:T(4,128)(2,1)S(1)}, u32[]{:S(2)}, u32[]{:S(2)}) collective-permute-start(bf16[4,3712]{1,0:T(4,128)(2,1)S(1)} %get-tuple-element.56), channel_id=1, source_target_pairs={{0,4},{1,5},{2,6},{3,7},{4,0},{5,1},{6,2},{7,3},{8,12},{9,13},{10,... | collective-permute-start | bytes 89096 | tf_op jit(solution)/shard_map/ppermute | solution.py:174
  51.1 5.1 %collective-permute-start.14 = (bf16[2,3712]{1,0:T(2,128)(2,1)S(1)}, bf16[2,3712]{1,0:T(2,128)(2,1)S(1)}, u32[]{:S(2)}, u32[]{:S(2)}) collective-permute-start(bf16[2,3712]{1,0:T(2,128)(2,1)S(1)} %get-tuple-element.68), channel_id=1, source_target_pairs={{0,8},{1,9},{2,10},{3,11},{4,12},{5,13},{6,14},{7,15},{8,0},{9,1},... | collective-permute-start | bytes 44552 | tf_op jit(solution)/shard_map/ppermute | solution.py:174
  53.5 4.7 %collective-permute-start.9 = (bf16[2,3712]{1,0:T(2,128)(2,1)S(1)}, bf16[2,3712]{1,0:T(2,128)(2,1)S(1)}, u32[]{:S(2)}, u32[]{:S(2)}) collective-permute-start(bf16[2,3712]{1,0:T(2,128)(2,1)S(1)} %get-tuple-element.58), channel_id=1, source_target_pairs={{0,8},{1,9},{2,10},{3,11},{4,12},{5,13},{6,14},{7,15},{8,0},{9,1},... | collective-permute-start | bytes 44552 | tf_op jit(solution)/shard_map/ppermute | solution.py:174

commit v7 on v6

--- a/solution.py
+++ b/solution.py
@@ -13,6 +13,7 @@
 ANY = pl.BlockSpec(memory_space=pl.ANY)
 BLOCKS = 2
 CHUNKS = 2
+APART = 4
 
 
 def cost(flops, moved):
@@ -125,23 +126,29 @@
     )(*(pltpu.with_memory_space_constraint(one, pltpu.VMEM) for one in (*hidden, *pieces)))
 
 
-def fold_kernel(keep, came, kept, send):
-    total = keep[...] + came[...].astype(jnp.float32)
+def fold_kernel(*refs):
+    parts, kept, send = refs[:-2], refs[-2], refs[-1]
     rows = kept.shape[0]
-    kept[...] = total[:rows]
-    send[...] = total[rows:].astype(send.dtype)
-
-
-def fold(keep, came):
-    rows, columns = keep.shape[0] // 2, keep.shape[1]
+    at = 0
+    for keep, came in zip(parts[::2], parts[1::2]):
+        total = keep[...] + came[...].astype(jnp.float32)
+        columns = total.shape[1]
+        kept[:, at : at + columns] = total[:rows]
+        send[:, at : at + columns] = total[rows:].astype(send.dtype)
+        at += columns
+
+
+def fold(*parts):
+    flat = [one for part in parts for one in part]
+    rows, columns = flat[0].shape[0] // 2, sum(one.shape[1] for one in flat[::2])
     return pl.pallas_call(
         fold_kernel,
         out_shape=(pltpu.VMEM((rows, columns), jnp.float32), pltpu.VMEM((rows, columns), jnp.bfloat16)),
-        in_specs=[VMEM, VMEM],
+        in_specs=[VMEM] * len(flat),
         out_specs=(VMEM, VMEM),
         compiler_params=pltpu.CompilerParams(vmem_limit_bytes=4 * MIB),
-        cost_estimate=cost(0, 8 * keep.size),
-    )(keep, came)
+        cost_estimate=cost(0, 16 * rows * columns),
+    )(*flat)
 
 
 def last_kernel(counts, *refs):
@@ -220,9 +227,12 @@
     parts = []
     for chunk in range(CHUNKS):
         keep, send = down_of(hidden, (d0, d1), chunk * columns, columns)
-        for mask in masks[:-1]:
-            keep, send = fold(keep, exchange(send, mask, count))
-        parts.append((keep, exchange(send, masks[-1], count)))
+        for mask in masks[: APART - 1]:
+            keep, send = fold((keep, exchange(send, mask, count)))
+        parts.append((keep, exchange(send, masks[APART - 1], count)))
+    for mask in masks[APART:]:
+        keep, send = fold(*parts)
+        parts = [(keep, exchange(send, mask, count))]
     return last(valid_counts, parts)
 
 

time: 59.1 us -> 58.5 us (0.990)
  starting transfers between devices: 22 us -> 20.6 us
  waiting for transfers between devices: 7.37 us -> 8.22 us
    ppermute x15 -> x14, starting transfers between devices: 22 us -> 20.6 us  [exchange(): return lax.ppermute(array, ('groups', 'tensor'), pairs)]
    ppermute x15 -> x14, waiting for transfers between devices: 7.37 us -> 8.22 us  [exchange(): return lax.ppermute(array, ('groups', 'tensor'), pairs)]
  transfers between devices with their start and end apart: 15 -> 14, of which waited for: 7 -> 8; matrix products, arithmetic and copies ran while one was open for 0% -> 0% of each run, Pallas kernels for 32% -> 32%
where the time goes in v7:
time: 58.5 us; the launch traced here: 58.3 us
  Pallas kernels  28.7 us (49%)
  starting transfers between devices  20.6 us (35%)
  waiting for transfers between devices  8.22 us (14%)
  between operations  0.82 us (1%)
    ppermute x14, starting transfers between devices, exchange(): return lax.ppermute(array, ('groups', 'tensor'), pairs)  20.6 us
    pallas_call x5, Pallas kernels, load(): pl.pallas_call(functools.partial(load_kernel, [start for _, start, _ in w...  17.4 us
    ppermute x14, waiting for transfers between devices, exchange(): return lax.ppermute(array, ('groups', 'tensor'), pairs)  8.22 us
    pallas_call x1, Pallas kernels, hidden_of(): pl.pallas_call(hidden_kernel, out_shape=tuple((pltpu.VMEM((count, piece.s...  7.89 us
    pallas_call x2, Pallas kernels, down_of(): pl.pallas_call(functools.partial(down_kernel, start), out_shape=(pltpu.VM...  2.41 us
  transfers between devices with their start and end apart: 14, of which 8 were waited for; matrix products, arithmetic and copies ran while one was open for 0% of the time, Pallas kernels for 32%

profile of v7, /device:TPU:0, one launch (start us, length us, event | category | flops | bytes accessed | tf_op | source)
XLA Modules:
  0.0 58.3 jit_solution(12299191214594996215)
XLA Ops:
  0.0 4.0 %collective-permute-start = (bf16[2,7424]{1,0:T(2,128)(2,1)}, bf16[2,7424]{1,0:T(2,128)(2,1)S(1)}, u32[]{:S(2)}, u32[]{:S(2)}) collective-permute-start(bf16[2,7424]{1,0:T(2,128)(2,1)} %refs_0_.2), channel_id=1, source_target_pairs={{0,8},{1,9},{2,10},{3,11},{4,12},{5,13},{6,14},{7,15},{8,0},{9,1},... | collective-permute-start | bytes 89096 | tf_op jit(solution)/shard_map/ppermute | solution.py:181
  4.0 3.0 %shard_map.55 = (bf16[464,7424]{1,0:T(8,128)(2,1)S(1)}, f32[8,128]{1,0:T(8,128)S(1)}) custom-call(bf16[1856,7424]{1,0:T(8,128)(2,1)} %bitcast.2), custom_call_target="tpu_custom_call" | custom-call | bytes 6889472 | tf_op jit(solution)/shard_map/pallas_call | solution.py:43
  7.0 0.0 collective-permute-done.refs_1_
  7.1 1.6 %collective-permute-start.1 = (bf16[4,7424]{1,0:T(4,128)(2,1)S(1)}, bf16[4,7424]{1,0:T(4,128)(2,1)S(1)}, u32[]{:S(2)}, u32[]{:S(2)}) collective-permute-start(bf16[4,7424]{1,0:T(4,128)(2,1)S(1)} %shard_map.56.refs_1_.refs_0_), channel_id=1, source_target_pairs={{0,4},{1,5},{2,6},{3,7},{4,0},{5,1},{6,2},{7,3},{8,12},{9,13},{10,... | collective-permute-start | bytes 178184 | tf_op jit(solution)/shard_map/ppermute | solution.py:181
  8.7 3.0 %shard_map.57 = (bf16[464,7424]{1,0:T(8,128)(2,1)S(1)}, f32[8,128]{1,0:T(8,128)S(1)}) custom-call(bf16[1856,7424]{1,0:T(8,128)(2,1)} %bitcast.4, bf16[4,7424]{1,0:T(4,128)(2,1)S(1)} %shard_map.56.refs_1_.refs_0_), custom_call_target="tpu_custom_call" | custom-call | bytes 6889472 | tf_op jit(solution)/shard_map/pallas_call | solution.py:43
  11.7 1.6 %collective-permute-start.2 = (bf16[8,7424]{1,0:T(8,128)(2,1)S(1)}, bf16[8,7424]{1,0:T(8,128)(2,1)S(1)}, u32[]{:S(2)}, u32[]{:S(2)}) collective-permute-start(bf16[8,7424]{1,0:T(8,128)(2,1)S(1)} %shard_map.58.refs_1_.refs_0_), channel_id=1, source_target_pairs={{0,16},{1,3},{2,18},{3,1},{4,20},{5,7},{6,22},{7,5},{8,24},{9,11},... | collective-permute-start | bytes 356360 | tf_op jit(solution)/shard_map/ppermute | solution.py:181
  13.3 3.0 %shard_map.59 = (bf16[464,7424]{1,0:T(8,128)(2,1)S(1)}, f32[8,128]{1,0:T(8,128)S(1)}) custom-call(bf16[1856,7424]{1,0:T(8,128)(2,1)} %bitcast.3, bf16[8,7424]{1,0:T(8,128)(2,1)S(1)} %shard_map.58.refs_1_.refs_0_), custom_call_target="tpu_custom_call" | custom-call | bytes 6889472 | tf_op jit(solution)/shard_map/pallas_call | solution.py:43
  16.3 0.4 collective-permute-done.2.refs_1_
  16.7 1.6 %collective-permute-start.3 = (bf16[16,7424]{1,0:T(8,128)(2,1)S(1)}, bf16[16,7424]{1,0:T(8,128)(2,1)S(1)}, u32[]{:S(2)}, u32[]{:S(2)}) collective-permute-start(bf16[16,7424]{1,0:T(8,128)(2,1)S(1)} %shard_map.60.refs_2_.refs_0_), channel_id=1, source_target_pairs={{0,2},{1,17},{2,0},{3,19},{4,6},{5,21},{6,4},{7,23},{8,10},{9,25},... | collective-permute-start | bytes 712712 | tf_op jit(solution)/shard_map/ppermute | solution.py:181
  18.2 4.9 %shard_map.61 = (bf16[464,7424]{1,0:T(8,128)(2,1)S(1)}, bf16[464,7424]{1,0:T(8,128)(2,1)S(1)}, f32[8,128]{1,0:T(8,128)S(1)}) custom-call(bf16[1856,7424]{1,0:T(8,128)(2,1)} %bitcast.5, bf16[1856,7424]{1,0:T(8,128)(2,1)} %refs_0_.3, bf16[16,7424]{1,0:T(8,128)(2,1)S(1)} %shard_map.60.refs_2_.refs_0_), custom_call_target="tpu_custom_call" | custom-call | bytes 13778944 | tf_op jit(solution)/shard_map/pallas_call | solution.py:43
  23.2 0.1 collective-permute-start.4
  23.3 3.6 %shard_map.64 = (bf16[464,7424]{1,0:T(8,128)(2,1)S(1)}, f32[8,128]{1,0:T(8,128)}) custom-call(bf16[1856,7424]{1,0:T(8,128)(2,1)} %refs_0_.3, bf16[32,7424]{1,0:T(8,128)(2,1)S(1)} %shard_map.62.mine.refs_1_), custom_call_target="tpu_custom_call" | custom-call | bytes 6889472 | tf_op jit(solution)/shard_map/pallas_call | solution.py:43
  26.9 7.9 %shard_map.63 = (bf16[64,464]{1,0:T(8,128)(2,1)S(1)}, bf16[64,464]{1,0:T(8,128)(2,1)S(1)}) custom-call(bf16[32,7424]{1,0:T(8,128)(2,1)S(1)} %shard_map.62.mine.refs_1_, bf16[32,7424]{1,0:T(8,128)(2,1)S(1)} %collective-permute-done.4.theirs, bf16[464,7424]{1,0:T(8,128)(2,1)S(1)} %get-tuple-element.39.refs_0_, ...), custom_call_target="tpu_custom_call" | custom-call | flops 1763704832 | bytes 27557888 | tf_op jit(solution)/shard_map/pallas_call | solution.py:94
  34.8 1.2 %shard_map.69 = (f32[32,3712]{1,0:T(8,128)S(1)}, bf16[32,3712]{1,0:T(8,128)(2,1)S(1)}) custom-call(bf16[64,464]{1,0:T(8,128)(2,1)S(1)} %get-tuple-element.43.refs_0_, bf16[64,464]{1,0:T(8,128)(2,1)S(1)} %get-tuple-element.44.refs_1_, bf16[464,7424]{1,0:T(8,128)(2,1)S(1)} %get-tuple-element.45.refs_2_, bf16[464,7424]{1,0:T(8,128)(2,1)S(1)} %get-tuple-element.46.refs_3_), custom_call_target="tpu_custom_call" | custom-call | flops 440926208 | bytes 6889472 | tf_op jit(solution)/shard_map/pallas_call | solution.py:119
  36.0 0.6 collective-permute-start.9
  36.5 1.2 %shard_map.65 = (f32[32,3712]{1,0:T(8,128)S(1)}, bf16[32,3712]{1,0:T(8,128)(2,1)S(1)}) custom-call(bf16[64,464]{1,0:T(8,128)(2,1)S(1)} %get-tuple-element.43.refs_0_, bf16[64,464]{1,0:T(8,128)(2,1)S(1)} %get-tuple-element.44.refs_1_, bf16[464,7424]{1,0:T(8,128)(2,1)S(1)} %get-tuple-element.45.refs_2_, bf16[464,7424]{1,0:T(8,128)(2,1)S(1)} %get-tuple-element.46.refs_3_), custom_call_target="tpu_custom_call" | custom-call | flops 440926208 | bytes 6889472 | tf_op jit(solution)/shard_map/pallas_call | solution.py:119
  37.8 0.1 collective-permute-start.5
  37.9 1.2 %collective-permute-start.10 = (bf16[16,3712]{1,0:T(8,128)(2,1)S(1)}, bf16[16,3712]{1,0:T(8,128)(2,1)S(1)}, u32[]{:S(2)}, u32[]{:S(2)}) collective-permute-start(bf16[16,3712]{1,0:T(8,128)(2,1)S(1)} %get-tuple-element.58), channel_id=1, source_target_pairs={{0,2},{1,17},{2,0},{3,19},{4,6},{5,21},{6,4},{7,23},{8,10},{9,25},... | collective-permute-start | bytes 356360 | tf_op jit(solution)/shard_map/ppermute | solution.py:181
  39.1 0.2 collective-permute-done.5.refs_1_
  39.4 1.2 %collective-permute-start.6 = (bf16[16,3712]{1,0:T(8,128)(2,1)S(1)}, bf16[16,3712]{1,0:T(8,128)(2,1)S(1)}, u32[]{:S(2)}, u32[]{:S(2)}) collective-permute-start(bf16[16,3712]{1,0:T(8,128)(2,1)S(1)} %get-tuple-element.50), channel_id=1, source_target_pairs={{0,2},{1,17},{2,0},{3,19},{4,6},{5,21},{6,4},{7,23},{8,10},{9,25},... | collective-permute-start | bytes 356360 | tf_op jit(solution)/shard_map/ppermute | solution.py:181
  40.6 2.2 %collective-permute-done.10.refs_1_ = bf16[16,3712]{1,0:T(8,128)(2,1)S(1)} collective-permute-done((bf16[16,3712]{1,0:T(8,128)(2,1)S(1)}, bf16[16,3712]{1,0:T(8,128)(2,1)S(1)}, u32[]{:S(2)}, u32[]{:S(2)}) %collective-permute-start.10) | collective-permute-done | bytes 118816 | tf_op jit(solution)/shard_map/ppermute | solution.py:181
  42.8 1.6 %collective-permute-start.11 = (bf16[8,3712]{1,0:T(8,128)(2,1)S(1)}, bf16[8,3712]{1,0:T(8,128)(2,1)S(1)}, u32[]{:S(2)}, u32[]{:S(2)}) collective-permute-start(bf16[8,3712]{1,0:T(8,128)(2,1)S(1)} %get-tuple-element.60), channel_id=1, source_target_pairs={{0,16},{1,3},{2,18},{3,1},{4,20},{5,7},{6,22},{7,5},{8,24},{9,11},... | collective-permute-start | bytes 178184 | tf_op jit(solution)/shard_map/ppermute | solution.py:181
  44.4 1.4 %collective-permute-start.7 = (bf16[8,3712]{1,0:T(8,128)(2,1)S(1)}, bf16[8,3712]{1,0:T(8,128)(2,1)S(1)}, u32[]{:S(2)}, u32[]{:S(2)}) collective-permute-start(bf16[8,3712]{1,0:T(8,128)(2,1)S(1)} %get-tuple-element.52), channel_id=1, source_target_pairs={{0,16},{1,3},{2,18},{3,1},{4,20},{5,7},{6,22},{7,5},{8,24},{9,11},... | collective-permute-start | bytes 178184 | tf_op jit(solution)/shard_map/ppermute | solution.py:181
  45.9 1.2 %collective-permute-done.11.refs_1_ = bf16[8,3712]{1,0:T(8,128)(2,1)S(1)} collective-permute-done((bf16[8,3712]{1,0:T(8,128)(2,1)S(1)}, bf16[8,3712]{1,0:T(8,128)(2,1)S(1)}, u32[]{:S(2)}, u32[]{:S(2)}) %collective-permute-start.11) | collective-permute-done | bytes 59424 | tf_op jit(solution)/shard_map/ppermute | solution.py:181
  47.1 1.3 %collective-permute-start.12 = (bf16[4,3712]{1,0:T(4,128)(2,1)S(1)}, bf16[4,3712]{1,0:T(4,128)(2,1)S(1)}, u32[]{:S(2)}, u32[]{:S(2)}) collective-permute-start(bf16[4,3712]{1,0:T(4,128)(2,1)S(1)} %get-tuple-element.62), channel_id=1, source_target_pairs={{0,4},{1,5},{2,6},{3,7},{4,0},{5,1},{6,2},{7,3},{8,12},{9,13},{10,... | collective-permute-start | bytes 89096 | tf_op jit(solution)/shard_map/ppermute | solution.py:181
  48.4 0.3 collective-permute-done.7.refs_1_
  48.7 1.3 %collective-permute-start.8 = (bf16[4,3712]{1,0:T(4,128)(2,1)S(1)}, bf16[4,3712]{1,0:T(4,128)(2,1)S(1)}, u32[]{:S(2)}, u32[]{:S(2)}) collective-permute-start(bf16[4,3712]{1,0:T(4,128)(2,1)S(1)} %get-tuple-element.54), channel_id=1, source_target_pairs={{0,4},{1,5},{2,6},{3,7},{4,0},{5,1},{6,2},{7,3},{8,12},{9,13},{10,... | collective-permute-start | bytes 89096 | tf_op jit(solution)/shard_map/ppermute | solution.py:181
  50.0 1.1 %collective-permute-done.12.refs_3_ = bf16[4,3712]{1,0:T(4,128)(2,1)S(1)} collective-permute-done((bf16[4,3712]{1,0:T(4,128)(2,1)S(1)}, bf16[4,3712]{1,0:T(4,128)(2,1)S(1)}, u32[]{:S(2)}, u32[]{:S(2)}) %collective-permute-start.12) | collective-permute-done | bytes 29728 | tf_op jit(solution)/shard_map/ppermute | solution.py:181
  51.1 1.6 %collective-permute-done.8.refs_1_ = bf16[4,3712]{1,0:T(4,128)(2,1)S(1)} collective-permute-done((bf16[4,3712]{1,0:T(4,128)(2,1)S(1)}, bf16[4,3712]{1,0:T(4,128)(2,1)S(1)}, u32[]{:S(2)}, u32[]{:S(2)}) %collective-permute-start.8) | collective-permute-done | bytes 29728 | tf_op jit(solution)/shard_map/ppermute | solution.py:181
  52.7 3.1 %collective-permute-start.13 = (bf16[2,7424]{1,0:T(2,128)(2,1)S(1)}, bf16[2,7424]{1,0:T(2,128)(2,1)S(1)}, u32[]{:S(2)}, u32[]{:S(2)}) collective-permute-start(bf16[2,7424]{1,0:T(2,128)(2,1)S(1)} %get-tuple-element.64), channel_id=1, source_target_pairs={{0,8},{1,9},{2,10},{3,11},{4,12},{5,13},{6,14},{7,15},{8,0},{9,1},... | collective-permute-start | bytes 89096 | tf_op jit(solution)/shard_map/ppermute | solution.py:181
  56.4 1.2 %collective-permute-done.13.refs_1_ = bf16[2,7424]{1,0:T(2,128)(2,1)S(1)} collective-permute-done((bf16[2,7424]{1,0:T(2,128)(2,1)S(1)}, bf16[2,7424]{1,0:T(2,128)(2,1)S(1)}, u32[]{:S(2)}, u32[]{:S(2)}) %collective-permute-start.13) | collective-permute-done | bytes 29728 | tf_op jit(solution)/shard_map/ppermute | solution.py:181
  57.6 0.7 %shard_map.74 = bf16[2,7424]{1,0:T(2,128)(2,1)} custom-call(s32[1]{0:T(128)S(6)} %copy.6.counts, f32[2,7424]{1,0:T(2,128)S(1)} %get-tuple-element.63.refs_0_, bf16[2,7424]{1,0:T(2,128)(2,1)S(1)} %collective-permute-done.13.refs_1_), custom_call_target="tpu_custom_call" | custom-call | bytes 59392 | tf_op jit(solution)/shard_map/pallas_call | solution.py:169
  (18 shorter events, 0.3 us)
Async XLA Ops:
  0.0 7.0 %collective-permute-start = (bf16[2,7424]{1,0:T(2,128)(2,1)}, bf16[2,7424]{1,0:T(2,128)(2,1)S(1)}, u32[]{:S(2)}, u32[]{:S(2)}) collective-permute-start(bf16[2,7424]{1,0:T(2,128)(2,1)} %refs_0_.2), channel_id=1, source_target_pairs={{0,8},{1,9},{2,10},{3,11},{4,12},{5,13},{6,14},{7,15},{8,0},{9,1},... | collective-permute-start | bytes 89096 | tf_op jit(solution)/shard_map/ppermute | solution.py:181
  4.0 3.0 %copy-start = (bf16[2,7424]{1,0:T(2,128)(2,1)S(1)}, bf16[2,7424]{1,0:T(2,128)(2,1)}, u32[]{:S(2)}) copy-start(bf16[2,7424]{1,0:T(2,128)(2,1)} %refs_0_.2) | copy-start | bytes 89092
  7.1 4.6 %collective-permute-start.1 = (bf16[4,7424]{1,0:T(4,128)(2,1)S(1)}, bf16[4,7424]{1,0:T(4,128)(2,1)S(1)}, u32[]{:S(2)}, u32[]{:S(2)}) collective-permute-start(bf16[4,7424]{1,0:T(4,128)(2,1)S(1)} %shard_map.56.refs_1_.refs_0_), channel_id=1, source_target_pairs={{0,4},{1,5},{2,6},{3,7},{4,0},{5,1},{6,2},{7,3},{8,12},{9,13},{10,... | collective-permute-start | bytes 178184 | tf_op jit(solution)/shard_map/ppermute | solution.py:181
  11.7 4.9 %collective-permute-start.2 = (bf16[8,7424]{1,0:T(8,128)(2,1)S(1)}, bf16[8,7424]{1,0:T(8,128)(2,1)S(1)}, u32[]{:S(2)}, u32[]{:S(2)}) collective-permute-start(bf16[8,7424]{1,0:T(8,128)(2,1)S(1)} %shard_map.58.refs_1_.refs_0_), channel_id=1, source_target_pairs={{0,16},{1,3},{2,18},{3,1},{4,20},{5,7},{6,22},{7,5},{8,24},{9,11},... | collective-permute-start | bytes 356360 | tf_op jit(solution)/shard_map/ppermute | solution.py:181
  16.7 6.5 %collective-permute-start.3 = (bf16[16,7424]{1,0:T(8,128)(2,1)S(1)}, bf16[16,7424]{1,0:T(8,128)(2,1)S(1)}, u32[]{:S(2)}, u32[]{:S(2)}) collective-permute-start(bf16[16,7424]{1,0:T(8,128)(2,1)S(1)} %shard_map.60.refs_2_.refs_0_), channel_id=1, source_target_pairs={{0,2},{1,17},{2,0},{3,19},{4,6},{5,21},{6,4},{7,23},{8,10},{9,25},... | collective-permute-start | bytes 712712 | tf_op jit(solution)/shard_map/ppermute | solution.py:181
  23.2 3.7 %collective-permute-start.4 = (bf16[32,7424]{1,0:T(8,128)(2,1)S(1)}, bf16[32,7424]{1,0:T(8,128)(2,1)S(1)}, u32[]{:S(2)}, u32[]{:S(2)}) collective-permute-start(bf16[32,7424]{1,0:T(8,128)(2,1)S(1)} %shard_map.62.mine.refs_1_), channel_id=1, source_target_pairs={{0,1},{1,0},{2,3},{3,2},{4,5},{5,4},{6,7},{7,6},{8,9},{9,8},{10,11... | collective-permute-start | bytes 1425416 | tf_op jit(solution)/shard_map/ppermute | solution.py:181
  36.0 1.9 %collective-permute-start.9 = (bf16[32,3712]{1,0:T(8,128)(2,1)S(1)}, bf16[32,3712]{1,0:T(8,128)(2,1)S(1)}, u32[]{:S(2)}, u32[]{:S(2)}) collective-permute-start(bf16[32,3712]{1,0:T(8,128)(2,1)S(1)} %get-tuple-element.56), channel_id=1, source_target_pairs={{0,1},{1,0},{2,3},{3,2},{4,5},{5,4},{6,7},{7,6},{8,9},{9,8},{10,11... | collective-permute-start | bytes 712712 | tf_op jit(solution)/shard_map/ppermute | solution.py:181
  37.8 1.6 %collective-permute-start.5 = (bf16[32,3712]{1,0:T(8,128)(2,1)S(1)}, bf16[32,3712]{1,0:T(8,128)(2,1)S(1)}, u32[]{:S(2)}, u32[]{:S(2)}) collective-permute-start(bf16[32,3712]{1,0:T(8,128)(2,1)S(1)} %get-tuple-element.48), channel_id=1, source_target_pairs={{0,1},{1,0},{2,3},{3,2},{4,5},{5,4},{6,7},{7,6},{8,9},{9,8},{10,11... | collective-permute-start | bytes 712712 | tf_op jit(solution)/shard_map/ppermute | solution.py:181
  37.9 4.9 %collective-permute-start.10 = (bf16[16,3712]{1,0:T(8,128)(2,1)S(1)}, bf16[16,3712]{1,0:T(8,128)(2,1)S(1)}, u32[]{:S(2)}, u32[]{:S(2)}) collective-permute-start(bf16[16,3712]{1,0:T(8,128)(2,1)S(1)} %get-tuple-element.58), channel_id=1, source_target_pairs={{0,2},{1,17},{2,0},{3,19},{4,6},{5,21},{6,4},{7,23},{8,10},{9,25},... | collective-permute-start | bytes 356360 | tf_op jit(solution)/shard_map/ppermute | solution.py:181
  39.4 5.0 %collective-permute-start.6 = (bf16[16,3712]{1,0:T(8,128)(2,1)S(1)}, bf16[16,3712]{1,0:T(8,128)(2,1)S(1)}, u32[]{:S(2)}, u32[]{:S(2)}) collective-permute-start(bf16[16,3712]{1,0:T(8,128)(2,1)S(1)} %get-tuple-element.50), channel_id=1, source_target_pairs={{0,2},{1,17},{2,0},{3,19},{4,6},{5,21},{6,4},{7,23},{8,10},{9,25},... | collective-permute-start | bytes 356360 | tf_op jit(solution)/shard_map/ppermute | solution.py:181
  42.8 4.3 %collective-permute-start.11 = (bf16[8,3712]{1,0:T(8,128)(2,1)S(1)}, bf16[8,3712]{1,0:T(8,128)(2,1)S(1)}, u32[]{:S(2)}, u32[]{:S(2)}) collective-permute-start(bf16[8,3712]{1,0:T(8,128)(2,1)S(1)} %get-tuple-element.60), channel_id=1, source_target_pairs={{0,16},{1,3},{2,18},{3,1},{4,20},{5,7},{6,22},{7,5},{8,24},{9,11},... | collective-permute-start | bytes 178184 | tf_op jit(solution)/shard_map/ppermute | solution.py:181
  44.4 4.3 %collective-permute-start.7 = (bf16[8,3712]{1,0:T(8,128)(2,1)S(1)}, bf16[8,3712]{1,0:T(8,128)(2,1)S(1)}, u32[]{:S(2)}, u32[]{:S(2)}) collective-permute-start(bf16[8,3712]{1,0:T(8,128)(2,1)S(1)} %get-tuple-element.52), channel_id=1, source_target_pairs={{0,16},{1,3},{2,18},{3,1},{4,20},{5,7},{6,22},{7,5},{8,24},{9,11},... | collective-permute-start | bytes 178184 | tf_op jit(solution)/shard_map/ppermute | solution.py:181
  47.1 3.9 %collective-permute-start.12 = (bf16[4,3712]{1,0:T(4,128)(2,1)S(1)}, bf16[4,3712]{1,0:T(4,128)(2,1)S(1)}, u32[]{:S(2)}, u32[]{:S(2)}) collective-permute-start(bf16[4,3712]{1,0:T(4,128)(2,1)S(1)} %get-tuple-element.62), channel_id=1, source_target_pairs={{0,4},{1,5},{2,6},{3,7},{4,0},{5,1},{6,2},{7,3},{8,12},{9,13},{10,... | collective-permute-start | bytes 89096 | tf_op jit(solution)/shard_map/ppermute | solution.py:181
  48.7 3.9 %collective-permute-start.8 = (bf16[4,3712]{1,0:T(4,128)(2,1)S(1)}, bf16[4,3712]{1,0:T(4,128)(2,1)S(1)}, u32[]{:S(2)}, u32[]{:S(2)}) collective-permute-start(bf16[4,3712]{1,0:T(4,128)(2,1)S(1)} %get-tuple-element.54), channel_id=1, source_target_pairs={{0,4},{1,5},{2,6},{3,7},{4,0},{5,1},{6,2},{7,3},{8,12},{9,13},{10,... | collective-permute-start | bytes 89096 | tf_op jit(solution)/shard_map/ppermute | solution.py:181
  52.7 5.0 %collective-permute-start.13 = (bf16[2,7424]{1,0:T(2,128)(2,1)S(1)}, bf16[2,7424]{1,0:T(2,128)(2,1)S(1)}, u32[]{:S(2)}, u32[]{:S(2)}) collective-permute-start(bf16[2,7424]{1,0:T(2,128)(2,1)S(1)} %get-tuple-element.64), channel_id=1, source_target_pairs={{0,8},{1,9},{2,10},{3,11},{4,12},{5,13},{6,14},{7,15},{8,0},{9,1},... | collective-permute-start | bytes 89096 | tf_op jit(solution)/shard_map/ppermute | solution.py:181
